TPU v7x, 256 devices: a whole 4x4x8 slice. The times are simulated.
256 devices in a mesh: occ: 16 (over x_lo, z), aux: 16 (over y, x_hi, core).
Axes of the slice: x: 4 (x_hi: 2, x_lo: 2; x = x_hi * 2 + x_lo), y: 4, z: 8, core: 2. Of those that a mesh axis runs over, the one named last changes fastest.
Arguments:
- half_integrals: bfloat16 [16, 1024, 1024], P(None, 'aux'), may hold values from -1 to 1
- vir_coef: bfloat16 [1024, 768], P(None, 'occ'), may hold values from -0.1875 to 0.1875
- occ_energy: float32 [16], replicated, may hold values from -3 to -0.3
- vir_energy: float32 [768], replicated, may hold values from 0.1 to 2
Outputs:
- three_index: float32 [1024, 16, 768], P('aux', 'occ')
- vir_density: float32 [768, 768], P(('occ', 'aux'))
All inputs are finite; a program needn't handle non-finite values.
Results may differ from a plain program's by a relative error of at most 0.0006.
The roundings to bfloat16 on the way count: a program that leaves them out, or rounds other values in their place, can miss the bound.
Values may be sent and summed in bfloat16 or wider, within the bound.
No kernel may reach another device: no remote copies, remote signals or barrier semaphores. Data moves between devices by JAX's collectives and lax.ppermute only.
A program may use at most 64 MiB of HBM per device.

v0:
```python
import jax
import jax.numpy as jnp
from jax import lax
from jax.sharding import PartitionSpec as P


def from_behind(array, axis, by):
    size = lax.axis_size(axis)
    return lax.ppermute(array, axis, [(i, (i + by) % size) for i in range(size)])


def amplitudes(own_block, own_energy, arrival, arrival_energy, vir_energy, slice_energy):
    coulomb = jnp.einsum("jbp,iap->ijba", arrival, own_block, preferred_element_type=jnp.float32)
    denominator = (
        own_energy[:, None, None, None]
        + arrival_energy[None, :, None, None]
        - slice_energy[None, None, :, None]
        - vir_energy[None, None, None, :]
    )
    return (coulomb / denominator).astype(jnp.bfloat16)


def per_device(half_integrals, vir_coef, occ_energy, vir_energy):
    partial_block = jnp.einsum(
        "ipm,ma->iap", half_integrals, vir_coef, preferred_element_type=jnp.float32
    ).astype(jnp.bfloat16)
    local_block = lax.all_to_all(partial_block, "occ", split_axis=0, concat_axis=1, tiled=True)
    own_block = lax.all_gather(local_block, "aux", axis=2, tiled=True)
    cycle_size = lax.axis_size("occ")
    aux_size = lax.axis_size("aux")
    block_rows, virtuals, aux_total = own_block.shape
    slice_width = virtuals // aux_size
    first_virtual = lax.axis_index("aux") * slice_width
    visitor = lax.dynamic_slice_in_dim(own_block, first_virtual, slice_width, 1)
    slice_energy = lax.dynamic_slice_in_dim(vir_energy, first_virtual, slice_width, 0)
    my_index = lax.axis_index("occ")

    def energy_of(anchor):
        return lax.dynamic_slice_in_dim(occ_energy, anchor % cycle_size * block_rows, block_rows, 0)

    own_energy = energy_of(my_index)
    amp_stack = jnp.zeros((cycle_size, block_rows, block_rows, slice_width, virtuals), jnp.bfloat16)
    store_buffer = jnp.zeros((aux_total, block_rows, virtuals), jnp.float32)

    def absorb(ledger, position, arrival, arrival_energy):
        stacked, keeper = ledger
        amplitude = amplitudes(
            own_block, own_energy, arrival, arrival_energy, vir_energy, slice_energy
        )
        stacked = lax.dynamic_update_index_in_dim(stacked, amplitude, position, 0)
        keeper = keeper + jnp.einsum(
            "ijba,jbp->pia", amplitude, arrival, preferred_element_type=jnp.float32
        )
        return (stacked, keeper)

    ledger = absorb((amp_stack, store_buffer), 0, visitor, own_energy)

    def one_turn(turn_index, payload):
        ledger, arrival = payload
        arrival = from_behind(arrival, "occ", 1)
        ledger = absorb(ledger, turn_index, arrival, energy_of(my_index - turn_index))
        return (ledger, arrival)

    ledger, arrival = lax.fori_loop(1, cycle_size, one_turn, (ledger, visitor))
    amp_stack, store_buffer = ledger
    three_index = lax.psum_scatter(store_buffer, "aux", scatter_dimension=0, tiled=True)
    vir_sum = jnp.einsum(
        "sijca,sijcd->ad", amp_stack, amp_stack, preferred_element_type=jnp.float32
    )
    vir_rows = lax.psum_scatter(vir_sum, ("occ", "aux"), scatter_dimension=0, tiled=True)
    return (three_index, vir_rows / (block_rows * cycle_size * virtuals))


def solution(mesh):
    return jax.shard_map(
        per_device,
        mesh=mesh,
        in_specs=(P(None, "aux", None), P(None, "occ"), P(), P()),
        out_specs=(P("aux", "occ", None), P(("occ", "aux"), None)),
        check_vma=False,
    )
```

profile of v0, /device:TPU:32, one launch (start us, length us, event | category | flops | bytes accessed | tf_op | source)
XLA Modules:
  0.0 705.0 jit_solution(6458239080354881372)
XLA Ops:
  10.9 17.0 %all_to_all.12 = bf16[16,2,1536]{2,1,0:T(2,128)(2,1)S(1)} all-to-all(bf16[16,2,1536]{2,1,0:T(2,128)(2,1)S(1)} %reshape.209), channel_id=1, replica_groups=mesh['occ'=16,'aux'=16] {'occ'}, dimensions={0} | all-to-all | bytes 196608 | tf_op jit(solution)/shard_map/all_to_all | solution.py:27
  31.0 46.8 %all-gather.2.cloned.1.call-done = bf16[1,768,1024]{1,2,0:T(8,128)(2,1)} async-done(((bf16[1,768,64]{1,2,0:T(8,128)(2,1)}), bf16[1,768,1024]{1,2,0:T(8,128)(2,1)}) %all-gather.2.cloned.1.call-update) | async-done | bytes 1572880 | tf_op jit(solution)/shard_map/all_gather | solution.py:28
  85.9 191.3 %while.21 = (s32[]{:T(128)}, bf16[16,1,1,48,768]{4,3,2,1,0:T(8,128)(2,1)S(1)}, f32[1024,1,768]{0,2,1:T(8,128)}, bf16[1,48,1024]{2,1,0:T(8,128)(2,1)S(1)}, bf16[1...) while((s32[]{:T(128)}, ...), condition=%wide.region_1.2_spmd, body=%wide.region_0.1_spmd.sunk | while | flops 151892032 | bytes 8877338 | solution.py:64
  104.3 4.2 bitcast_add_fusion.2
  117.2 4.2 bitcast_add_fusion.2
  123.2 4.8 collective-permute-done
  130.1 4.2 bitcast_add_fusion.2
  136.1 4.8 collective-permute-done
  143.0 4.2 bitcast_add_fusion.2
  149.0 4.8 collective-permute-done
  155.9 4.2 bitcast_add_fusion.2
  161.9 4.8 collective-permute-done
  174.8 4.8 collective-permute-done
  187.7 4.8 collective-permute-done
  200.6 4.8 collective-permute-done
  213.5 5.7 collective-permute-done
  227.3 5.4 collective-permute-done
  234.7 4.2 bitcast_add_fusion.2
  240.7 4.5 collective-permute-done
  253.4 4.8 collective-permute-done
  266.3 4.8 collective-permute-done
  279.9 8.6 %copy.12 = f32[1024,1,768]{2,1,0:T(1,128)} copy(f32[1024,1,768]{0,2,1:T(8,128)} %get-tuple-element.319) | data formatting | bytes 6291456 | tf_op jit(solution)/shard_map/while | solution.py:64
  290.5 246.2 %all-reduce.8.cloned.1.call-done = f32[768,768]{1,0:T(8,128)} async-done(((f32[768,768]{1,0:T(8,128)}), f32[768,768]{1,0:T(8,128)}) %all-reduce.8.cloned.1.call-update) | async-done | bytes 2359312
  538.1 158.8 %all-reduce.6.cloned.1.call-done = f32[1024,1,768]{2,1,0:T(1,128)} async-done(((f32[1024,1,768]{2,1,0:T(1,128)}), f32[1024,1,768]{2,1,0:T(1,128)}) %all-reduce.6.cloned.1.call-update) | async-done | bytes 3145744
  (117 shorter events, 108.1 us)
Async XLA Ops:
  7.2 1.6 copy-start
  7.2 21.8 %copy-start.2 = (f32[16]{0:T(128)S(1)}, f32[16]{0:T(128)}, u32[]{:S(2)}) copy-start(f32[16]{0:T(128)} %param.8) | copy-start | bytes 196
  7.2 23.7 %copy-start.1 = (f32[768]{0:T(1024)S(1)}, f32[768]{0:T(1024)}, u32[]{:S(2)}) copy-start(f32[768]{0:T(1024)} %param.9) | copy-start | bytes 9220
  7.2 70.6 %all-gather.2.cloned.1.call-start = ((), (), s32[]{:S(2)}) async-start(), calls=%async_computation.1 | async-start | bytes 1671168 | tf_op jit(solution)/shard_map/all_gather | solution.py:28
  28.9 507.8 %all-reduce.8.cloned.1.call-start = ((), (), s32[]{:S(2)}) async-start(), calls=%async_computation.3 | async-start | bytes 4718592
  85.9 5.0 collective-permute-start
  97.1 5.2 collective-permute-start
  108.4 6.7 collective-permute-start
  121.3 6.7 collective-permute-start
  134.2 6.7 collective-permute-start
  147.1 6.7 collective-permute-start
  160.0 6.7 collective-permute-start
  172.9 6.7 collective-permute-start
  185.8 6.7 collective-permute-start
  198.7 6.7 collective-permute-start
  211.6 7.6 %collective-permute-start = (bf16[1,48,1024]{2,1,0:T(8,128)(2,1)S(1)}, bf16[1,48,1024]{2,1,0:T(8,128)(2,1)S(1)}, u32[]{:S(2)}, u32[]{:S(2)}) collective-permute-start(bf16[1,48,1024]{2,1,0:T(8,128)(2,1)S(1)} %get-tuple-element.448), channel_id=1, source_target_pairs={{0,16},{16,32},{32,48},{48,64},{64,80},{80,96},{96,112},{112,128},... | collective-permute-start | bytes 294920 | tf_op jit(solution)/shard_map/while/body/eval_jaxpr/ppermute | solution.py:9
  225.4 7.3 %collective-permute-start = (bf16[1,48,1024]{2,1,0:T(8,128)(2,1)S(1)}, bf16[1,48,1024]{2,1,0:T(8,128)(2,1)S(1)}, u32[]{:S(2)}, u32[]{:S(2)}) collective-permute-start(bf16[1,48,1024]{2,1,0:T(8,128)(2,1)S(1)} %get-tuple-element.448), channel_id=1, source_target_pairs={{0,16},{16,32},{32,48},{48,64},{64,80},{80,96},{96,112},{112,128},... | collective-permute-start | bytes 294920 | tf_op jit(solution)/shard_map/while/body/eval_jaxpr/ppermute | solution.py:9
  238.8 6.4 collective-permute-start
  251.5 6.7 collective-permute-start
  264.4 6.7 collective-permute-start
  279.9 417.0 %all-reduce.6.cloned.1.call-start = ((), (), s32[]{:S(2)}) async-start(), calls=%async_computation.2 | async-start | bytes 6291456
  288.5 0.7 copy-start.3
Sparse Core Ops, SparseCore 0:
  29.0 48.7 all-gather.1
  280.0 256.6 all-reduce.7
  539.4 157.4 all-reduce.5
where the time goes:
time: 707 us; the launch traced here: 705 us
  waiting for transfers between devices  518 us (73%)
  matrix products  101 us (14%)
  local copies, waits for them, and re-layouts  27.6 us (4%)
  loops' own time  19.8 us (3%)
  blocking collectives  17 us (2%)
  between operations  15.8 us (2%)
    unnamed x5, waiting for transfers between devices  405 us
    ppermute x15, waiting for transfers between devices, from_behind(): lax.ppermute(array, axis, [(i, (i + by) % size) for i in range(size)])  66.1 us
    dot_general x16, matrix products, absorb(): jnp.einsum('ijba,jbp->pia', amplitude, arrival, preferred_element_type=jn...  64.7 us
    all_gather x1, waiting for transfers between devices, per_device(): own_block = lax.all_gather(local_block, 'aux', axis=2, tiled=True)  46.8 us
    dot_general x16, matrix products, amplitudes(): jnp.einsum('jbp,iap->ijba', arrival, own_block, preferred_element_type=jn...  31.8 us
    another operation x1, loops' own time, per_device(): ledger, arrival = lax.fori_loop(1, cycle_size, one_turn, (ledger, visitor))  19.8 us
    all_to_all x1, blocking collectives, per_device(): lax.all_to_all(partial_block, 'occ', split_axis=0, concat_axis=1, tiled=T...  17 us
  transfers between devices with their start and end apart: 18, of which 18 were waited for; matrix products, arithmetic and copies ran while one was open for 3% of the time, Pallas kernels for 0%

commit v1 on v0

v1 whole, which is shorter than its diff:
```python
import functools

import jax
import jax.numpy as jnp
import numpy as np
from jax import lax
from jax.experimental import pallas as pl
from jax.experimental.pallas import tpu as pltpu
from jax.sharding import Mesh, PartitionSpec as P

OCC = ("xl", "z")
CHIPS = ("y", "xh")
AUX = ("y", "xh", "c")
ALL = OCC + AUX
XL, Z, Y, XH, C = 2, 8, 4, 2, 2
NO, NV, NP = 16, 768, 1024
PW, VW = 64, 48
VMEM = pl.BlockSpec(memory_space=pltpu.VMEM)
SMEM = pl.BlockSpec(memory_space=pltpu.SMEM)


def swap(array, axis):
    return lax.ppermute(array, axis, [(0, 1), (1, 0)])


def ring(array, by):
    return lax.ppermute(array, "z", [(i, (i + by) % Z) for i in range(Z)])


def from_chip(array, dy, dx):
    pairs = [
        (y * XH + x, (y + dy) % Y * XH + (x + dx) % XH) for y in range(Y) for x in range(XH)
    ]
    return lax.ppermute(array, CHIPS, pairs)


def rows_of_slice(piece):
    xl, z = lax.axis_index("xl"), lax.axis_index("z")
    pair = jnp.concatenate([piece, swap(piece, "xl")], 0)
    blocks = [(pair, xl, z, 0)]
    up = down = pair
    for step in range(1, Z // 2):
        up, down = ring(up, 1), ring(down, -1)
        blocks += [(up, xl, z - step, 0), (down, xl, z + step, 0)]
    far = (z + Z // 2) % Z
    blocks += [(ring(up[:PW], 1), xl, far, 1), (ring(down[PW:], -1), 1 - xl, far, 1)]
    arrays, starts = [], []
    for array, lo, at, single in blocks:
        arrays.append(array)
        starts.append((lo * Z + at % Z) * PW)
        if not single:
            starts.append(((1 - lo) * Z + at % Z) * PW)
    return arrays, starts


def columns_of_block(local):
    y, xh, c = (lax.axis_index(n) for n in AUX)
    pieces, starts = [], []
    for dy in range(Y):
        for dx in range(XH):
            piece = from_chip(local, dy, dx) if dy or dx else local
            pieces.append(piece)
            starts.append((((y - dy) % Y) * XH + (xh - dx) % XH) * (C * PW))
    other = swap(jnp.stack(pieces), "c")
    return pieces + [other], [s + c * PW for s in starts] + [s + (1 - c) * PW for s in starts]


def work(n_rows, n_cols, starts_ref, *refs):
    row_refs, col_refs = refs[:n_rows], refs[n_rows : n_rows + n_cols]
    row_energy, col_energy, three_ref, vir_ref, rows, cols, amp = refs[n_rows + n_cols :]

    at = 0
    for ref in row_refs:
        for part in range(ref.shape[0] // PW):
            start = pl.multiple_of(starts_ref[at], PW)
            rows[pl.ds(start, PW), :] = ref[part * PW : (part + 1) * PW, :]
            at += 1
    for ref in col_refs:
        for part in range(ref.shape[0] if len(ref.shape) == 3 else 1):
            start = pl.multiple_of(starts_ref[at], PW)
            cols[pl.ds(start, PW), :] = ref[part] if len(ref.shape) == 3 else ref[...]
            at += 1

    transposed = (((0,), (0,)), ((), ()))
    block = 128

    @pl.loop(0, NV // block)
    def _(k):
        here = pl.ds(pl.multiple_of(k * block, block), block)
        coulomb = lax.dot_general(
            rows[:, here], cols[...], transposed, preferred_element_type=jnp.float32
        )
        amp[here, :] = (coulomb / (row_energy[here, :] - col_energy[...])).astype(jnp.bfloat16)

    step = 128

    @pl.loop(0, NP // step)
    def _(k):
        here = pl.ds(pl.multiple_of(k * step, step), step)
        three_ref[here, :] = jnp.dot(rows[here, :], amp[...], preferred_element_type=jnp.float32)

    @pl.loop(0, NV // block)
    def _(k):
        here = pl.ds(pl.multiple_of(k * block, block), block)
        vir_ref[here, :] = lax.dot_general(
            amp[:, here], amp[...], transposed, preferred_element_type=jnp.float32
        )


def per_device(half_integrals, vir_coef, occ_energy, vir_energy):
    xl, z, y, xh, c = (lax.axis_index(n) for n in ALL)
    own = xl * Z + z
    mine = (y * XH + xh) * C + c
    native = jnp.einsum(
        "ipm,ma->ipa", half_integrals, vir_coef, preferred_element_type=jnp.float32
    ).astype(jnp.bfloat16)

    flat = jnp.transpose(native, (1, 0, 2)).reshape(PW, NV)
    turned = lax.ppermute(flat, ALL, [(o * NO + x, x * NO + o) for o in range(NO) for x in range(NO)])
    row_arrays, row_starts = rows_of_slice(turned)

    local = lax.all_to_all(native, OCC, split_axis=0, concat_axis=0, tiled=True)
    local = jnp.transpose(local, (1, 0, 2)).reshape(PW, NV)
    col_arrays, col_starts = columns_of_block(local)

    slice_energy = lax.dynamic_slice_in_dim(vir_energy, mine * VW, VW, 0)
    own_energy = lax.dynamic_slice_in_dim(occ_energy, own, 1, 0)
    row_energy = ((own_energy + occ_energy)[:, None] - slice_energy[None, :]).reshape(NV, 1)
    starts = jnp.stack(row_starts + col_starts).astype(jnp.int32)

    three, vir = pl.pallas_call(
        functools.partial(work, len(row_arrays), len(col_arrays)),
        out_shape=[
            jax.ShapeDtypeStruct((NP, NV), jnp.float32),
            jax.ShapeDtypeStruct((NV, NV), jnp.float32),
        ],
        in_specs=[SMEM] + [VMEM] * (len(row_arrays) + len(col_arrays) + 2),
        out_specs=[VMEM, VMEM],
        scratch_shapes=[
            pltpu.VMEM((NP, NV), jnp.bfloat16),
            pltpu.VMEM((NP, NV), jnp.bfloat16),
            pltpu.VMEM((NV, NV), jnp.bfloat16),
        ],
        compiler_params=pltpu.CompilerParams(vmem_limit_bytes=40 * 2**20),
        cost_estimate=pl.CostEstimate(
            flops=4 * NV * NV * NP + 2 * NV**3, bytes_accessed=10 * 2**20, transcendentals=0
        ),
    )(starts, *row_arrays, *col_arrays, row_energy, vir_energy[None, :])

    three = three.reshape(Y * XH, C, PW, NV)
    keep = lax.dynamic_index_in_dim(three, c, 1, keepdims=False)
    give = lax.dynamic_index_in_dim(three, 1 - c, 1, keepdims=False)
    three = keep + swap(give, "c")
    three = lax.all_to_all(three, CHIPS, split_axis=0, concat_axis=0, tiled=True)
    three_index = jnp.sum(three, 0)[:, None, :]

    half = NV // C
    keep = lax.dynamic_slice_in_dim(vir, c * half, half, 1)
    give = lax.dynamic_slice_in_dim(vir, (1 - c) * half, half, 1)
    vir = (keep + swap(give, "c")).reshape(NO, VW, half)
    vir = lax.all_to_all(vir, OCC, split_axis=0, concat_axis=0, tiled=True)
    vir = jnp.sum(vir, 0).reshape(NO, VW // NO, half)
    vir = lax.all_to_all(vir, AUX, split_axis=0, concat_axis=0, tiled=True)
    vir = jnp.sum(vir.reshape(Y * XH, C, VW // NO, half), 0)
    vir_rows = jnp.concatenate([vir[0], vir[1]], 1)
    return (three_index, vir_rows / (NO * NV))


def solution(mesh):
    fine = Mesh(mesh.devices.reshape(XL, Z, Y, XH, C), ALL)
    return jax.shard_map(
        per_device,
        mesh=fine,
        in_specs=(P(None, AUX, None), P(None, OCC), P(), P()),
        out_specs=(P(AUX, OCC, None), P(ALL, None)),
        check_vma=False,
    )
```

time: 707 us -> 172 us (0.24)
  waiting for transfers between devices: 518 us -> 71 us
  matrix products: 101 us -> 1.99 us
  starting transfers between devices: 4.25 us -> 56.5 us
  loops' own time: 19.8 us -> 0 us
  blocking collectives: 17 us -> 0 us
  between operations: 15.8 us -> 0.81 us
  Pallas kernels: 0 us -> 9.07 us
  other arithmetic: 1.55 us -> 8.95 us
    unnamed x5 -> x0, waiting for transfers between devices: 405 us -> none
    dot_general x34 -> x1, matrix products: 101 us -> 1.99 us  [per_device(): jnp.einsum('ipm,ma->ipa', half_integrals, vir_coef, preferred_element_typ...]
    all_to_all x0 -> x4, waiting for transfers between devices: none -> 51.5 us  [the longest x1 19.9 us: per_device(): lax.all_to_all(three, CHIPS, split_axis=0, concat_axis=0, tiled=True)]
    all_gather x1 -> x0, waiting for transfers between devices: 46.8 us -> none  [per_device(): own_block = lax.all_gather(local_block, 'aux', axis=2, tiled=True)]
    ppermute x15 -> x20, waiting for transfers between devices: 66.1 us -> 19.6 us  [the longest x8 11.1 us: ring(): return lax.ppermute(array, 'z', [(i, (i + by) % Z) for i in range(Z)])]
    all_to_all x0 -> x4, starting transfers between devices: none -> 28.2 us  [the longest x1 10.8 us: per_device(): local = lax.all_to_all(native, OCC, split_axis=0, concat_axis=0, tiled=True)]
    ppermute x15 -> x20, starting transfers between devices: 4.12 us -> 28.3 us  [the longest x7 15.7 us: from_chip(): return lax.ppermute(array, CHIPS, pairs)]
    another operation x1 -> x0, loops' own time: 19.8 us -> none  [per_device(): ledger, arrival = lax.fori_loop(1, cycle_size, one_turn, (ledger, visitor))]
  transfers between devices with their start and end apart: 18 -> 24, of which waited for: 18 -> 11; matrix products, arithmetic and copies ran while one was open for 3% -> 11% of each run, Pallas kernels for 0% -> 0%
where the time goes in v1:
time: 172 us; the launch traced here: 170 us
  waiting for transfers between devices  71 us (41%)
  starting transfers between devices  56.5 us (33%)
  local copies, waits for them, and re-layouts  21.2 us (12%)
  Pallas kernels  9.07 us (5%)
  other arithmetic  8.95 us (5%)
  matrix products  1.99 us (1%)
    all_to_all x1, waiting for transfers between devices, per_device(): lax.all_to_all(three, CHIPS, split_axis=0, concat_axis=0, tiled=True)  19.9 us
    all_to_all x1, waiting for transfers between devices, per_device(): vir = lax.all_to_all(vir, OCC, split_axis=0, concat_axis=0, tiled=True)  19.6 us
    ppermute x7, starting transfers between devices, from_chip(): return lax.ppermute(array, CHIPS, pairs)  15.7 us
    unnamed x32, local copies, waits for them, and re-layouts  13.6 us
    ppermute x8, waiting for transfers between devices, ring(): return lax.ppermute(array, 'z', [(i, (i + by) % Z) for i in range(Z)])  11.1 us
    all_to_all x1, starting transfers between devices, per_device(): local = lax.all_to_all(native, OCC, split_axis=0, concat_axis=0, tiled=True)  10.8 us
    pallas_call x1, Pallas kernels, per_device(): pl.pallas_call(functools.partial(work, len(row_arrays), len(col_arrays)),...  9.07 us
    ppermute x8, starting transfers between devices, ring(): return lax.ppermute(array, 'z', [(i, (i + by) % Z) for i in range(Z)])  9.07 us
  transfers between devices with their start and end apart: 24, of which 11 were waited for; matrix products, arithmetic and copies ran while one was open for 11% of the time, Pallas kernels for 0%

profile of v1, /device:TPU:32, one launch (start us, length us, event | category | flops | bytes accessed | tf_op | source)
XLA Modules:
  0.0 169.5 jit_solution(17265896026042555613)
XLA Ops:
  2.2 2.0 %convolution_convert_fusion = bf16[16,64,48]{1,2,0:T(8,128)(2,1)S(1)} fusion(bf16[16,64,1024]{2,1,0:T(8,128)(2,1)S(1)} %copy-done, bf16[1024,48]{0,1:T(8,128)(2,1)} %param.5), kind=kOutput, calls=%fused_computation.3 | convolution fusion | flops 100712448 | bytes 2293760 | tf_op jit(solution)/shard_map/ipm,ma->ipa/dot_general | solution.py:114
  4.4 1.9 %collective-permute-start = (bf16[64,768]{1,0:T(8,128)(2,1)S(1)}, bf16[64,768]{1,0:T(8,128)(2,1)S(1)}, u32[]{:S(2)}, u32[]{:S(2)}) collective-permute-start(bf16[64,768]{1,0:T(8,128)(2,1)S(1)} %copy.13), channel_id=1, source_target_pairs={{0,0},{1,16},{2,32},{3,48},{4,64},{5,80},{6,96},{7,112},{8,128},{9... | collective-permute-start | bytes 294920 | tf_op jit(solution)/shard_map/ppermute | solution.py:119
  7.1 10.8 %all-to-all-start = ((bf16[16,2,1536]{2,1,0:T(2,128)(2,1)}), bf16[16,2,1536]{2,1,0:T(2,128)(2,1)S(1)}, u32[]{:S(2)}, u32[]{:S(2)}) async-start(bf16[16,2,1536]{2,1,0:T(2,128)(2,1)} %reshape.54), calls=%async_computation | async-start | bytes 196608 | tf_op jit(solution)/shard_map/all_to_all | solution.py:122
  19.5 6.5 %all-to-all-done = bf16[16,2,1536]{2,1,0:T(2,128)(2,1)S(1)} async-done(((bf16[16,2,1536]{2,1,0:T(2,128)(2,1)}), bf16[16,2,1536]{2,1,0:T(2,128)(2,1)S(1)}, u32[]{:S(2)}, u32[]{:S(2)}) %all-to-all-start) | async-done | bytes 98336 | tf_op jit(solution)/shard_map/all_to_all | solution.py:122
  26.3 4.1 %collective-permute-start.10 = (bf16[64,768]{1,0:T(8,128)(2,1)S(1)}, bf16[64,768]{1,0:T(8,128)(2,1)S(1)}, u32[]{:S(2)}, u32[]{:S(2)}) collective-permute-start(bf16[64,768]{1,0:T(8,128)(2,1)S(1)} %copy.14.refs_9_), channel_id=1, source_target_pairs={{0,2},{2,0},{4,6},{6,4},{8,10},{10,8},{12,14},{14,12},{1,3},{3,1},... | collective-permute-start | bytes 294920 | tf_op jit(solution)/shard_map/ppermute | solution.py:34
  30.4 2.3 %collective-permute-start.11 = (bf16[64,768]{1,0:T(8,128)(2,1)S(1)}, bf16[64,768]{1,0:T(8,128)(2,1)S(1)}, u32[]{:S(2)}, u32[]{:S(2)}) collective-permute-start(bf16[64,768]{1,0:T(8,128)(2,1)S(1)} %copy.14.refs_9_), channel_id=1, source_target_pairs={{0,4},{2,6},{4,8},{6,10},{8,12},{10,14},{12,0},{14,2},{1,5},{3,7},... | collective-permute-start | bytes 294920 | tf_op jit(solution)/shard_map/ppermute | solution.py:34
  32.7 2.4 %collective-permute-start.13 = (bf16[64,768]{1,0:T(8,128)(2,1)S(1)}, bf16[64,768]{1,0:T(8,128)(2,1)S(1)}, u32[]{:S(2)}, u32[]{:S(2)}) collective-permute-start(bf16[64,768]{1,0:T(8,128)(2,1)S(1)} %copy.14.refs_9_), channel_id=1, source_target_pairs={{0,8},{2,10},{4,12},{6,14},{8,0},{10,2},{12,4},{14,6},{1,9},{3,11}... | collective-permute-start | bytes 294920 | tf_op jit(solution)/shard_map/ppermute | solution.py:34
  35.8 3.6 %collective-permute-start.14 = (bf16[64,768]{1,0:T(8,128)(2,1)S(1)}, bf16[64,768]{1,0:T(8,128)(2,1)S(1)}, u32[]{:S(2)}, u32[]{:S(2)}) collective-permute-start(bf16[64,768]{1,0:T(8,128)(2,1)S(1)} %copy.14.refs_9_), channel_id=1, source_target_pairs={{0,10},{2,8},{4,14},{6,12},{8,2},{10,0},{12,6},{14,4},{1,11},{3,9}... | collective-permute-start | bytes 294920 | tf_op jit(solution)/shard_map/ppermute | solution.py:34
  39.4 3.3 %collective-permute-start.15 = (bf16[64,768]{1,0:T(8,128)(2,1)S(1)}, bf16[64,768]{1,0:T(8,128)(2,1)S(1)}, u32[]{:S(2)}, u32[]{:S(2)}) collective-permute-start(bf16[64,768]{1,0:T(8,128)(2,1)S(1)} %copy.14.refs_9_), channel_id=1, source_target_pairs={{0,12},{2,14},{4,0},{6,2},{8,4},{10,6},{12,8},{14,10},{1,13},{3,15... | collective-permute-start | bytes 294920 | tf_op jit(solution)/shard_map/ppermute | solution.py:34
  53.9 4.7 %collective-permute-done.4.refs_3_ = bf16[128,768]{1,0:T(8,128)(2,1)} collective-permute-done((bf16[128,768]{1,0:T(8,128)(2,1)S(1)}, bf16[128,768]{1,0:T(8,128)(2,1)}, u32[]{:S(2)}, u32[]{:S(2)}) %collective-permute-start.4) | collective-permute-done | bytes 196640 | tf_op jit(solution)/shard_map/ppermute | solution.py:27
  61.2 4.0 %collective-permute-done.6.refs_5_ = bf16[128,768]{1,0:T(8,128)(2,1)S(1)} collective-permute-done((bf16[128,768]{1,0:T(8,128)(2,1)}, bf16[128,768]{1,0:T(8,128)(2,1)S(1)}, u32[]{:S(2)}, u32[]{:S(2)}) %collective-permute-start.6) | collective-permute-done | bytes 196640 | tf_op jit(solution)/shard_map/ppermute | solution.py:27
  67.8 2.3 %collective-permute-start.9 = (bf16[64,768]{1,0:T(8,128)(2,1)}, bf16[64,768]{1,0:T(8,128)(2,1)}, u32[]{:S(2)}, u32[]{:S(2)}) collective-permute-start(bf16[64,768]{1,0:T(8,128)(2,1)} %slice.17), channel_id=1, source_target_pairs={{0,112},{16,0},{32,16},{48,32},{64,48},{80,64},{96,80},{112,96},{1... | collective-permute-start | bytes 294920 | tf_op jit(solution)/shard_map/ppermute | solution.py:27
  75.7 9.1 %shard_map.59 = (f32[1024,768]{1,0:T(8,128)S(1)}, f32[768,768]{1,0:T(8,128)S(1)}) custom-call(s32[32]{0:T(128)S(1)} %stack.155.starts_ref, bf16[128,768]{1,0:T(8,128)(2,1)S(1)} %copy-done.6, bf16[128,768]{1,0:T(8,128)(2,1)S(1)} %copy-done.8, bf16[128,768]{1,0:T(8,128)(2,1)} %collective-permute-done.3.refs_2_, ...), custom_call_target="tpu_custom_call" | custom-call | flops 3321888768 | bytes 10485760 | tf_op jit(solution)/shard_map/pallas_call | solution.py:131
  88.0 3.0 %collective-permute-done.19 = f32[768,384]{1,0:T(8,128)} collective-permute-done((f32[768,384]{1,0:T(8,128)S(1)}, f32[768,384]{1,0:T(8,128)}, u32[]{:S(2)}, u32[]{:S(2)}) %collective-permute-start.19) | collective-permute-done | bytes 1179680 | tf_op jit(solution)/shard_map/ppermute | solution.py:23
  91.0 2.8 %dynamic-slice_add_fusion = f32[768,384]{1,0:T(8,128)} fusion(f32[768,384]{1,0:T(8,128)} %collective-permute-done.19, f32[768,768]{1,0:T(8,128)} %copy-done.2, s32[]{:T(128)S(6)} %select_n.137), kind=kLoop, calls=%fused_computation.2 | loop fusion | flops 294912 | bytes 3538948 | tf_op jit(solution)/shard_map/add | solution.py:160
  93.8 9.0 %all-to-all-start.2 = ((f32[16,48,384]{2,1,0:T(8,128)}), f32[16,48,384]{2,1,0:T(8,128)S(1)}, u32[]{:S(2)}, u32[]{:S(2)}) async-start(f32[16,48,384]{2,1,0:T(8,128)} %bitcast.74), calls=%async_computation.2 | async-start | bytes 2359296 | tf_op jit(solution)/shard_map/all_to_all | solution.py:161
  102.8 2.7 %dynamic-slice_bitcast_fusion = f32[8,64,768]{2,1,0:T(8,128)} fusion(f32[8,2,64,768]{3,2,1,0:T(8,128)} %bitcast.72, s32[]{:T(128)S(6)} %select_n.136), kind=kLoop, calls=%fused_computation.1 | loop fusion | bytes 3145732 | tf_op jit(solution)/shard_map/jit(dynamic_index_in_dim)/squeeze | solution.py:152
  105.5 3.7 %collective-permute-done.18 = f32[8,64,768]{2,1,0:T(8,128)} collective-permute-done((f32[8,64,768]{2,1,0:T(8,128)}, f32[8,64,768]{2,1,0:T(8,128)}, u32[]{:S(2)}, u32[]{:S(2)}) %collective-permute-start.18) | collective-permute-done | bytes 1572896 | tf_op jit(solution)/shard_map/ppermute | solution.py:23
  109.2 3.2 %bitcast_add_fusion = f32[8,64,768]{2,1,0:T(8,128)} fusion(f32[8,64,768]{2,1,0:T(8,128)} %collective-permute-done.18, f32[8,2,64,768]{3,2,1,0:T(8,128)} %bitcast.73, s32[]{:T(128)S(6)} %select_n.135), kind=kLoop, calls=%fused_computation | loop fusion | flops 393216 | bytes 4718596 | tf_op jit(solution)/shard_map/add | solution.py:153
  112.4 19.6 %all-to-all-done.2 = f32[16,48,384]{2,1,0:T(8,128)S(1)} async-done(((f32[16,48,384]{2,1,0:T(8,128)}), f32[16,48,384]{2,1,0:T(8,128)S(1)}, u32[]{:S(2)}, u32[]{:S(2)}) %all-to-all-start.2) | async-done | bytes 1179680 | tf_op jit(solution)/shard_map/all_to_all | solution.py:161
  132.1 4.8 %all-to-all-start.1 = ((f32[8,64,768]{2,1,0:T(8,128)}), f32[8,64,768]{2,1,0:T(8,128)}, u32[]{:S(2)}, u32[]{:S(2)}) async-start(f32[8,64,768]{2,1,0:T(8,128)} %bitcast_add_fusion), calls=%async_computation.1 | async-start | bytes 3145728 | tf_op jit(solution)/shard_map/all_to_all | solution.py:154
  137.7 19.9 %all-to-all-done.1 = f32[8,64,768]{2,1,0:T(8,128)} async-done(((f32[8,64,768]{2,1,0:T(8,128)}), f32[8,64,768]{2,1,0:T(8,128)}, u32[]{:S(2)}, u32[]{:S(2)}) %all-to-all-start.1) | async-done | bytes 1572896 | tf_op jit(solution)/shard_map/all_to_all | solution.py:154
  157.6 3.5 %all-to-all-start.3 = ((f32[16,3,384]{2,1,0:T(4,128)}), f32[16,3,384]{2,1,0:T(4,128)S(1)}, u32[]{:S(2)}, u32[]{:S(2)}) async-start(f32[16,3,384]{2,1,0:T(4,128)} %reshape.51), calls=%async_computation.3 | async-start | bytes 196608 | tf_op jit(solution)/shard_map/all_to_all | solution.py:163
  163.4 5.5 %all-to-all-done.3 = f32[16,3,384]{2,1,0:T(4,128)S(1)} async-done(((f32[16,3,384]{2,1,0:T(4,128)}), f32[16,3,384]{2,1,0:T(4,128)S(1)}, u32[]{:S(2)}, u32[]{:S(2)}) %all-to-all-start.3) | async-done | bytes 73760 | tf_op jit(solution)/shard_map/all_to_all | solution.py:163
  (83 shorter events, 34.0 us)
Async XLA Ops:
  4.4 13.5 %collective-permute-start = (bf16[64,768]{1,0:T(8,128)(2,1)S(1)}, bf16[64,768]{1,0:T(8,128)(2,1)S(1)}, u32[]{:S(2)}, u32[]{:S(2)}) collective-permute-start(bf16[64,768]{1,0:T(8,128)(2,1)S(1)} %copy.13), channel_id=1, source_target_pairs={{0,0},{1,16},{2,32},{3,48},{4,64},{5,80},{6,96},{7,112},{8,128},{9... | collective-permute-start | bytes 294920 | tf_op jit(solution)/shard_map/ppermute | solution.py:119
  7.1 18.8 %all-to-all-start = ((bf16[16,2,1536]{2,1,0:T(2,128)(2,1)}), bf16[16,2,1536]{2,1,0:T(2,128)(2,1)S(1)}, u32[]{:S(2)}, u32[]{:S(2)}) async-start(bf16[16,2,1536]{2,1,0:T(2,128)(2,1)} %reshape.54), calls=%async_computation | async-start | bytes 196608 | tf_op jit(solution)/shard_map/all_to_all | solution.py:122
  17.9 17.9 %collective-permute-start.1 = (bf16[64,768]{1,0:T(8,128)(2,1)S(1)}, bf16[64,768]{1,0:T(8,128)(2,1)S(1)}, u32[]{:S(2)}, u32[]{:S(2)}) collective-permute-start(bf16[64,768]{1,0:T(8,128)(2,1)S(1)} %collective-permute-done), channel_id=1, source_target_pairs={{0,128},{128,0},{1,129},{129,1},{2,130},{130,2},{3,131},{131,3},{4... | collective-permute-start | bytes 294920 | tf_op jit(solution)/shard_map/ppermute | solution.py:23
  26.3 13.2 %collective-permute-start.10 = (bf16[64,768]{1,0:T(8,128)(2,1)S(1)}, bf16[64,768]{1,0:T(8,128)(2,1)S(1)}, u32[]{:S(2)}, u32[]{:S(2)}) collective-permute-start(bf16[64,768]{1,0:T(8,128)(2,1)S(1)} %copy.14.refs_9_), channel_id=1, source_target_pairs={{0,2},{2,0},{4,6},{6,4},{8,10},{10,8},{12,14},{14,12},{1,3},{3,1},... | collective-permute-start | bytes 294920 | tf_op jit(solution)/shard_map/ppermute | solution.py:34
  30.4 13.0 %collective-permute-start.11 = (bf16[64,768]{1,0:T(8,128)(2,1)S(1)}, bf16[64,768]{1,0:T(8,128)(2,1)S(1)}, u32[]{:S(2)}, u32[]{:S(2)}) collective-permute-start(bf16[64,768]{1,0:T(8,128)(2,1)S(1)} %copy.14.refs_9_), channel_id=1, source_target_pairs={{0,4},{2,6},{4,8},{6,10},{8,12},{10,14},{12,0},{14,2},{1,5},{3,7},... | collective-permute-start | bytes 294920 | tf_op jit(solution)/shard_map/ppermute | solution.py:34
  32.7 11.3 %collective-permute-start.12 = (bf16[64,768]{1,0:T(8,128)(2,1)S(1)}, bf16[64,768]{1,0:T(8,128)(2,1)S(1)}, u32[]{:S(2)}, u32[]{:S(2)}) collective-permute-start(bf16[64,768]{1,0:T(8,128)(2,1)S(1)} %copy.14.refs_9_), channel_id=1, source_target_pairs={{0,6},{2,4},{4,10},{6,8},{8,14},{10,12},{12,2},{14,0},{1,7},{3,5},... | collective-permute-start | bytes 294920 | tf_op jit(solution)/shard_map/ppermute | solution.py:34
  32.7 12.8 %collective-permute-start.13 = (bf16[64,768]{1,0:T(8,128)(2,1)S(1)}, bf16[64,768]{1,0:T(8,128)(2,1)S(1)}, u32[]{:S(2)}, u32[]{:S(2)}) collective-permute-start(bf16[64,768]{1,0:T(8,128)(2,1)S(1)} %copy.14.refs_9_), channel_id=1, source_target_pairs={{0,8},{2,10},{4,12},{6,14},{8,0},{10,2},{12,4},{14,6},{1,9},{3,11}... | collective-permute-start | bytes 294920 | tf_op jit(solution)/shard_map/ppermute | solution.py:34
  35.8 11.5 %collective-permute-start.14 = (bf16[64,768]{1,0:T(8,128)(2,1)S(1)}, bf16[64,768]{1,0:T(8,128)(2,1)S(1)}, u32[]{:S(2)}, u32[]{:S(2)}) collective-permute-start(bf16[64,768]{1,0:T(8,128)(2,1)S(1)} %copy.14.refs_9_), channel_id=1, source_target_pairs={{0,10},{2,8},{4,14},{6,12},{8,2},{10,0},{12,6},{14,4},{1,11},{3,9}... | collective-permute-start | bytes 294920 | tf_op jit(solution)/shard_map/ppermute | solution.py:34
  39.4 8.6 %collective-permute-start.15 = (bf16[64,768]{1,0:T(8,128)(2,1)S(1)}, bf16[64,768]{1,0:T(8,128)(2,1)S(1)}, u32[]{:S(2)}, u32[]{:S(2)}) collective-permute-start(bf16[64,768]{1,0:T(8,128)(2,1)S(1)} %copy.14.refs_9_), channel_id=1, source_target_pairs={{0,12},{2,14},{4,0},{6,2},{8,4},{10,6},{12,8},{14,10},{1,13},{3,15... | collective-permute-start | bytes 294920 | tf_op jit(solution)/shard_map/ppermute | solution.py:34
  43.4 7.0 %collective-permute-start.16 = (bf16[64,768]{1,0:T(8,128)(2,1)S(1)}, bf16[64,768]{1,0:T(8,128)(2,1)S(1)}, u32[]{:S(2)}, u32[]{:S(2)}) collective-permute-start(bf16[64,768]{1,0:T(8,128)(2,1)S(1)} %copy.14.refs_9_), channel_id=1, source_target_pairs={{0,14},{2,12},{4,2},{6,0},{8,6},{10,4},{12,10},{14,8},{1,15},{3,13... | collective-permute-start | bytes 294920 | tf_op jit(solution)/shard_map/ppermute | solution.py:34
  44.0 7.0 %collective-permute-start.2 = (bf16[128,768]{1,0:T(8,128)(2,1)S(1)}, bf16[128,768]{1,0:T(8,128)(2,1)S(1)}, u32[]{:S(2)}, u32[]{:S(2)}) collective-permute-start(bf16[128,768]{1,0:T(8,128)(2,1)S(1)} %constant_dynamic-update-slice_fusion.refs_0_), channel_id=1, source_target_pairs={{0,16},{16,32},{32,48},{48,64},{64,80},{80,96},{96,112},{112,0},{1... | collective-permute-start | bytes 589832 | tf_op jit(solution)/shard_map/ppermute | solution.py:27
  45.5 6.2 %collective-permute-start.3 = (bf16[128,768]{1,0:T(8,128)(2,1)S(1)}, bf16[128,768]{1,0:T(8,128)(2,1)}, u32[]{:S(2)}, u32[]{:S(2)}) collective-permute-start(bf16[128,768]{1,0:T(8,128)(2,1)S(1)} %constant_dynamic-update-slice_fusion.refs_0_), channel_id=1, source_target_pairs={{0,112},{16,0},{32,16},{48,32},{64,48},{80,64},{96,80},{112,96},{1... | collective-permute-start | bytes 589832 | tf_op jit(solution)/shard_map/ppermute | solution.py:27
  51.1 21.8 %collective-permute-start.17 = (bf16[8,64,768]{2,1,0:T(8,128)(2,1)}, bf16[8,64,768]{2,1,0:T(8,128)(2,1)}, u32[]{:S(2)}, u32[]{:S(2)}) collective-permute-start(bf16[8,64,768]{2,1,0:T(8,128)(2,1)} %bitcast_dynamic-update-slice_fusion), channel_id=1, source_target_pairs={{0,1},{1,0},{2,3},{3,2},{4,5},{5,4},{6,7},{7,6},{8,9},{9,8},{10,11... | collective-permute-start | bytes 2359304 | tf_op jit(solution)/shard_map/ppermute | solution.py:23
  51.1 7.4 %collective-permute-start.4 = (bf16[128,768]{1,0:T(8,128)(2,1)S(1)}, bf16[128,768]{1,0:T(8,128)(2,1)}, u32[]{:S(2)}, u32[]{:S(2)}) collective-permute-start(bf16[128,768]{1,0:T(8,128)(2,1)S(1)} %collective-permute-done.2.refs_1_), channel_id=1, source_target_pairs={{0,16},{16,32},{32,48},{48,64},{64,80},{80,96},{96,112},{112,0},{1... | collective-permute-start | bytes 589832 | tf_op jit(solution)/shard_map/ppermute | solution.py:27
  51.8 7.4 %collective-permute-start.5 = (bf16[128,768]{1,0:T(8,128)(2,1)}, bf16[128,768]{1,0:T(8,128)(2,1)}, u32[]{:S(2)}, u32[]{:S(2)}) collective-permute-start(bf16[128,768]{1,0:T(8,128)(2,1)} %collective-permute-done.3.refs_2_), channel_id=1, source_target_pairs={{0,112},{16,0},{32,16},{48,32},{64,48},{80,64},{96,80},{112,96},{1... | collective-permute-start | bytes 589832 | tf_op jit(solution)/shard_map/ppermute | solution.py:27
  58.5 6.7 %collective-permute-start.6 = (bf16[128,768]{1,0:T(8,128)(2,1)}, bf16[128,768]{1,0:T(8,128)(2,1)S(1)}, u32[]{:S(2)}, u32[]{:S(2)}) collective-permute-start(bf16[128,768]{1,0:T(8,128)(2,1)} %collective-permute-done.4.refs_3_), channel_id=1, source_target_pairs={{0,16},{16,32},{32,48},{48,64},{64,80},{80,96},{96,112},{112,0},{1... | collective-permute-start | bytes 589832 | tf_op jit(solution)/shard_map/ppermute | solution.py:27
  59.1 7.3 %collective-permute-start.7 = (bf16[128,768]{1,0:T(8,128)(2,1)}, bf16[128,768]{1,0:T(8,128)(2,1)S(1)}, u32[]{:S(2)}, u32[]{:S(2)}) collective-permute-start(bf16[128,768]{1,0:T(8,128)(2,1)} %collective-permute-done.5.refs_4_), channel_id=1, source_target_pairs={{0,112},{16,0},{32,16},{48,32},{64,48},{80,64},{96,80},{112,96},{1... | collective-permute-start | bytes 589832 | tf_op jit(solution)/shard_map/ppermute | solution.py:27
  65.8 5.8 %collective-permute-start.8 = (bf16[64,768]{1,0:T(8,128)(2,1)}, bf16[64,768]{1,0:T(8,128)(2,1)}, u32[]{:S(2)}, u32[]{:S(2)}) collective-permute-start(bf16[64,768]{1,0:T(8,128)(2,1)} %slice.16), channel_id=1, source_target_pairs={{0,16},{16,32},{32,48},{48,64},{64,80},{80,96},{96,112},{112,0},{1... | collective-permute-start | bytes 294920 | tf_op jit(solution)/shard_map/ppermute | solution.py:27
  67.8 5.1 %collective-permute-start.9 = (bf16[64,768]{1,0:T(8,128)(2,1)}, bf16[64,768]{1,0:T(8,128)(2,1)}, u32[]{:S(2)}, u32[]{:S(2)}) collective-permute-start(bf16[64,768]{1,0:T(8,128)(2,1)} %slice.17), channel_id=1, source_target_pairs={{0,112},{16,0},{32,16},{48,32},{64,48},{80,64},{96,80},{112,96},{1... | collective-permute-start | bytes 294920 | tf_op jit(solution)/shard_map/ppermute | solution.py:27
  87.9 3.1 %collective-permute-start.19 = (f32[768,384]{1,0:T(8,128)S(1)}, f32[768,384]{1,0:T(8,128)}, u32[]{:S(2)}, u32[]{:S(2)}) collective-permute-start(f32[768,384]{1,0:T(8,128)S(1)} %constant_dynamic-slice_fusion), channel_id=1, source_target_pairs={{0,1},{1,0},{2,3},{3,2},{4,5},{5,4},{6,7},{7,6},{8,9},{9,8},{10,11... | collective-permute-start | bytes 3538952 | tf_op jit(solution)/shard_map/ppermute | solution.py:23
  93.8 38.3 %all-to-all-start.2 = ((f32[16,48,384]{2,1,0:T(8,128)}), f32[16,48,384]{2,1,0:T(8,128)S(1)}, u32[]{:S(2)}, u32[]{:S(2)}) async-start(f32[16,48,384]{2,1,0:T(8,128)} %bitcast.74), calls=%async_computation.2 | async-start | bytes 2359296 | tf_op jit(solution)/shard_map/all_to_all | solution.py:161
  105.5 3.8 %collective-permute-start.18 = (f32[8,64,768]{2,1,0:T(8,128)}, f32[8,64,768]{2,1,0:T(8,128)}, u32[]{:S(2)}, u32[]{:S(2)}) collective-permute-start(f32[8,64,768]{2,1,0:T(8,128)} %dynamic-slice_bitcast_fusion), channel_id=1, source_target_pairs={{0,1},{1,0},{2,3},{3,2},{4,5},{5,4},{6,7},{7,6},{8,9},{9,8},{10,11... | collective-permute-start | bytes 4718600 | tf_op jit(solution)/shard_map/ppermute | solution.py:23
  132.1 25.5 %all-to-all-start.1 = ((f32[8,64,768]{2,1,0:T(8,128)}), f32[8,64,768]{2,1,0:T(8,128)}, u32[]{:S(2)}, u32[]{:S(2)}) async-start(f32[8,64,768]{2,1,0:T(8,128)} %bitcast_add_fusion), calls=%async_computation.1 | async-start | bytes 3145728 | tf_op jit(solution)/shard_map/all_to_all | solution.py:154
  157.6 11.3 %all-to-all-start.3 = ((f32[16,3,384]{2,1,0:T(4,128)}), f32[16,3,384]{2,1,0:T(4,128)S(1)}, u32[]{:S(2)}, u32[]{:S(2)}) async-start(f32[16,3,384]{2,1,0:T(4,128)} %reshape.51), calls=%async_computation.3 | async-start | bytes 196608 | tf_op jit(solution)/shard_map/all_to_all | solution.py:163
  (11 other events, 150.2 us)

commit v2 on v1

v2 whole, which is shorter than its diff:
```python
import functools

import jax
import jax.numpy as jnp
import numpy as np
from jax import lax
from jax.experimental import pallas as pl
from jax.experimental.pallas import tpu as pltpu
from jax.sharding import Mesh, PartitionSpec as P

OCC = ("xl", "z")
CHIPS = ("y", "xh")
AUX = ("y", "xh", "c")
ALL = OCC + AUX
XL, Z, Y, XH, C = 2, 8, 4, 2, 2
NO, NV, NP = 16, 768, 1024
PW, VW = 64, 48
VMEM = pl.BlockSpec(memory_space=pltpu.VMEM)
SMEM = pl.BlockSpec(memory_space=pltpu.SMEM)


def swap(array, axis):
    return lax.ppermute(array, axis, [(0, 1), (1, 0)])


def ring(array, by):
    return lax.ppermute(array, "z", [(i, (i + by) % Z) for i in range(Z)])


def next_chip(array, hop):
    pairs = [(q, hop_from(q, hop)) for q in range(Y * XH)]
    return lax.ppermute(array, CHIPS, pairs)


def hop_from(q, hop):
    return (q // XH + hop // XH) % Y * XH + (q + hop) % XH


def rows_of_slice(piece):
    xl, z = lax.axis_index("xl"), lax.axis_index("z")
    pair = jnp.concatenate([piece, swap(piece, "xl")], 0)
    arrays, owners = [pair], [(xl, z), (1 - xl, z)]
    up = down = pair
    first = None
    for step in range(1, Z // 2):
        up, down = ring(up, 1), ring(down, -1)
        first = up if first is None else first
        arrays += [up, down]
        owners += [(xl, z - step), (1 - xl, z - step), (xl, z + step), (1 - xl, z + step)]
    arrays += [ring(up[:PW], 1), ring(down[PW:], -1)]
    owners += [(xl, z + Z // 2), (1 - xl, z + Z // 2)]
    return arrays, [lo * Z + at % Z for lo, at in owners], first


TRANSPOSED = (((0,), (0,)), ((), ()))
HALF_P, HALF_V = NP // C, NV // C


def amplitudes(n_rows, place, *refs):
    row_refs, (own_cols, other_cols, row_energy, col_energy) = refs[:n_rows], refs[n_rows : n_rows + 4]
    rows, amp, vir, cols = refs[n_rows + 4 :]
    core = place[24]
    at = 0
    for ref in row_refs:
        for part in range(ref.shape[0] // PW):
            start = pl.multiple_of(place[at], PW)
            rows[pl.ds(start, PW), :] = ref[part * PW : (part + 1) * PW, :]
            at += 1
    cols[pl.ds(pl.multiple_of(core * HALF_P, HALF_P), HALF_P), :] = own_cols[...]
    cols[pl.ds(pl.multiple_of((1 - core) * HALF_P, HALF_P), HALF_P), :] = other_cols[...]
    for k in range(NV // 256):
        here = slice(k * 256, (k + 1) * 256)
        coulomb = lax.dot_general(
            rows[:, here], cols[...], TRANSPOSED, preferred_element_type=jnp.float32
        )
        amp[here, :] = (coulomb / (row_energy[here, :] - col_energy[...])).astype(jnp.bfloat16)
    virtual_block(amp, 1 - core, vir)


def virtual_block(amp, half, vir):
    side = amp[:, pl.ds(pl.multiple_of(half * HALF_V, HALF_V), HALF_V)]
    for k in range(NV // 256):
        here = slice(k * 256, (k + 1) * 256)
        vir[here, :] = lax.dot_general(
            amp[:, here], side, TRANSPOSED, preferred_element_type=jnp.float32
        )


def give_and_keep(place, rows, amp, vir, three):
    core = place[24]
    virtual_block(amp, core, vir)
    for k in range(HALF_P // 256):
        start = pl.multiple_of((1 - core) * HALF_P + k * 256, 256)
        three[k * 256 : (k + 1) * 256, :] = jnp.dot(
            rows[pl.ds(start, 256), :], amp[...], preferred_element_type=jnp.float32
        )


def pack_virtual(keep, got, out):
    total = keep[...] + got[...]
    top = jnp.maximum(jnp.max(jnp.abs(total), keepdims=True), 2.0**-100)
    power = jnp.ceil(jnp.log2(top))
    total = total * jnp.exp2(SCALE - power)
    tail = jnp.broadcast_to(power, (2, HALF_V))
    for g in range(NV // 6):
        out[8 * g : 8 * g + 8, :] = jnp.concatenate([total[6 * g : 6 * g + 6, :], tail], 0)


def keep_three(place, rows, amp, got, *outs):
    *outs, total = outs
    core = place[24]
    for k in range(HALF_P // 256):
        start = pl.multiple_of(core * HALF_P + k * 256, 256)
        here = slice(k * 256, (k + 1) * 256)
        total[here, :] = got[here, :] + jnp.dot(
            rows[pl.ds(start, 256), :], amp[...], preferred_element_type=jnp.float32
        )
    for hop, out in enumerate(outs):
        out[...] = total[pl.ds(pl.multiple_of(place[16 + hop], PW), PW), :]


SCALE = 14.0


def call(kernel, shapes, args, scratch=(), flops=0):
    return pl.pallas_call(
        kernel,
        out_shape=[jax.ShapeDtypeStruct(s, t) for s, t in shapes],
        in_specs=[SMEM if a.dtype == jnp.int32 else VMEM for a in args],
        out_specs=[VMEM] * len(shapes),
        scratch_shapes=[pltpu.VMEM(s, t) for s, t in scratch],
        compiler_params=pltpu.CompilerParams(vmem_limit_bytes=32 * 2**20),
        cost_estimate=pl.CostEstimate(flops=flops, bytes_accessed=6 * 2**20, transcendentals=0),
    )(*args)


def per_device(half_integrals, vir_coef, occ_energy, vir_energy):
    xl, z, y, xh, c = (lax.axis_index(n) for n in ALL)
    own = xl * Z + z
    chip = y * XH + xh
    native = jnp.einsum(
        "ipm,ma->ipa", half_integrals, vir_coef, preferred_element_type=jnp.float32
    ).astype(jnp.bfloat16)

    flat = jnp.transpose(native, (1, 0, 2)).reshape(PW, NV)
    turned = lax.ppermute(flat, ALL, [(o * NO + x, x * NO + o) for o in range(NO) for x in range(NO)])
    row_arrays, owners, first = rows_of_slice(turned)

    local = lax.all_to_all(native, OCC, split_axis=0, concat_axis=0, tiled=True)
    local = jnp.transpose(local, (1, 0, 2)).reshape(PW, NV)
    local, _ = lax.optimization_barrier((local, first))
    own_cols = lax.all_to_all(
        jnp.broadcast_to(local, (Y * XH, PW, NV)), CHIPS, split_axis=0, concat_axis=0, tiled=True
    ).reshape(HALF_P, NV)
    other_cols = swap(own_cols, "c")

    slice_energy = lax.dynamic_slice_in_dim(vir_energy, (chip * C + c) * VW, VW, 0)
    own_energy = lax.dynamic_slice_in_dim(occ_energy, own, 1, 0)
    row_energy = ((own_energy + occ_energy)[:, None] - slice_energy[None, :]).reshape(NV, 1)
    places = [o % C * HALF_P + o // C * PW for o in owners]
    places += [hop_from(chip, hop) * PW for hop in range(Y * XH)] + [c]
    place = jnp.stack(places).astype(jnp.int32)

    bf16, f32 = jnp.bfloat16, jnp.float32
    dot = 2 * NV * NV
    rows, amp, vir_give = call(
        functools.partial(amplitudes, len(row_arrays)),
        [((NP, NV), bf16), ((NV, NV), bf16), ((NV, HALF_V), f32)],
        [place, *row_arrays, own_cols, other_cols, row_energy, vir_energy[None, :]],
        [((NP, NV), bf16)],
        dot * (NP + HALF_V),
    )
    vir_got = swap(vir_give, "c")
    vir_keep, three_give = call(
        give_and_keep, [((NV, HALF_V), f32), ((HALF_P, NV), f32)], [place, rows, amp], (), dot * (HALF_V + HALF_P)
    )
    three_got = swap(three_give, "c")
    (packed,) = call(pack_virtual, [((NV // 6 * 8, HALF_V), f32)], [vir_keep, vir_got])
    sent = packed.astype(jnp.float16).reshape(NV // 6, 8, HALF_V)
    met = lax.all_to_all(sent, OCC + CHIPS, split_axis=0, concat_axis=0, tiled=True)

    pieces = call(
        keep_three,
        [((PW, NV), f32)] * (Y * XH),
        [place, rows, amp, three_got],
        [((HALF_P, NV), f32)],
        dot * HALF_P,
    )
    three = pieces[0]
    for hop in range(1, Y * XH):
        three = three + next_chip(pieces[hop], hop)
    three_index = three[:, None, :]

    met = met.astype(f32)
    weight = jnp.exp2(met[:, 6:7, :] - SCALE)
    vir = jnp.sum(met[:, :6, :] * weight, 0).reshape(C, 3, HALF_V)
    give, keep = jnp.where(c == 0, vir[1], vir[0]), jnp.where(c == 0, vir[0], vir[1])
    got = swap(give, "c")
    vir_rows = jnp.concatenate([jnp.where(c == 0, keep, got), jnp.where(c == 0, got, keep)], 1)
    return (three_index, vir_rows / (NO * NV))


def solution(mesh):
    fine = Mesh(mesh.devices.reshape(XL, Z, Y, XH, C), ALL)
    return jax.shard_map(
        per_device,
        mesh=fine,
        in_specs=(P(None, AUX, None), P(None, OCC), P(), P()),
        out_specs=(P(AUX, OCC, None), P(ALL, None)),
        check_vma=False,
    )
```

time: 172 us -> 157 us (0.913)
  waiting for transfers between devices: 71 us -> 46.9 us
  blocking collectives: 0 us -> 20.5 us
  starting transfers between devices: 56.5 us -> 51.4 us
  local copies, waits for them, and re-layouts: 21.2 us -> 16.6 us
  other arithmetic: 8.95 us -> 5.41 us
  Pallas kernels: 9.07 us -> 10.9 us
    all_to_all x4 -> x2, waiting for transfers between devices: 51.5 us -> 18.8 us  [the longest x1 12.3 us: per_device(): lax.all_to_all(jnp.broadcast_to(local, (Y * XH, PW, NV)), CHIPS, split_ax...]
    all_to_all x0 -> x1, blocking collectives: none -> 20.5 us  [per_device(): local = lax.all_to_all(native, OCC, split_axis=0, concat_axis=0, tiled=True)]
    all_to_all x4 -> x2, starting transfers between devices: 28.2 us -> 17.6 us  [the longest x1 10.2 us: per_device(): lax.all_to_all(sent, OCC + CHIPS, split_axis=0, concat_axis=0, tiled=True)]
    ppermute x7, waiting for transfers between devices: 1.75 us -> 8.41 us  [next_chip(): return lax.ppermute(array, CHIPS, pairs)]
    add x2 -> x0, other arithmetic: 6.03 us -> none  [the longest x1 3.24 us: per_device(): three = keep + swap(give, 'c')]
    ppermute x1, waiting for transfers between devices: 0.01 us -> 4.01 us  [per_device(): lax.ppermute(flat, ALL, [(o * NO + x, x * NO + o) for o in range(NO) for...]
    ppermute x4 -> x5, starting transfers between devices: 1.65 us -> 5.49 us  [swap(): return lax.ppermute(array, axis, [(0, 1), (1, 0)])]
    ppermute x4 -> x5, waiting for transfers between devices: 6.72 us -> 3.83 us  [swap(): return lax.ppermute(array, axis, [(0, 1), (1, 0)])]
  transfers between devices with their start and end apart: 24 -> 23, of which waited for: 11 -> 13; matrix products, arithmetic and copies ran while one was open for 11% -> 6% of each run, Pallas kernels for 0% -> 4%
where the time goes in v2:
time: 157 us; the launch traced here: 155 us
  starting transfers between devices  51.4 us (33%)
  waiting for transfers between devices  46.9 us (30%)
  blocking collectives  20.5 us (13%)
  local copies, waits for them, and re-layouts  16.6 us (11%)
  Pallas kernels  10.9 us (7%)
  other arithmetic  5.41 us (3%)
  matrix products  1.99 us (1%)
    all_to_all x1, blocking collectives, per_device(): local = lax.all_to_all(native, OCC, split_axis=0, concat_axis=0, tiled=True)  20.5 us
    ppermute x7, starting transfers between devices, next_chip(): return lax.ppermute(array, CHIPS, pairs)  15.1 us
    unnamed x45, local copies, waits for them, and re-layouts  12.3 us
    all_to_all x1, waiting for transfers between devices, per_device(): lax.all_to_all(jnp.broadcast_to(local, (Y * XH, PW, NV)), CHIPS, split_ax...  12.3 us
    ppermute x8, waiting for transfers between devices, ring(): return lax.ppermute(array, 'z', [(i, (i + by) % Z) for i in range(Z)])  11.8 us
    ppermute x8, starting transfers between devices, ring(): return lax.ppermute(array, 'z', [(i, (i + by) % Z) for i in range(Z)])  11.3 us
    pallas_call x4, Pallas kernels, call(): pl.pallas_call(kernel, out_shape=[jax.ShapeDtypeStruct(s, t) for s, t in...  10.9 us
    all_to_all x1, starting transfers between devices, per_device(): lax.all_to_all(sent, OCC + CHIPS, split_axis=0, concat_axis=0, tiled=True)  10.2 us
  transfers between devices with their start and end apart: 23, of which 13 were waited for; matrix products, arithmetic and copies ran while one was open for 6% of the time, Pallas kernels for 4%

profile of v2, /device:TPU:32, one launch (start us, length us, event | category | flops | bytes accessed | tf_op | source)
XLA Modules:
  0.0 155.0 jit_solution(7010435268499463956)
XLA Ops:
  2.2 2.0 %convolution_convert_fusion = bf16[16,64,48]{1,2,0:T(8,128)(2,1)S(1)} fusion(bf16[16,64,1024]{2,1,0:T(8,128)(2,1)S(1)} %copy-done, bf16[1024,48]{0,1:T(8,128)(2,1)} %param.5), kind=kOutput, calls=%fused_computation.2 | convolution fusion | flops 100712448 | bytes 2293760 | tf_op jit(solution)/shard_map/ipm,ma->ipa/dot_general | solution.py:141
  4.4 1.9 %collective-permute-start = (bf16[64,768]{1,0:T(8,128)(2,1)S(1)}, bf16[64,768]{1,0:T(8,128)(2,1)S(1)}, u32[]{:S(2)}, u32[]{:S(2)}) collective-permute-start(bf16[64,768]{1,0:T(8,128)(2,1)S(1)} %copy.13), channel_id=1, source_target_pairs={{0,0},{1,16},{2,32},{3,48},{4,64},{5,80},{6,96},{7,112},{8,128},{9... | collective-permute-start | bytes 294920 | tf_op jit(solution)/shard_map/ppermute | solution.py:146
  6.3 4.0 %collective-permute-done = bf16[64,768]{1,0:T(8,128)(2,1)S(1)} collective-permute-done((bf16[64,768]{1,0:T(8,128)(2,1)S(1)}, bf16[64,768]{1,0:T(8,128)(2,1)S(1)}, u32[]{:S(2)}, u32[]{:S(2)}) %collective-permute-start) | collective-permute-done | bytes 98336 | tf_op jit(solution)/shard_map/ppermute | solution.py:146
  10.3 4.8 %collective-permute-start.1 = (bf16[64,768]{1,0:T(8,128)(2,1)S(1)}, bf16[64,768]{1,0:T(8,128)(2,1)S(1)}, u32[]{:S(2)}, u32[]{:S(2)}) collective-permute-start(bf16[64,768]{1,0:T(8,128)(2,1)S(1)} %collective-permute-done), channel_id=1, source_target_pairs={{0,128},{128,0},{1,129},{129,1},{2,130},{130,2},{3,131},{131,3},{4... | collective-permute-start | bytes 294920 | tf_op jit(solution)/shard_map/ppermute | solution.py:23
  15.1 3.8 %collective-permute-done.1 = bf16[64,768]{1,0:T(8,128)(2,1)S(1)} collective-permute-done((bf16[64,768]{1,0:T(8,128)(2,1)S(1)}, bf16[64,768]{1,0:T(8,128)(2,1)S(1)}, u32[]{:S(2)}, u32[]{:S(2)}) %collective-permute-start.1) | collective-permute-done | bytes 98336 | tf_op jit(solution)/shard_map/ppermute | solution.py:23
  18.9 4.3 %collective-permute-start.2 = (bf16[128,768]{1,0:T(8,128)(2,1)S(1)}, bf16[128,768]{1,0:T(8,128)(2,1)S(1)}, u32[]{:S(2)}, u32[]{:S(2)}) collective-permute-start(bf16[128,768]{1,0:T(8,128)(2,1)S(1)} %constant_dynamic-update-slice_fusion.refs_0_), channel_id=1, source_target_pairs={{0,16},{16,32},{32,48},{48,64},{64,80},{80,96},{96,112},{112,0},{1... | collective-permute-start | bytes 589832 | tf_op jit(solution)/shard_map/ppermute | solution.py:27
  23.4 20.5 %all_to_all.15 = bf16[16,2,1536]{2,1,0:T(2,128)(2,1)S(1)} all-to-all(bf16[16,2,1536]{2,1,0:T(2,128)(2,1)S(1)} %reshape.51), channel_id=1, replica_groups=mesh['xl'=2,'z'=8,'y'=4,'xh'=2,'c'=2] {'xl','z'}, dimensions={0} | all-to-all | bytes 196608 | tf_op jit(solution)/shard_map/all_to_all | solution.py:149
  45.2 7.4 %all-to-all-start.1 = ((bf16[8,64,768]{2,1,0:T(8,128)(2,1)}), bf16[8,64,768]{2,1,0:T(8,128)(2,1)S(1)}, u32[]{:S(2)}, u32[]{:S(2)}) async-start(bf16[8,64,768]{2,1,0:T(8,128)(2,1)} %broadcast_in_dim.11), calls=%async_computation.1 | async-start | bytes 1572864 | tf_op jit(solution)/shard_map/all_to_all | solution.py:152
  53.5 12.3 %all-to-all-done.1 = bf16[8,64,768]{2,1,0:T(8,128)(2,1)S(1)} async-done(((bf16[8,64,768]{2,1,0:T(8,128)(2,1)}), bf16[8,64,768]{2,1,0:T(8,128)(2,1)S(1)}, u32[]{:S(2)}, u32[]{:S(2)}) %all-to-all-start.1) | async-done | bytes 786464 | tf_op jit(solution)/shard_map/all_to_all | solution.py:152
  69.3 4.0 %collective-permute-done.5.refs_4_ = bf16[128,768]{1,0:T(8,128)(2,1)} collective-permute-done((bf16[128,768]{1,0:T(8,128)(2,1)S(1)}, bf16[128,768]{1,0:T(8,128)(2,1)}, u32[]{:S(2)}, u32[]{:S(2)}) %collective-permute-start.5) | collective-permute-done | bytes 196640 | tf_op jit(solution)/shard_map/ppermute | solution.py:27
  76.3 3.6 %collective-permute-done.7.refs_6_ = bf16[128,768]{1,0:T(8,128)(2,1)S(1)} collective-permute-done((bf16[128,768]{1,0:T(8,128)(2,1)}, bf16[128,768]{1,0:T(8,128)(2,1)S(1)}, u32[]{:S(2)}, u32[]{:S(2)}) %collective-permute-start.7) | collective-permute-done | bytes 196640 | tf_op jit(solution)/shard_map/ppermute | solution.py:27
  85.5 3.2 %collective-permute-done.8.refs_7_ = bf16[64,768]{1,0:T(8,128)(2,1)} collective-permute-done((bf16[64,768]{1,0:T(8,128)(2,1)}, bf16[64,768]{1,0:T(8,128)(2,1)}, u32[]{:S(2)}, u32[]{:S(2)}) %collective-permute-start.8) | collective-permute-done | bytes 98336 | tf_op jit(solution)/shard_map/ppermute | solution.py:27
  94.6 4.1 %shard_map.59 = (bf16[1024,768]{1,0:T(8,128)(2,1)S(1)}, bf16[768,768]{1,0:T(8,128)(2,1)S(1)}, f32[768,384]{1,0:T(8,128)S(1)}) custom-call(s32[25]{0:T(128)S(1)} %stack.103.place, bf16[128,768]{1,0:T(8,128)(2,1)S(1)} %copy-done.9, bf16[128,768]{1,0:T(8,128)(2,1)S(1)} %copy-done.11, bf16[128,768]{1,0:T(8,128)(2,1)S(1)} %copy-done.13, ...), custom_call_target="tpu_custom_call" | custom-call | flops 1660944384 | bytes 6291456 | tf_op jit(solution)/shard_map/pallas_call | solution.py:126
  98.8 3.1 %shard_map.60 = (f32[768,384]{1,0:T(8,128)S(1)}, f32[512,768]{1,0:T(8,128)}) custom-call(s32[25]{0:T(128)S(1)} %stack.103.place, bf16[1024,768]{1,0:T(8,128)(2,1)S(1)} %get-tuple-element.17.rows, bf16[768,768]{1,0:T(8,128)(2,1)S(1)} %get-tuple-element.18.amp), custom_call_target="tpu_custom_call" | custom-call | flops 1056964608 | bytes 6291456 | tf_op jit(solution)/shard_map/pallas_call | solution.py:126
  103.9 10.2 %all-to-all-start.2 = ((f16[128,8,384]{2,1,0:T(8,128)(2,1)}), f16[128,8,384]{2,1,0:T(8,128)(2,1)}, u32[]{:S(2)}, u32[]{:S(2)}) async-start(f16[128,8,384]{2,1,0:T(8,128)(2,1)} %convert_bitcast_fusion), calls=%async_computation.2 | async-start | bytes 1572864 | tf_op jit(solution)/shard_map/all_to_all | solution.py:180
  115.5 3.2 %shard_map.61 = (f32[64,768]{1,0:T(8,128)S(1)}, f32[64,768]{1,0:T(8,128)}, f32[64,768]{1,0:T(8,128)}, f32[64,768]{1,0:T(8,128)}, f32[64,768]{1,0:T(8,128)}, /*in...) custom-call(s32[25]{0:T(128)S(1)} %stack.103.place, bf16[1024,768]{1,0:T(8,128)(2,1)S(1)} %copy-done.2, ...), custom_call_target="tpu_custom_call" | custom-call | flops 603979776 | bytes 6291456 | tf_op jit(solution)/shard_map/pallas_call | solution.py:126
  120.1 3.0 %collective-permute-start.12 = (f32[64,768]{1,0:T(8,128)}, f32[64,768]{1,0:T(8,128)S(1)}, u32[]{:S(2)}, u32[]{:S(2)}) collective-permute-start(f32[64,768]{1,0:T(8,128)} %get-tuple-element.21), channel_id=1, source_target_pairs={{0,2},{2,0},{4,6},{6,4},{8,10},{10,8},{12,14},{14,12},{1,3},{3,1},... | collective-permute-start | bytes 589832 | tf_op jit(solution)/shard_map/ppermute | solution.py:32
  126.0 1.8 %collective-permute-start.15 = (f32[64,768]{1,0:T(8,128)}, f32[64,768]{1,0:T(8,128)}, u32[]{:S(2)}, u32[]{:S(2)}) collective-permute-start(f32[64,768]{1,0:T(8,128)} %get-tuple-element.24), channel_id=1, source_target_pairs={{0,8},{2,10},{4,12},{6,14},{8,0},{10,2},{12,4},{14,6},{1,9},{3,11}... | collective-permute-start | bytes 589832 | tf_op jit(solution)/shard_map/ppermute | solution.py:32
  127.7 4.2 %collective-permute-start.16 = (f32[64,768]{1,0:T(8,128)}, f32[64,768]{1,0:T(8,128)}, u32[]{:S(2)}, u32[]{:S(2)}) collective-permute-start(f32[64,768]{1,0:T(8,128)} %get-tuple-element.25), channel_id=1, source_target_pairs={{0,10},{2,8},{4,14},{6,12},{8,2},{10,0},{12,6},{14,4},{1,11},{3,9}... | collective-permute-start | bytes 589832 | tf_op jit(solution)/shard_map/ppermute | solution.py:32
  131.9 6.5 %all-to-all-done.2 = f16[128,8,384]{2,1,0:T(8,128)(2,1)} async-done(((f16[128,8,384]{2,1,0:T(8,128)(2,1)}), f16[128,8,384]{2,1,0:T(8,128)(2,1)}, u32[]{:S(2)}, u32[]{:S(2)}) %all-to-all-start.2) | async-done | bytes 786464 | tf_op jit(solution)/shard_map/all_to_all | solution.py:180
  142.0 2.2 %collective-permute-done.13 = f32[64,768]{1,0:T(8,128)S(1)} collective-permute-done((f32[64,768]{1,0:T(8,128)}, f32[64,768]{1,0:T(8,128)S(1)}, u32[]{:S(2)}, u32[]{:S(2)}) %collective-permute-start.13) | collective-permute-done | bytes 196640 | tf_op jit(solution)/shard_map/ppermute | solution.py:32
  144.3 1.8 %collective-permute-start.18 = (f32[64,768]{1,0:T(8,128)S(1)}, f32[64,768]{1,0:T(8,128)S(1)}, u32[]{:S(2)}, u32[]{:S(2)}) collective-permute-start(f32[64,768]{1,0:T(8,128)S(1)} %copy-done.15), channel_id=1, source_target_pairs={{0,14},{2,12},{4,2},{6,0},{8,6},{10,4},{12,10},{14,8},{1,15},{3,13... | collective-permute-start | bytes 589832 | tf_op jit(solution)/shard_map/ppermute | solution.py:32
  146.2 2.1 %collective-permute-done.15 = f32[64,768]{1,0:T(8,128)} collective-permute-done((f32[64,768]{1,0:T(8,128)}, f32[64,768]{1,0:T(8,128)}, u32[]{:S(2)}, u32[]{:S(2)}) %collective-permute-start.15) | collective-permute-done | bytes 196640 | tf_op jit(solution)/shard_map/ppermute | solution.py:32
  148.3 4.0 %collective-permute-done.18 = f32[64,768]{1,0:T(8,128)S(1)} collective-permute-done((f32[64,768]{1,0:T(8,128)S(1)}, f32[64,768]{1,0:T(8,128)S(1)}, u32[]{:S(2)}, u32[]{:S(2)}) %collective-permute-start.18) | collective-permute-done | bytes 196640 | tf_op jit(solution)/shard_map/ppermute | solution.py:32
  (94 shorter events, 35.6 us)
Async XLA Ops:
  4.4 5.9 %collective-permute-start = (bf16[64,768]{1,0:T(8,128)(2,1)S(1)}, bf16[64,768]{1,0:T(8,128)(2,1)S(1)}, u32[]{:S(2)}, u32[]{:S(2)}) collective-permute-start(bf16[64,768]{1,0:T(8,128)(2,1)S(1)} %copy.13), channel_id=1, source_target_pairs={{0,0},{1,16},{2,32},{3,48},{4,64},{5,80},{6,96},{7,112},{8,128},{9... | collective-permute-start | bytes 294920 | tf_op jit(solution)/shard_map/ppermute | solution.py:146
  10.3 8.6 %collective-permute-start.1 = (bf16[64,768]{1,0:T(8,128)(2,1)S(1)}, bf16[64,768]{1,0:T(8,128)(2,1)S(1)}, u32[]{:S(2)}, u32[]{:S(2)}) collective-permute-start(bf16[64,768]{1,0:T(8,128)(2,1)S(1)} %collective-permute-done), channel_id=1, source_target_pairs={{0,128},{128,0},{1,129},{129,1},{2,130},{130,2},{3,131},{131,3},{4... | collective-permute-start | bytes 294920 | tf_op jit(solution)/shard_map/ppermute | solution.py:23
  18.9 25.1 %collective-permute-start.2 = (bf16[128,768]{1,0:T(8,128)(2,1)S(1)}, bf16[128,768]{1,0:T(8,128)(2,1)S(1)}, u32[]{:S(2)}, u32[]{:S(2)}) collective-permute-start(bf16[128,768]{1,0:T(8,128)(2,1)S(1)} %constant_dynamic-update-slice_fusion.refs_0_), channel_id=1, source_target_pairs={{0,16},{16,32},{32,48},{48,64},{64,80},{80,96},{96,112},{112,0},{1... | collective-permute-start | bytes 589832 | tf_op jit(solution)/shard_map/ppermute | solution.py:27
  44.1 38.2 %copy-start.10 = (bf16[128,768]{1,0:T(8,128)(2,1)}, bf16[128,768]{1,0:T(8,128)(2,1)S(1)}, u32[]{:S(2)}) copy-start(bf16[128,768]{1,0:T(8,128)(2,1)S(1)} %collective-permute-done.2.refs_1_) | copy-start | bytes 589828
  45.2 20.7 %all-to-all-start.1 = ((bf16[8,64,768]{2,1,0:T(8,128)(2,1)}), bf16[8,64,768]{2,1,0:T(8,128)(2,1)S(1)}, u32[]{:S(2)}, u32[]{:S(2)}) async-start(bf16[8,64,768]{2,1,0:T(8,128)(2,1)} %broadcast_in_dim.11), calls=%async_computation.1 | async-start | bytes 1572864 | tf_op jit(solution)/shard_map/all_to_all | solution.py:152
  52.6 13.2 %collective-permute-start.3 = (bf16[128,768]{1,0:T(8,128)(2,1)S(1)}, bf16[128,768]{1,0:T(8,128)(2,1)S(1)}, u32[]{:S(2)}, u32[]{:S(2)}) collective-permute-start(bf16[128,768]{1,0:T(8,128)(2,1)S(1)} %constant_dynamic-update-slice_fusion.refs_0_), channel_id=1, source_target_pairs={{0,112},{16,0},{32,16},{48,32},{64,48},{80,64},{96,80},{112,96},{1... | collective-permute-start | bytes 589832 | tf_op jit(solution)/shard_map/ppermute | solution.py:27
  65.8 22.9 %collective-permute-start.10 = (bf16[512,768]{1,0:T(8,128)(2,1)S(1)}, bf16[512,768]{1,0:T(8,128)(2,1)}, u32[]{:S(2)}, u32[]{:S(2)}) collective-permute-start(bf16[512,768]{1,0:T(8,128)(2,1)S(1)} %bitcast.46), channel_id=1, source_target_pairs={{0,1},{1,0},{2,3},{3,2},{4,5},{5,4},{6,7},{7,6},{8,9},{9,8},{10,11... | collective-permute-start | bytes 2359304 | tf_op jit(solution)/shard_map/ppermute | solution.py:23
  65.8 7.4 %collective-permute-start.5 = (bf16[128,768]{1,0:T(8,128)(2,1)S(1)}, bf16[128,768]{1,0:T(8,128)(2,1)}, u32[]{:S(2)}, u32[]{:S(2)}) collective-permute-start(bf16[128,768]{1,0:T(8,128)(2,1)S(1)} %collective-permute-done.3.refs_2_), channel_id=1, source_target_pairs={{0,112},{16,0},{32,16},{48,32},{64,48},{80,64},{96,80},{112,96},{1... | collective-permute-start | bytes 589832 | tf_op jit(solution)/shard_map/ppermute | solution.py:27
  67.2 7.1 %collective-permute-start.4 = (bf16[128,768]{1,0:T(8,128)(2,1)S(1)}, bf16[128,768]{1,0:T(8,128)(2,1)}, u32[]{:S(2)}, u32[]{:S(2)}) collective-permute-start(bf16[128,768]{1,0:T(8,128)(2,1)S(1)} %collective-permute-done.2.refs_1_), channel_id=1, source_target_pairs={{0,16},{16,32},{32,48},{48,64},{64,80},{80,96},{96,112},{112,0},{1... | collective-permute-start | bytes 589832 | tf_op jit(solution)/shard_map/ppermute | solution.py:27
  73.3 6.7 %collective-permute-start.7 = (bf16[128,768]{1,0:T(8,128)(2,1)}, bf16[128,768]{1,0:T(8,128)(2,1)S(1)}, u32[]{:S(2)}, u32[]{:S(2)}) collective-permute-start(bf16[128,768]{1,0:T(8,128)(2,1)} %collective-permute-done.5.refs_4_), channel_id=1, source_target_pairs={{0,112},{16,0},{32,16},{48,32},{64,48},{80,64},{96,80},{112,96},{1... | collective-permute-start | bytes 589832 | tf_op jit(solution)/shard_map/ppermute | solution.py:27
  74.2 7.4 %collective-permute-start.6 = (bf16[128,768]{1,0:T(8,128)(2,1)}, bf16[128,768]{1,0:T(8,128)(2,1)S(1)}, u32[]{:S(2)}, u32[]{:S(2)}) collective-permute-start(bf16[128,768]{1,0:T(8,128)(2,1)} %collective-permute-done.4.refs_3_), channel_id=1, source_target_pairs={{0,16},{16,32},{32,48},{48,64},{64,80},{80,96},{96,112},{112,0},{1... | collective-permute-start | bytes 589832 | tf_op jit(solution)/shard_map/ppermute | solution.py:27
  80.6 4.9 %collective-permute-start.9 = (bf16[64,768]{1,0:T(8,128)(2,1)}, bf16[64,768]{1,0:T(8,128)(2,1)}, u32[]{:S(2)}, u32[]{:S(2)}) collective-permute-start(bf16[64,768]{1,0:T(8,128)(2,1)} %slice.29), channel_id=1, source_target_pairs={{0,112},{16,0},{32,16},{48,32},{64,48},{80,64},{96,80},{112,96},{1... | collective-permute-start | bytes 294920 | tf_op jit(solution)/shard_map/ppermute | solution.py:27
  82.3 6.4 %collective-permute-start.8 = (bf16[64,768]{1,0:T(8,128)(2,1)}, bf16[64,768]{1,0:T(8,128)(2,1)}, u32[]{:S(2)}, u32[]{:S(2)}) collective-permute-start(bf16[64,768]{1,0:T(8,128)(2,1)} %slice.28), channel_id=1, source_target_pairs={{0,16},{16,32},{32,48},{48,64},{64,80},{80,96},{96,112},{112,0},{1... | collective-permute-start | bytes 294920 | tf_op jit(solution)/shard_map/ppermute | solution.py:27
  98.7 3.8 %collective-permute-start.19 = (f32[768,384]{1,0:T(8,128)S(1)}, f32[768,384]{1,0:T(8,128)S(1)}, u32[]{:S(2)}, u32[]{:S(2)}) collective-permute-start(f32[768,384]{1,0:T(8,128)S(1)} %get-tuple-element.29), channel_id=1, source_target_pairs={{0,1},{1,0},{2,3},{3,2},{4,5},{5,4},{6,7},{7,6},{8,9},{9,8},{10,11... | collective-permute-start | bytes 3538952 | tf_op jit(solution)/shard_map/ppermute | solution.py:23
  102.0 12.2 %collective-permute-start.11 = (f32[512,768]{1,0:T(8,128)}, f32[512,768]{1,0:T(8,128)}, u32[]{:S(2)}, u32[]{:S(2)}) collective-permute-start(f32[512,768]{1,0:T(8,128)} %get-tuple-element.19), channel_id=1, source_target_pairs={{0,1},{1,0},{2,3},{3,2},{4,5},{5,4},{6,7},{7,6},{8,9},{9,8},{10,11... | collective-permute-start | bytes 4718600 | tf_op jit(solution)/shard_map/ppermute | solution.py:23
  103.9 34.5 %all-to-all-start.2 = ((f16[128,8,384]{2,1,0:T(8,128)(2,1)}), f16[128,8,384]{2,1,0:T(8,128)(2,1)}, u32[]{:S(2)}, u32[]{:S(2)}) async-start(f16[128,8,384]{2,1,0:T(8,128)(2,1)} %convert_bitcast_fusion), calls=%async_computation.2 | async-start | bytes 1572864 | tf_op jit(solution)/shard_map/all_to_all | solution.py:180
  120.1 20.3 %collective-permute-start.12 = (f32[64,768]{1,0:T(8,128)}, f32[64,768]{1,0:T(8,128)S(1)}, u32[]{:S(2)}, u32[]{:S(2)}) collective-permute-start(f32[64,768]{1,0:T(8,128)} %get-tuple-element.21), channel_id=1, source_target_pairs={{0,2},{2,0},{4,6},{6,4},{8,10},{10,8},{12,14},{14,12},{1,3},{3,1},... | collective-permute-start | bytes 589832 | tf_op jit(solution)/shard_map/ppermute | solution.py:32
  123.0 21.2 %collective-permute-start.13 = (f32[64,768]{1,0:T(8,128)}, f32[64,768]{1,0:T(8,128)S(1)}, u32[]{:S(2)}, u32[]{:S(2)}) collective-permute-start(f32[64,768]{1,0:T(8,128)} %get-tuple-element.22), channel_id=1, source_target_pairs={{0,4},{2,6},{4,8},{6,10},{8,12},{10,14},{12,0},{14,2},{1,5},{3,7},... | collective-permute-start | bytes 589832 | tf_op jit(solution)/shard_map/ppermute | solution.py:32
  124.5 21.6 %collective-permute-start.14 = (f32[64,768]{1,0:T(8,128)}, f32[64,768]{1,0:T(8,128)}, u32[]{:S(2)}, u32[]{:S(2)}) collective-permute-start(f32[64,768]{1,0:T(8,128)} %get-tuple-element.23), channel_id=1, source_target_pairs={{0,6},{2,4},{4,10},{6,8},{8,14},{10,12},{12,2},{14,0},{1,7},{3,5},... | collective-permute-start | bytes 589832 | tf_op jit(solution)/shard_map/ppermute | solution.py:32
  126.0 22.3 %collective-permute-start.15 = (f32[64,768]{1,0:T(8,128)}, f32[64,768]{1,0:T(8,128)}, u32[]{:S(2)}, u32[]{:S(2)}) collective-permute-start(f32[64,768]{1,0:T(8,128)} %get-tuple-element.24), channel_id=1, source_target_pairs={{0,8},{2,10},{4,12},{6,14},{8,0},{10,2},{12,4},{14,6},{1,9},{3,11}... | collective-permute-start | bytes 589832 | tf_op jit(solution)/shard_map/ppermute | solution.py:32
  127.7 20.6 %collective-permute-start.16 = (f32[64,768]{1,0:T(8,128)}, f32[64,768]{1,0:T(8,128)}, u32[]{:S(2)}, u32[]{:S(2)}) collective-permute-start(f32[64,768]{1,0:T(8,128)} %get-tuple-element.25), channel_id=1, source_target_pairs={{0,10},{2,8},{4,14},{6,12},{8,2},{10,0},{12,6},{14,4},{1,11},{3,9}... | collective-permute-start | bytes 589832 | tf_op jit(solution)/shard_map/ppermute | solution.py:32
  140.5 7.8 %collective-permute-start.17 = (f32[64,768]{1,0:T(8,128)S(1)}, f32[64,768]{1,0:T(8,128)S(1)}, u32[]{:S(2)}, u32[]{:S(2)}) collective-permute-start(f32[64,768]{1,0:T(8,128)S(1)} %copy-done.17), channel_id=1, source_target_pairs={{0,12},{2,14},{4,0},{6,2},{8,4},{10,6},{12,8},{14,10},{1,13},{3,15... | collective-permute-start | bytes 589832 | tf_op jit(solution)/shard_map/ppermute | solution.py:32
  144.3 8.1 %collective-permute-start.18 = (f32[64,768]{1,0:T(8,128)S(1)}, f32[64,768]{1,0:T(8,128)S(1)}, u32[]{:S(2)}, u32[]{:S(2)}) collective-permute-start(f32[64,768]{1,0:T(8,128)S(1)} %copy-done.15), channel_id=1, source_target_pairs={{0,14},{2,12},{4,2},{6,0},{8,6},{10,4},{12,10},{14,8},{1,15},{3,13... | collective-permute-start | bytes 589832 | tf_op jit(solution)/shard_map/ppermute | solution.py:32
  146.1 8.3 %collective-permute-start.20 = (f32[3,384]{1,0:T(4,128)S(1)}, f32[3,384]{1,0:T(4,128)S(1)}, u32[]{:S(2)}, u32[]{:S(2)}) collective-permute-start(f32[3,384]{1,0:T(4,128)S(1)} %slice_select_fusion), channel_id=1, source_target_pairs={{0,1},{1,0},{2,3},{3,2},{4,5},{5,4},{6,7},{7,6},{8,9},{9,8},{10,11... | collective-permute-start | bytes 13832 | tf_op jit(solution)/shard_map/ppermute | solution.py:23
  (19 other events, 133.4 us)

commit v3 on v2

v3 whole, which is shorter than its diff:
```python
import functools

import jax
import jax.numpy as jnp
import numpy as np
from jax import lax
from jax.experimental import pallas as pl
from jax.experimental.pallas import tpu as pltpu
from jax.sharding import Mesh, PartitionSpec as P

OCC = ("xl", "z")
CHIPS = ("y", "xh")
AUX = ("y", "xh", "c")
ALL = OCC + AUX
XL, Z, Y, XH, C = 2, 8, 4, 2, 2
NO, NV, NP = 16, 768, 1024
PW, VW = 64, 48
VMEM = pl.BlockSpec(memory_space=pltpu.VMEM)
SMEM = pl.BlockSpec(memory_space=pltpu.SMEM)


def swap(array, axis):
    return lax.ppermute(array, axis, [(0, 1), (1, 0)])


def ring(array, by):
    return lax.ppermute(array, "z", [(i, (i + by) % Z) for i in range(Z)])


def next_chip(array, hop):
    pairs = [(q, hop_from(q, hop)) for q in range(Y * XH)]
    return lax.ppermute(array, CHIPS, pairs)


def hop_from(q, hop):
    return (q // XH + hop // XH) % Y * XH + (q + hop) % XH


def paced(array, us):
    def kernel(given, out):
        out[...] = given[...]

    return pl.pallas_call(
        kernel,
        out_shape=jax.ShapeDtypeStruct(array.shape, array.dtype),
        in_specs=[VMEM],
        out_specs=VMEM,
        cost_estimate=pl.CostEstimate(flops=us * 10**9, bytes_accessed=2**20, transcendentals=0),
    )(array)


TRANSPOSED = (((0,), (0,)), ((), ()))
HALF_P, HALF_V = NP // C, NV // C


def amplitudes(n_rows, place, *refs):
    row_refs, (own_cols, other_cols, row_energy, col_energy) = refs[:n_rows], refs[n_rows : n_rows + 4]
    rows, amp, vir, cols, sems = refs[n_rows + 4 :]
    core = place[24]
    moves = []
    for ref in row_refs:
        for part in range(ref.shape[0] // PW):
            start = pl.multiple_of(place[len(moves)], PW)
            moves.append((ref.at[pl.ds(part * PW, PW)], rows.at[pl.ds(start, PW)]))
    for ref, side in ((own_cols, core), (other_cols, 1 - core)):
        moves.append((ref, cols.at[pl.ds(pl.multiple_of(side * HALF_P, HALF_P), HALF_P)]))
    copies = [pltpu.make_async_copy(f, t, sems.at[k]) for k, (f, t) in enumerate(moves)]
    for copy in copies:
        copy.start()
    for copy in copies:
        copy.wait()
    for k in range(NV // 256):
        here = slice(k * 256, (k + 1) * 256)
        coulomb = lax.dot_general(
            rows[:, here], cols[...], TRANSPOSED, preferred_element_type=jnp.float32
        )
        amp[here, :] = (coulomb / (row_energy[here, :] - col_energy[...])).astype(jnp.bfloat16)
    virtual_block(amp, 1 - core, vir)


def virtual_block(amp, half, vir):
    side = amp[:, pl.ds(pl.multiple_of(half * HALF_V, HALF_V), HALF_V)]
    for k in range(NV // 256):
        here = slice(k * 256, (k + 1) * 256)
        vir[here, :] = lax.dot_general(
            amp[:, here], side, TRANSPOSED, preferred_element_type=jnp.float32
        )


def give_and_keep(place, rows, amp, vir, give, keep):
    core = place[24]
    for out, side in ((give, 1 - core), (keep, core)):
        start = pl.multiple_of(side * HALF_P, HALF_P)
        out[...] = jnp.dot(rows[pl.ds(start, HALF_P), :], amp[...], preferred_element_type=jnp.float32)
    virtual_block(amp, core, vir)


def pack_virtual(keep, got, out):
    total = keep[...] + got[...]
    top = jnp.maximum(jnp.max(jnp.abs(total), keepdims=True), 2.0**-100)
    power = jnp.ceil(jnp.log2(top))
    total = total * jnp.exp2(SCALE - power)
    tail = jnp.broadcast_to(power, (8, HALF_V))
    for g in range(NO):
        out[g, :VW, :] = total[VW * g : VW * g + VW, :]
        out[g, VW:, :] = tail


def add_three(place, keep, got, *outs):
    *outs, total, sems = outs
    total[...] = keep[...] + got[...]
    copies = [
        pltpu.make_async_copy(total.at[pl.ds(pl.multiple_of(place[16 + hop], PW), PW)], out, sems.at[hop])
        for hop, out in enumerate(outs)
    ]
    for copy in copies:
        copy.start()
    for copy in copies:
        copy.wait()


SCALE = 14.0
PACE = 25


def call(kernel, shapes, args, scratch=(), flops=0, anywhere=0, n_sems=0, out_space=pltpu.VMEM):
    spaces = [SMEM if a.dtype == jnp.int32 else VMEM for a in args]
    first = 1 if args[0].dtype == jnp.int32 else 0
    spaces[first : first + anywhere] = [pl.BlockSpec(memory_space=pl.ANY)] * anywhere
    sems = [pltpu.SemaphoreType.DMA((n_sems,))] if n_sems else []
    return pl.pallas_call(
        kernel,
        out_shape=[jax.ShapeDtypeStruct(s, t) for s, t in shapes],
        in_specs=spaces,
        out_specs=[pl.BlockSpec(memory_space=out_space)] * len(shapes),
        scratch_shapes=[pltpu.VMEM(s, t) for s, t in scratch] + sems,
        compiler_params=pltpu.CompilerParams(vmem_limit_bytes=32 * 2**20),
        cost_estimate=pl.CostEstimate(flops=flops, bytes_accessed=6 * 2**20, transcendentals=0),
    )(*args)


def per_device(half_integrals, vir_coef, occ_energy, vir_energy):
    xl, z, y, xh, c = (lax.axis_index(n) for n in ALL)
    own = xl * Z + z
    chip = y * XH + xh
    native = jnp.einsum(
        "ipm,ma->ipa", half_integrals, vir_coef, preferred_element_type=jnp.float32
    ).astype(jnp.bfloat16)

    flat = jnp.transpose(native, (1, 0, 2)).reshape(PW, NV)
    pair = jnp.concatenate(
        [
            lax.ppermute(flat, ALL, [(o * NO + x, (x ^ flip) * NO + o) for o in range(NO) for x in range(NO)])
            for flip in (0, Z)
        ],
        0,
    )
    slice_energy = lax.dynamic_slice_in_dim(vir_energy, (chip * C + c) * VW, VW, 0)
    own_energy = lax.dynamic_slice_in_dim(occ_energy, own, 1, 0)
    row_energy = ((own_energy + occ_energy)[:, None] - slice_energy[None, :]).reshape(NV, 1)
    col_energy = vir_energy[None, :]

    pair, native, row_energy = lax.optimization_barrier((pair, native, row_energy))
    up1, down1, up2, down2 = (ring(pair, by) for by in (1, -1, 2, -2))
    row_energy = paced(row_energy, PACE)
    local = lax.all_to_all(native, OCC, split_axis=0, concat_axis=0, tiled=True)
    local = jnp.transpose(local, (1, 0, 2)).reshape(PW, NV)
    local, up2, down2, col_energy, row_energy = lax.optimization_barrier(
        (local, up2, down2, col_energy, row_energy)
    )
    up3, down3 = ring(up2, 1), ring(down2, -1)
    up4, down4 = ring(up2[:PW], 2), ring(down2[PW:], -2)
    col_energy = paced(col_energy, PACE)
    own_cols = lax.all_to_all(
        jnp.broadcast_to(local, (Y * XH, PW, NV)), CHIPS, split_axis=0, concat_axis=0, tiled=True
    ).reshape(HALF_P, NV)
    other_cols = swap(own_cols, "c")
    row_arrays = [pair, up1, down1, up2, down2, up3, down3, up4, down4]
    owners = []
    for step in (0, -1, 1, -2, 2, -3, 3, Z // 2):
        owners += [(xl * Z + (z + step) % Z), ((1 - xl) * Z + (z + step) % Z)]
    places = [o % C * HALF_P + o // C * PW for o in owners]
    places += [hop_from(chip, hop) * PW for hop in range(Y * XH)] + [c]
    place = jnp.stack(places).astype(jnp.int32)

    bf16, f32 = jnp.bfloat16, jnp.float32
    dot = 2 * NV * NV
    rows, amp, vir_give = call(
        functools.partial(amplitudes, len(row_arrays)),
        [((NP, NV), bf16), ((NV, NV), bf16), ((NV, HALF_V), f32)],
        [place, *row_arrays, own_cols, other_cols, row_energy, col_energy],
        [((NP, NV), bf16)],
        dot * (NP + HALF_V),
        len(row_arrays) + 2,
        NO + 2,
    )
    vir_got = swap(vir_give, "c")
    vir_keep, three_give, three_keep = call(
        give_and_keep,
        [((NV, HALF_V), f32), ((HALF_P, NV), f32), ((HALF_P, NV), f32)],
        [place, rows, amp],
        flops=dot * (HALF_V + NP),
    )
    three_got = swap(three_give, "c")
    (packed,) = call(pack_virtual, [((NO, VW + 8, HALF_V), f32)], [vir_keep, vir_got])
    met = lax.all_to_all(packed.astype(jnp.float16), OCC, split_axis=0, concat_axis=0, tiled=True)

    pieces = call(
        add_three,
        [((PW, NV), f32)] * (Y * XH),
        [place, three_keep, three_got],
        [((HALF_P, NV), f32)],
        n_sems=Y * XH,
        out_space=pltpu.HBM,
    )
    three = pieces[0]
    for hop in range(1, Y * XH):
        three = three + next_chip(pieces[hop], hop)
    three_index = three[:, None, :]

    met = met.astype(f32)
    vir = jnp.sum(met[:, :VW, :] * jnp.exp2(met[:, VW : VW + 1, :] - SCALE), 0)
    vir = vir.reshape(NO, VW // NO, HALF_V)
    vir = lax.all_to_all(vir, AUX, split_axis=0, concat_axis=0, tiled=True)
    vir = jnp.sum(vir.reshape(Y * XH, C, VW // NO, HALF_V), 0)
    vir_rows = jnp.concatenate([vir[0], vir[1]], 1)
    return (three_index, vir_rows / (NO * NV))


def solution(mesh):
    fine = Mesh(mesh.devices.reshape(XL, Z, Y, XH, C), ALL)
    return jax.shard_map(
        per_device,
        mesh=fine,
        in_specs=(P(None, AUX, None), P(None, OCC), P(), P()),
        out_specs=(P(AUX, OCC, None), P(ALL, None)),
        check_vma=False,
    )
```

time: 157 us -> 131 us (0.83)
  waiting for transfers between devices: 46.9 us -> 17.3 us
  starting transfers between devices: 51.4 us -> 76.4 us
  blocking collectives: 20.5 us -> 0 us
  Pallas kernels: 10.9 us -> 15.3 us
  local copies, waits for them, and re-layouts: 16.6 us -> 12.4 us
    all_to_all x1 -> x0, blocking collectives: 20.5 us -> none  [per_device(): local = lax.all_to_all(native, OCC, split_axis=0, concat_axis=0, tiled=True)]
    ppermute x8, starting transfers between devices: 11.3 us -> 28.1 us  [ring(): return lax.ppermute(array, 'z', [(i, (i + by) % Z) for i in range(Z)])]
    all_to_all x1, waiting for transfers between devices: 12.3 us -> 1.19 us  [per_device(): lax.all_to_all(jnp.broadcast_to(local, (Y * XH, PW, NV)), CHIPS, split_ax...]
    ppermute x8, waiting for transfers between devices: 11.8 us -> 2.14 us  [ring(): return lax.ppermute(array, 'z', [(i, (i + by) % Z) for i in range(Z)])]
    all_to_all x1 -> x3, starting transfers between devices: 10.2 us -> 17.8 us  [the longest x1 8 us: per_device(): local = lax.all_to_all(native, OCC, split_axis=0, concat_axis=0, tiled=True)]
    unnamed x45 -> x18, local copies, waits for them, and re-layouts: 12.3 us -> 6.82 us
    ppermute x5 -> x3, starting transfers between devices: 5.49 us -> 0.59 us  [swap(): return lax.ppermute(array, axis, [(0, 1), (1, 0)])]
    ppermute x5 -> x3, waiting for transfers between devices: 3.83 us -> 0.01 us  [swap(): return lax.ppermute(array, axis, [(0, 1), (1, 0)])]
  transfers between devices with their start and end apart: 23 -> 24, of which waited for: 13 -> 8; matrix products, arithmetic and copies ran while one was open for 6% -> 8% of each run, Pallas kernels for 4% -> 8%
where the time goes in v3:
time: 131 us; the launch traced here: 129 us
  starting transfers between devices  76.4 us (58%)
  waiting for transfers between devices  17.3 us (13%)
  Pallas kernels  15.3 us (12%)
  local copies, waits for them, and re-layouts  12.4 us (9%)
  other arithmetic  5.12 us (4%)
  matrix products  2 us (2%)
    ppermute x8, starting transfers between devices, ring(): return lax.ppermute(array, 'z', [(i, (i + by) % Z) for i in range(Z)])  28.1 us
    ppermute x7, starting transfers between devices, next_chip(): return lax.ppermute(array, CHIPS, pairs)  18.8 us
    pallas_call x4, Pallas kernels, call(): pl.pallas_call(kernel, out_shape=[jax.ShapeDtypeStruct(s, t) for s, t in...  12.3 us
    all_to_all x1, starting transfers between devices, per_device(): local = lax.all_to_all(native, OCC, split_axis=0, concat_axis=0, tiled=True)  8 us
    unnamed x18, local copies, waits for them, and re-layouts  6.82 us
    all_to_all x1, starting transfers between devices, per_device(): lax.all_to_all(jnp.broadcast_to(local, (Y * XH, PW, NV)), CHIPS, split_ax...  6.48 us
    all_to_all x1, starting transfers between devices, per_device(): lax.all_to_all(packed.astype(jnp.float16), OCC, split_axis=0, concat_axis...  6.34 us
    ppermute x7, waiting for transfers between devices, next_chip(): return lax.ppermute(array, CHIPS, pairs)  5.27 us
  transfers between devices with their start and end apart: 24, of which 8 were waited for; matrix products, arithmetic and copies ran while one was open for 8% of the time, Pallas kernels for 8%

profile of v3, /device:TPU:32, one launch (start us, length us, event | category | flops | bytes accessed | tf_op | source)
XLA Modules:
  0.0 129.4 jit_solution(15162839812329789184)
XLA Ops:
  0.7 1.6 %copy-done = bf16[16,64,1024]{2,1,0:T(8,128)(2,1)S(1)} copy-done((bf16[16,64,1024]{2,1,0:T(8,128)(2,1)S(1)}, bf16[16,64,1024]{2,1,0:T(8,128)(2,1)}, u32[]{:S(2)}) %copy-start) | copy-done | bytes 2097176
  2.2 2.0 %convolution_convert_fusion = bf16[16,64,48]{1,2,0:T(8,128)(2,1)S(1)} fusion(bf16[16,64,1024]{2,1,0:T(8,128)(2,1)S(1)} %copy-done, bf16[1024,48]{0,1:T(8,128)(2,1)} %param.5), kind=kOutput, calls=%fused_computation.2 | convolution fusion | flops 100712448 | bytes 2293760 | tf_op jit(solution)/shard_map/ipm,ma->ipa/dot_general | solution.py:146
  4.9 4.1 %collective-permute-start = (bf16[64,768]{1,0:T(8,128)(2,1)S(1)}, bf16[64,768]{1,0:T(8,128)(2,1)S(1)}, u32[]{:S(2)}, u32[]{:S(2)}) collective-permute-start(bf16[64,768]{1,0:T(8,128)(2,1)S(1)} %copy.13), channel_id=1, source_target_pairs={{0,0},{1,16},{2,32},{3,48},{4,64},{5,80},{6,96},{7,112},{8,128},{9... | collective-permute-start | bytes 294920 | tf_op jit(solution)/shard_map/ppermute | solution.py:153
  11.9 18.8 %collective-permute-start.5 = (bf16[128,768]{1,0:T(8,128)(2,1)S(1)}, bf16[128,768]{1,0:T(8,128)(2,1)S(1)}, u32[]{:S(2)}, u32[]{:S(2)}) collective-permute-start(bf16[128,768]{1,0:T(8,128)(2,1)S(1)} %pad_maximum_fusion.refs_0_), channel_id=1, source_target_pairs={{0,96},{16,112},{32,0},{48,16},{64,32},{80,48},{96,64},{112,80},{1... | collective-permute-start | bytes 589832 | tf_op jit(solution)/shard_map/ppermute | solution.py:27
  31.6 8.0 %all-to-all-start = ((bf16[16,2,1536]{2,1,0:T(2,128)(2,1)}), bf16[16,2,1536]{2,1,0:T(2,128)(2,1)S(1)}, u32[]{:S(2)}, u32[]{:S(2)}) async-start(bf16[16,2,1536]{2,1,0:T(2,128)(2,1)} %reshape.50), calls=%async_computation | async-start | bytes 196608 | tf_op jit(solution)/shard_map/all_to_all | solution.py:166
  40.5 1.8 %shard_map.59.refs_11_ = f32[768,1]{1,0:T(8,128)} custom-call(f32[768,1]{1,0:T(8,128)} %copy.10.given), custom_call_target="tpu_custom_call" | custom-call | flops 24999999488 | bytes 1048576 | tf_op jit(solution)/shard_map/pallas_call | solution.py:43
  42.3 5.1 %all-to-all-done = bf16[16,2,1536]{2,1,0:T(2,128)(2,1)S(1)} async-done(((bf16[16,2,1536]{2,1,0:T(2,128)(2,1)}), bf16[16,2,1536]{2,1,0:T(2,128)(2,1)S(1)}, u32[]{:S(2)}, u32[]{:S(2)}) %all-to-all-start) | async-done | bytes 98336 | tf_op jit(solution)/shard_map/all_to_all | solution.py:166
  48.7 6.5 %all-to-all-start.1 = ((bf16[8,64,768]{2,1,0:T(8,128)(2,1)}), bf16[8,64,768]{2,1,0:T(8,128)(2,1)S(1)}, u32[]{:S(2)}, u32[]{:S(2)}) async-start(bf16[8,64,768]{2,1,0:T(8,128)(2,1)} %broadcast_in_dim.12), calls=%async_computation.1 | async-start | bytes 1572864 | tf_op jit(solution)/shard_map/all_to_all | solution.py:174
  60.6 2.7 %collective-permute-start.9 = (bf16[64,768]{1,0:T(8,128)(2,1)}, bf16[64,768]{1,0:T(8,128)(2,1)}, u32[]{:S(2)}, u32[]{:S(2)}) collective-permute-start(bf16[64,768]{1,0:T(8,128)(2,1)} %slice.19), channel_id=1, source_target_pairs={{0,96},{16,112},{32,0},{48,16},{64,32},{80,48},{96,64},{112,80},{1... | collective-permute-start | bytes 294920 | tf_op jit(solution)/shard_map/ppermute | solution.py:27
  63.3 2.5 %collective-permute-start.8 = (bf16[64,768]{1,0:T(8,128)(2,1)}, bf16[64,768]{1,0:T(8,128)(2,1)}, u32[]{:S(2)}, u32[]{:S(2)}) collective-permute-start(bf16[64,768]{1,0:T(8,128)(2,1)} %slice.18), channel_id=1, source_target_pairs={{0,32},{16,48},{32,64},{48,80},{64,96},{80,112},{96,0},{112,16},{1... | collective-permute-start | bytes 294920 | tf_op jit(solution)/shard_map/ppermute | solution.py:27
  68.5 1.8 %collective-permute-done.8.refs_7_ = bf16[64,768]{1,0:T(8,128)(2,1)} collective-permute-done((bf16[64,768]{1,0:T(8,128)(2,1)}, bf16[64,768]{1,0:T(8,128)(2,1)}, u32[]{:S(2)}, u32[]{:S(2)}) %collective-permute-start.8) | collective-permute-done | bytes 98336 | tf_op jit(solution)/shard_map/ppermute | solution.py:27
  72.0 5.4 %shard_map.61 = (bf16[1024,768]{1,0:T(8,128)(2,1)S(1)}, bf16[768,768]{1,0:T(8,128)(2,1)S(1)}, f32[768,384]{1,0:T(8,128)S(1)}) custom-call(s32[25]{0:T(128)S(1)} %stack.103.place, bf16[128,768]{1,0:T(8,128)(2,1)S(1)} %pad_maximum_fusion.refs_0_, bf16[128,768]{1,0:T(8,128)(2,1)} %collective-permute-done.2.refs_1_, ...), custom_call_target="tpu_custom_call" | custom-call | flops 1660944384 | bytes 6291456 | tf_op jit(solution)/shard_map/pallas_call | solution.py:131
  77.5 3.1 %shard_map.62 = (f32[768,384]{1,0:T(8,128)S(1)}, f32[512,768]{1,0:T(8,128)}, f32[512,768]{1,0:T(8,128)S(1)}) custom-call(s32[25]{0:T(128)S(1)} %stack.103.place, bf16[1024,768]{1,0:T(8,128)(2,1)S(1)} %get-tuple-element.32.rows, bf16[768,768]{1,0:T(8,128)(2,1)S(1)} %get-tuple-element.33.amp), custom_call_target="tpu_custom_call" | custom-call | flops 1660944384 | bytes 6291456 | tf_op jit(solution)/shard_map/pallas_call | solution.py:131
  82.7 6.3 %all-to-all-start.2 = ((f16[16,56,384]{2,1,0:T(8,128)(2,1)}), f16[16,56,384]{2,1,0:T(8,128)(2,1)}, u32[]{:S(2)}, u32[]{:S(2)}) async-start(f16[16,56,384]{2,1,0:T(8,128)(2,1)} %convert_element_type.15), calls=%async_computation.2 | async-start | bytes 1376256 | tf_op jit(solution)/shard_map/all_to_all | solution.py:206
  90.5 3.4 %shard_map.63 = (f32[64,768]{1,0:T(8,128)S(1)}, f32[64,768]{1,0:T(8,128)}, f32[64,768]{1,0:T(8,128)S(1)}, f32[64,768]{1,0:T(8,128)S(1)}, f32[64,768]{1,0:T(8,128...) custom-call(s32[25]{0:T(128)S(1)} %stack.103.place, f32[512,768]{1,0:T(8,128)S(1)} %copy-done.2, ...), custom_call_target="tpu_custom_call" | custom-call | bytes 6291456 | tf_op jit(solution)/shard_map/pallas_call | solution.py:131
  93.9 3.5 %collective-permute-start.12 = (f32[64,768]{1,0:T(8,128)}, f32[64,768]{1,0:T(8,128)}, u32[]{:S(2)}, u32[]{:S(2)}) collective-permute-start(f32[64,768]{1,0:T(8,128)} %get-tuple-element.37), channel_id=1, source_target_pairs={{0,2},{2,0},{4,6},{6,4},{8,10},{10,8},{12,14},{14,12},{1,3},{3,1},... | collective-permute-start | bytes 589832 | tf_op jit(solution)/shard_map/ppermute | solution.py:32
  97.4 1.5 %collective-permute-start.13 = (f32[64,768]{1,0:T(8,128)S(1)}, f32[64,768]{1,0:T(8,128)}, u32[]{:S(2)}, u32[]{:S(2)}) collective-permute-start(f32[64,768]{1,0:T(8,128)S(1)} %get-tuple-element.38), channel_id=1, source_target_pairs={{0,4},{2,6},{4,8},{6,10},{8,12},{10,14},{12,0},{14,2},{1,5},{3,7},... | collective-permute-start | bytes 589832 | tf_op jit(solution)/shard_map/ppermute | solution.py:32
  101.7 4.6 %collective-permute-start.16 = (f32[64,768]{1,0:T(8,128)S(1)}, f32[64,768]{1,0:T(8,128)}, u32[]{:S(2)}, u32[]{:S(2)}) collective-permute-start(f32[64,768]{1,0:T(8,128)S(1)} %get-tuple-element.41), channel_id=1, source_target_pairs={{0,10},{2,8},{4,14},{6,12},{8,2},{10,0},{12,6},{14,4},{1,11},{3,9}... | collective-permute-start | bytes 589832 | tf_op jit(solution)/shard_map/ppermute | solution.py:32
  106.3 2.7 %all-to-all-done.2 = f16[16,56,384]{2,1,0:T(8,128)(2,1)} async-done(((f16[16,56,384]{2,1,0:T(8,128)(2,1)}), f16[16,56,384]{2,1,0:T(8,128)(2,1)}, u32[]{:S(2)}, u32[]{:S(2)}) %all-to-all-start.2) | async-done | bytes 688160 | tf_op jit(solution)/shard_map/all_to_all | solution.py:206
  110.2 3.2 %collective-permute-start.17 = (f32[64,768]{1,0:T(8,128)S(1)}, f32[64,768]{1,0:T(8,128)}, u32[]{:S(2)}, u32[]{:S(2)}) collective-permute-start(f32[64,768]{1,0:T(8,128)S(1)} %get-tuple-element.42), channel_id=1, source_target_pairs={{0,12},{2,14},{4,0},{6,2},{8,4},{10,6},{12,8},{14,10},{1,13},{3,15... | collective-permute-start | bytes 589832 | tf_op jit(solution)/shard_map/ppermute | solution.py:32
  113.4 3.3 %collective-permute-start.18 = (f32[64,768]{1,0:T(8,128)S(1)}, f32[64,768]{1,0:T(8,128)}, u32[]{:S(2)}, u32[]{:S(2)}) collective-permute-start(f32[64,768]{1,0:T(8,128)S(1)} %get-tuple-element.43), channel_id=1, source_target_pairs={{0,14},{2,12},{4,2},{6,0},{8,6},{10,4},{12,10},{14,8},{1,15},{3,13... | collective-permute-start | bytes 589832 | tf_op jit(solution)/shard_map/ppermute | solution.py:32
  117.5 3.5 %all-to-all-start.3 = ((f32[16,3,384]{2,1,0:T(4,128)}), f32[16,3,384]{2,1,0:T(4,128)S(1)}, u32[]{:S(2)}, u32[]{:S(2)}) async-start(f32[16,3,384]{2,1,0:T(4,128)} %reshape.47), calls=%async_computation.3 | async-start | bytes 196608 | tf_op jit(solution)/shard_map/all_to_all | solution.py:224
  121.0 5.3 %collective-permute-done.17 = f32[64,768]{1,0:T(8,128)} collective-permute-done((f32[64,768]{1,0:T(8,128)S(1)}, f32[64,768]{1,0:T(8,128)}, u32[]{:S(2)}, u32[]{:S(2)}) %collective-permute-start.17) | collective-permute-done | bytes 196640 | tf_op jit(solution)/shard_map/ppermute | solution.py:32
  126.3 1.5 %add_bitcast_fusion = f32[64,1,768]{2,0,1:T(8,128)S(1)} fusion(f32[64,768]{1,0:T(8,128)} %collective-permute-done.18, f32[64,768]{1,0:T(8,128)} %collective-permute-done.17, f32[64,768]{1,0:T(8,128)} %collective-permute-done.16, f32[64,768]{1,0:T(8,128)} %collective-permute-done.15, f32[64,768]{1,0:T(8,128)} %collective-permute-done.14, ...), kind=kLoop, calls=%fused_computation.4 | loop fusion | flops 344064 | bytes 1769472 | tf_op jit(solution)/shard_map/broadcast_in_dim | solution.py:219
  (72 shorter events, 26.4 us)
Async XLA Ops:
  4.4 6.8 %collective-permute-start.1 = (bf16[64,768]{1,0:T(8,128)(2,1)S(1)}, bf16[64,768]{1,0:T(8,128)(2,1)S(1)}, u32[]{:S(2)}, u32[]{:S(2)}) collective-permute-start(bf16[64,768]{1,0:T(8,128)(2,1)S(1)} %copy.13), channel_id=1, source_target_pairs={{0,128},{1,144},{2,160},{3,176},{4,192},{5,208},{6,224},{7,240},{8... | collective-permute-start | bytes 294920 | tf_op jit(solution)/shard_map/ppermute | solution.py:153
  4.9 6.9 %collective-permute-start = (bf16[64,768]{1,0:T(8,128)(2,1)S(1)}, bf16[64,768]{1,0:T(8,128)(2,1)S(1)}, u32[]{:S(2)}, u32[]{:S(2)}) collective-permute-start(bf16[64,768]{1,0:T(8,128)(2,1)S(1)} %copy.13), channel_id=1, source_target_pairs={{0,0},{1,16},{2,32},{3,48},{4,64},{5,80},{6,96},{7,112},{8,128},{9... | collective-permute-start | bytes 294920 | tf_op jit(solution)/shard_map/ppermute | solution.py:153
  11.9 35.7 %collective-permute-start.5 = (bf16[128,768]{1,0:T(8,128)(2,1)S(1)}, bf16[128,768]{1,0:T(8,128)(2,1)S(1)}, u32[]{:S(2)}, u32[]{:S(2)}) collective-permute-start(bf16[128,768]{1,0:T(8,128)(2,1)S(1)} %pad_maximum_fusion.refs_0_), channel_id=1, source_target_pairs={{0,96},{16,112},{32,0},{48,16},{64,32},{80,48},{96,64},{112,80},{1... | collective-permute-start | bytes 589832 | tf_op jit(solution)/shard_map/ppermute | solution.py:27
  30.7 16.8 %collective-permute-start.4 = (bf16[128,768]{1,0:T(8,128)(2,1)S(1)}, bf16[128,768]{1,0:T(8,128)(2,1)S(1)}, u32[]{:S(2)}, u32[]{:S(2)}) collective-permute-start(bf16[128,768]{1,0:T(8,128)(2,1)S(1)} %pad_maximum_fusion.refs_0_), channel_id=1, source_target_pairs={{0,32},{16,48},{32,64},{48,80},{64,96},{80,112},{96,0},{112,16},{1... | collective-permute-start | bytes 589832 | tf_op jit(solution)/shard_map/ppermute | solution.py:27
  31.6 15.8 %all-to-all-start = ((bf16[16,2,1536]{2,1,0:T(2,128)(2,1)}), bf16[16,2,1536]{2,1,0:T(2,128)(2,1)S(1)}, u32[]{:S(2)}, u32[]{:S(2)}) async-start(bf16[16,2,1536]{2,1,0:T(2,128)(2,1)} %reshape.50), calls=%async_computation | async-start | bytes 196608 | tf_op jit(solution)/shard_map/all_to_all | solution.py:166
  48.7 18.3 %all-to-all-start.1 = ((bf16[8,64,768]{2,1,0:T(8,128)(2,1)}), bf16[8,64,768]{2,1,0:T(8,128)(2,1)S(1)}, u32[]{:S(2)}, u32[]{:S(2)}) async-start(bf16[8,64,768]{2,1,0:T(8,128)(2,1)} %broadcast_in_dim.12), calls=%async_computation.1 | async-start | bytes 1572864 | tf_op jit(solution)/shard_map/all_to_all | solution.py:174
  55.1 8.2 %collective-permute-start.3 = (bf16[128,768]{1,0:T(8,128)(2,1)S(1)}, bf16[128,768]{1,0:T(8,128)(2,1)}, u32[]{:S(2)}, u32[]{:S(2)}) collective-permute-start(bf16[128,768]{1,0:T(8,128)(2,1)S(1)} %pad_maximum_fusion.refs_0_), channel_id=1, source_target_pairs={{0,112},{16,0},{32,16},{48,32},{64,48},{80,64},{96,80},{112,96},{1... | collective-permute-start | bytes 589832 | tf_op jit(solution)/shard_map/ppermute | solution.py:27
  56.0 9.8 %collective-permute-start.2 = (bf16[128,768]{1,0:T(8,128)(2,1)S(1)}, bf16[128,768]{1,0:T(8,128)(2,1)}, u32[]{:S(2)}, u32[]{:S(2)}) collective-permute-start(bf16[128,768]{1,0:T(8,128)(2,1)S(1)} %pad_maximum_fusion.refs_0_), channel_id=1, source_target_pairs={{0,16},{16,32},{32,48},{48,64},{64,80},{80,96},{96,112},{112,0},{1... | collective-permute-start | bytes 589832 | tf_op jit(solution)/shard_map/ppermute | solution.py:27
  57.9 12.4 %collective-permute-start.6 = (bf16[128,768]{1,0:T(8,128)(2,1)S(1)}, bf16[128,768]{1,0:T(8,128)(2,1)}, u32[]{:S(2)}, u32[]{:S(2)}) collective-permute-start(bf16[128,768]{1,0:T(8,128)(2,1)S(1)} %collective-permute-done.4.refs_3_), channel_id=1, source_target_pairs={{0,16},{16,32},{32,48},{48,64},{64,80},{80,96},{96,112},{112,0},{1... | collective-permute-start | bytes 589832 | tf_op jit(solution)/shard_map/ppermute | solution.py:27
  59.2 11.1 %collective-permute-start.7 = (bf16[128,768]{1,0:T(8,128)(2,1)S(1)}, bf16[128,768]{1,0:T(8,128)(2,1)}, u32[]{:S(2)}, u32[]{:S(2)}) collective-permute-start(bf16[128,768]{1,0:T(8,128)(2,1)S(1)} %collective-permute-done.5.refs_4_), channel_id=1, source_target_pairs={{0,112},{16,0},{32,16},{48,32},{64,48},{80,64},{96,80},{112,96},{1... | collective-permute-start | bytes 589832 | tf_op jit(solution)/shard_map/ppermute | solution.py:27
  60.6 7.9 %collective-permute-start.9 = (bf16[64,768]{1,0:T(8,128)(2,1)}, bf16[64,768]{1,0:T(8,128)(2,1)}, u32[]{:S(2)}, u32[]{:S(2)}) collective-permute-start(bf16[64,768]{1,0:T(8,128)(2,1)} %slice.19), channel_id=1, source_target_pairs={{0,96},{16,112},{32,0},{48,16},{64,32},{80,48},{96,64},{112,80},{1... | collective-permute-start | bytes 294920 | tf_op jit(solution)/shard_map/ppermute | solution.py:27
  63.3 7.1 %collective-permute-start.8 = (bf16[64,768]{1,0:T(8,128)(2,1)}, bf16[64,768]{1,0:T(8,128)(2,1)}, u32[]{:S(2)}, u32[]{:S(2)}) collective-permute-start(bf16[64,768]{1,0:T(8,128)(2,1)} %slice.18), channel_id=1, source_target_pairs={{0,32},{16,48},{32,64},{48,80},{64,96},{80,112},{96,0},{112,16},{1... | collective-permute-start | bytes 294920 | tf_op jit(solution)/shard_map/ppermute | solution.py:27
  66.9 3.4 %collective-permute-start.10 = (bf16[512,768]{1,0:T(8,128)(2,1)S(1)}, bf16[512,768]{1,0:T(8,128)(2,1)}, u32[]{:S(2)}, u32[]{:S(2)}) collective-permute-start(bf16[512,768]{1,0:T(8,128)(2,1)S(1)} %bitcast.49), channel_id=1, source_target_pairs={{0,1},{1,0},{2,3},{3,2},{4,5},{5,4},{6,7},{7,6},{8,9},{9,8},{10,11... | collective-permute-start | bytes 2359304 | tf_op jit(solution)/shard_map/ppermute | solution.py:23
  77.4 3.7 %collective-permute-start.19 = (f32[768,384]{1,0:T(8,128)S(1)}, f32[768,384]{1,0:T(8,128)S(1)}, u32[]{:S(2)}, u32[]{:S(2)}) collective-permute-start(f32[768,384]{1,0:T(8,128)S(1)} %get-tuple-element.45), channel_id=1, source_target_pairs={{0,1},{1,0},{2,3},{3,2},{4,5},{5,4},{6,7},{7,6},{8,9},{9,8},{10,11... | collective-permute-start | bytes 3538952 | tf_op jit(solution)/shard_map/ppermute | solution.py:23
  80.7 8.4 %collective-permute-start.11 = (f32[512,768]{1,0:T(8,128)}, f32[512,768]{1,0:T(8,128)}, u32[]{:S(2)}, u32[]{:S(2)}) collective-permute-start(f32[512,768]{1,0:T(8,128)} %get-tuple-element.35), channel_id=1, source_target_pairs={{0,1},{1,0},{2,3},{3,2},{4,5},{5,4},{6,7},{7,6},{8,9},{9,8},{10,11... | collective-permute-start | bytes 4718600 | tf_op jit(solution)/shard_map/ppermute | solution.py:23
  82.7 26.3 %all-to-all-start.2 = ((f16[16,56,384]{2,1,0:T(8,128)(2,1)}), f16[16,56,384]{2,1,0:T(8,128)(2,1)}, u32[]{:S(2)}, u32[]{:S(2)}) async-start(f16[16,56,384]{2,1,0:T(8,128)(2,1)} %convert_element_type.15), calls=%async_computation.2 | async-start | bytes 1376256 | tf_op jit(solution)/shard_map/all_to_all | solution.py:206
  93.9 16.3 %collective-permute-start.12 = (f32[64,768]{1,0:T(8,128)}, f32[64,768]{1,0:T(8,128)}, u32[]{:S(2)}, u32[]{:S(2)}) collective-permute-start(f32[64,768]{1,0:T(8,128)} %get-tuple-element.37), channel_id=1, source_target_pairs={{0,2},{2,0},{4,6},{6,4},{8,10},{10,8},{12,14},{14,12},{1,3},{3,1},... | collective-permute-start | bytes 589832 | tf_op jit(solution)/shard_map/ppermute | solution.py:32
  97.4 16.0 %collective-permute-start.13 = (f32[64,768]{1,0:T(8,128)S(1)}, f32[64,768]{1,0:T(8,128)}, u32[]{:S(2)}, u32[]{:S(2)}) collective-permute-start(f32[64,768]{1,0:T(8,128)S(1)} %get-tuple-element.38), channel_id=1, source_target_pairs={{0,4},{2,6},{4,8},{6,10},{8,12},{10,14},{12,0},{14,2},{1,5},{3,7},... | collective-permute-start | bytes 589832 | tf_op jit(solution)/shard_map/ppermute | solution.py:32
  98.9 22.1 %collective-permute-start.14 = (f32[64,768]{1,0:T(8,128)S(1)}, f32[64,768]{1,0:T(8,128)}, u32[]{:S(2)}, u32[]{:S(2)}) collective-permute-start(f32[64,768]{1,0:T(8,128)S(1)} %get-tuple-element.39), channel_id=1, source_target_pairs={{0,6},{2,4},{4,10},{6,8},{8,14},{10,12},{12,2},{14,0},{1,7},{3,5},... | collective-permute-start | bytes 589832 | tf_op jit(solution)/shard_map/ppermute | solution.py:32
  100.4 20.6 %collective-permute-start.15 = (f32[64,768]{1,0:T(8,128)S(1)}, f32[64,768]{1,0:T(8,128)}, u32[]{:S(2)}, u32[]{:S(2)}) collective-permute-start(f32[64,768]{1,0:T(8,128)S(1)} %get-tuple-element.40), channel_id=1, source_target_pairs={{0,8},{2,10},{4,12},{6,14},{8,0},{10,2},{12,4},{14,6},{1,9},{3,11}... | collective-permute-start | bytes 589832 | tf_op jit(solution)/shard_map/ppermute | solution.py:32
  101.7 19.3 %collective-permute-start.16 = (f32[64,768]{1,0:T(8,128)S(1)}, f32[64,768]{1,0:T(8,128)}, u32[]{:S(2)}, u32[]{:S(2)}) collective-permute-start(f32[64,768]{1,0:T(8,128)S(1)} %get-tuple-element.41), channel_id=1, source_target_pairs={{0,10},{2,8},{4,14},{6,12},{8,2},{10,0},{12,6},{14,4},{1,11},{3,9}... | collective-permute-start | bytes 589832 | tf_op jit(solution)/shard_map/ppermute | solution.py:32
  110.2 16.1 %collective-permute-start.17 = (f32[64,768]{1,0:T(8,128)S(1)}, f32[64,768]{1,0:T(8,128)}, u32[]{:S(2)}, u32[]{:S(2)}) collective-permute-start(f32[64,768]{1,0:T(8,128)S(1)} %get-tuple-element.42), channel_id=1, source_target_pairs={{0,12},{2,14},{4,0},{6,2},{8,4},{10,6},{12,8},{14,10},{1,13},{3,15... | collective-permute-start | bytes 589832 | tf_op jit(solution)/shard_map/ppermute | solution.py:32
  113.4 12.9 %collective-permute-start.18 = (f32[64,768]{1,0:T(8,128)S(1)}, f32[64,768]{1,0:T(8,128)}, u32[]{:S(2)}, u32[]{:S(2)}) collective-permute-start(f32[64,768]{1,0:T(8,128)S(1)} %get-tuple-element.43), channel_id=1, source_target_pairs={{0,14},{2,12},{4,2},{6,0},{8,6},{10,4},{12,10},{14,8},{1,15},{3,13... | collective-permute-start | bytes 589832 | tf_op jit(solution)/shard_map/ppermute | solution.py:32
  117.5 11.3 %all-to-all-start.3 = ((f32[16,3,384]{2,1,0:T(4,128)}), f32[16,3,384]{2,1,0:T(4,128)S(1)}, u32[]{:S(2)}, u32[]{:S(2)}) async-start(f32[16,3,384]{2,1,0:T(4,128)} %reshape.47), calls=%async_computation.3 | async-start | bytes 196608 | tf_op jit(solution)/shard_map/all_to_all | solution.py:224
  (7 other events, 22.3 us)

commit v4 on v3

--- a/solution.py
+++ b/solution.py
@@ -45,6 +45,7 @@
         out_shape=jax.ShapeDtypeStruct(array.shape, array.dtype),
         in_specs=[VMEM],
         out_specs=VMEM,
+        compiler_params=pltpu.CompilerParams(vmem_limit_bytes=2**20),
         cost_estimate=pl.CostEstimate(flops=us * 10**9, bytes_accessed=2**20, transcendentals=0),
     )(array)
 
@@ -55,7 +56,7 @@
 
 def amplitudes(n_rows, place, *refs):
     row_refs, (own_cols, other_cols, row_energy, col_energy) = refs[:n_rows], refs[n_rows : n_rows + 4]
-    rows, amp, vir, cols, sems = refs[n_rows + 4 :]
+    rows, amp, vir, cols, row_side, col_side, sems = refs[n_rows + 4 :]
     core = place[24]
     moves = []
     for ref in row_refs:
@@ -64,6 +65,7 @@
             moves.append((ref.at[pl.ds(part * PW, PW)], rows.at[pl.ds(start, PW)]))
     for ref, side in ((own_cols, core), (other_cols, 1 - core)):
         moves.append((ref, cols.at[pl.ds(pl.multiple_of(side * HALF_P, HALF_P), HALF_P)]))
+    moves += [(row_energy, row_side), (col_energy, col_side)]
     copies = [pltpu.make_async_copy(f, t, sems.at[k]) for k, (f, t) in enumerate(moves)]
     for copy in copies:
         copy.start()
@@ -74,7 +76,7 @@
         coulomb = lax.dot_general(
             rows[:, here], cols[...], TRANSPOSED, preferred_element_type=jnp.float32
         )
-        amp[here, :] = (coulomb / (row_energy[here, :] - col_energy[...])).astype(jnp.bfloat16)
+        amp[here, :] = (coulomb / (row_side[here, :] - col_side[...])).astype(jnp.bfloat16)
     virtual_block(amp, 1 - core, vir)
 
 
@@ -87,54 +89,64 @@
         )
 
 
-def give_and_keep(place, rows, amp, vir, give, keep):
+def give_and_keep(place, rows, amp, give, keep):
     core = place[24]
     for out, side in ((give, 1 - core), (keep, core)):
         start = pl.multiple_of(side * HALF_P, HALF_P)
         out[...] = jnp.dot(rows[pl.ds(start, HALF_P), :], amp[...], preferred_element_type=jnp.float32)
-    virtual_block(amp, core, vir)
-
-
-def pack_virtual(keep, got, out):
-    total = keep[...] + got[...]
+
+
+def pack_virtual(place, amp, got, out, total):
+    virtual_block(amp, place[24], total)
+    total[...] += got[...]
+    scale, power = scale_of(total[...])
+    tail = jnp.broadcast_to(power, (8, HALF_V))
+    for g in range(NO):
+        out[g, :VW, :] = total[VW * g : VW * g + VW, :] * scale
+        out[g, VW:, :] = tail
+
+
+def add_three(place, keep, got, own, out, kept, met, sems):
+    copies = [pltpu.make_async_copy(keep, kept, sems.at[0]), pltpu.make_async_copy(got, met, sems.at[1])]
+    for copy in copies:
+        copy.start()
+    for copy in copies:
+        copy.wait()
+    kept[...] += met[...]
+    scale, power = scale_of(kept[...])
+    own[...] = kept[pl.ds(pl.multiple_of(place[16], PW), PW), :]
+    for hop in range(1, Y * XH):
+        out[hop - 1, :PW, :] = kept[pl.ds(pl.multiple_of(place[16 + hop], PW), PW), :] * scale
+        out[hop - 1, PW:, :] = jnp.broadcast_to(power, (8, NV))
+
+
+def scale_of(total):
     top = jnp.maximum(jnp.max(jnp.abs(total), keepdims=True), 2.0**-100)
     power = jnp.ceil(jnp.log2(top))
-    total = total * jnp.exp2(SCALE - power)
-    tail = jnp.broadcast_to(power, (8, HALF_V))
-    for g in range(NO):
-        out[g, :VW, :] = total[VW * g : VW * g + VW, :]
-        out[g, VW:, :] = tail
-
-
-def add_three(place, keep, got, *outs):
-    *outs, total, sems = outs
-    total[...] = keep[...] + got[...]
-    copies = [
-        pltpu.make_async_copy(total.at[pl.ds(pl.multiple_of(place[16 + hop], PW), PW)], out, sems.at[hop])
-        for hop, out in enumerate(outs)
-    ]
-    for copy in copies:
-        copy.start()
-    for copy in copies:
-        copy.wait()
+    return jnp.exp2(SCALE - power), power
+
+
+def weight_of(sent, rows):
+    power = lax.optimization_barrier(sent[..., rows : rows + 1, :])
+    return jnp.exp2(power.astype(jnp.float32) - SCALE)
 
 
 SCALE = 14.0
 PACE = 25
 
 
-def call(kernel, shapes, args, scratch=(), flops=0, anywhere=0, n_sems=0, out_space=pltpu.VMEM):
+def call(kernel, shapes, args, scratch=(), flops=0, anywhere=0, n_sems=0, space=pl.ANY):
     spaces = [SMEM if a.dtype == jnp.int32 else VMEM for a in args]
     first = 1 if args[0].dtype == jnp.int32 else 0
-    spaces[first : first + anywhere] = [pl.BlockSpec(memory_space=pl.ANY)] * anywhere
+    spaces[first : first + anywhere] = [pl.BlockSpec(memory_space=space)] * anywhere
     sems = [pltpu.SemaphoreType.DMA((n_sems,))] if n_sems else []
     return pl.pallas_call(
         kernel,
         out_shape=[jax.ShapeDtypeStruct(s, t) for s, t in shapes],
         in_specs=spaces,
-        out_specs=[pl.BlockSpec(memory_space=out_space)] * len(shapes),
+        out_specs=[VMEM] * len(shapes),
         scratch_shapes=[pltpu.VMEM(s, t) for s, t in scratch] + sems,
-        compiler_params=pltpu.CompilerParams(vmem_limit_bytes=32 * 2**20),
+        compiler_params=pltpu.CompilerParams(vmem_limit_bytes=16 * 2**20),
         cost_estimate=pl.CostEstimate(flops=flops, bytes_accessed=6 * 2**20, transcendentals=0),
     )(*args)
 
@@ -160,20 +172,20 @@
     row_energy = ((own_energy + occ_energy)[:, None] - slice_energy[None, :]).reshape(NV, 1)
     col_energy = vir_energy[None, :]
 
-    pair, native, row_energy = lax.optimization_barrier((pair, native, row_energy))
+    local = lax.all_to_all(native, OCC, split_axis=0, concat_axis=0, tiled=True)
+    row_energy = paced(row_energy, PACE)
+    pair, local, row_energy = lax.optimization_barrier((pair, local, row_energy))
+    local = jnp.transpose(local, (1, 0, 2)).reshape(PW, NV)
     up1, down1, up2, down2 = (ring(pair, by) for by in (1, -1, 2, -2))
-    row_energy = paced(row_energy, PACE)
-    local = lax.all_to_all(native, OCC, split_axis=0, concat_axis=0, tiled=True)
-    local = jnp.transpose(local, (1, 0, 2)).reshape(PW, NV)
-    local, up2, down2, col_energy, row_energy = lax.optimization_barrier(
-        (local, up2, down2, col_energy, row_energy)
-    )
-    up3, down3 = ring(up2, 1), ring(down2, -1)
-    up4, down4 = ring(up2[:PW], 2), ring(down2[PW:], -2)
-    col_energy = paced(col_energy, PACE)
     own_cols = lax.all_to_all(
         jnp.broadcast_to(local, (Y * XH, PW, NV)), CHIPS, split_axis=0, concat_axis=0, tiled=True
     ).reshape(HALF_P, NV)
+    row_energy, col_energy, local = lax.optimization_barrier((row_energy, col_energy, local))
+    col_energy = paced(col_energy, PACE)
+    up2, down2, col_energy = lax.optimization_barrier((up2, down2, col_energy))
+    col_energy = paced(col_energy, PACE)
+    up3, down3 = ring(up2, 1), ring(down2, -1)
+    up4, down4 = ring(up2[:PW], 2), ring(down2[PW:], -2)
     other_cols = swap(own_cols, "c")
     row_arrays = [pair, up1, down1, up2, down2, up3, down3, up4, down4]
     owners = []
@@ -189,37 +201,48 @@
         functools.partial(amplitudes, len(row_arrays)),
         [((NP, NV), bf16), ((NV, NV), bf16), ((NV, HALF_V), f32)],
         [place, *row_arrays, own_cols, other_cols, row_energy, col_energy],
-        [((NP, NV), bf16)],
+        [((NP, NV), bf16), ((NV, 1), f32), ((1, NV), f32)],
         dot * (NP + HALF_V),
-        len(row_arrays) + 2,
-        NO + 2,
+        len(row_arrays) + 4,
+        NO + 4,
+        pltpu.HBM,
     )
     vir_got = swap(vir_give, "c")
-    vir_keep, three_give, three_keep = call(
+    three_give, three_keep = call(
         give_and_keep,
-        [((NV, HALF_V), f32), ((HALF_P, NV), f32), ((HALF_P, NV), f32)],
+        [((HALF_P, NV), f32)] * 2,
         [place, rows, amp],
-        flops=dot * (HALF_V + NP),
-    )
+        flops=dot * NP,
+    )
+    vir_got, three_give = lax.optimization_barrier((vir_got, three_give))
     three_got = swap(three_give, "c")
-    (packed,) = call(pack_virtual, [((NO, VW + 8, HALF_V), f32)], [vir_keep, vir_got])
-    met = lax.all_to_all(packed.astype(jnp.float16), OCC, split_axis=0, concat_axis=0, tiled=True)
-
-    pieces = call(
+    (packed,) = call(
+        pack_virtual,
+        [((NO, VW + 8, HALF_V), f32)],
+        [place, amp, vir_got],
+        [((NV, HALF_V), f32)],
+        dot * HALF_V,
+    )
+    packed, three_keep = lax.optimization_barrier((packed.astype(jnp.float16), three_keep))
+    met = lax.all_to_all(packed, OCC, split_axis=0, concat_axis=0, tiled=True)
+    own_piece, pieces = call(
         add_three,
-        [((PW, NV), f32)] * (Y * XH),
+        [((PW, NV), f32), ((Y * XH - 1, PW + 8, NV), f32)],
         [place, three_keep, three_got],
-        [((HALF_P, NV), f32)],
-        n_sems=Y * XH,
-        out_space=pltpu.HBM,
-    )
-    three = pieces[0]
-    for hop in range(1, Y * XH):
-        three = three + next_chip(pieces[hop], hop)
+        [((HALF_P, NV), f32)] * 2,
+        anywhere=2,
+        n_sems=2,
+    )
+    got = [next_chip(piece.astype(jnp.float16), hop) for hop, piece in enumerate(pieces, 1)]
+    met, *got = lax.optimization_barrier((met, *got))
+    vir = jnp.sum(met[:, :VW].astype(f32) * weight_of(met, VW), 0)
+    vir, *got = lax.optimization_barrier((vir, *got))
+    weights = weight_of(jnp.concatenate([piece[PW:] for piece in got], 1), 0)
+    three = own_piece
+    for k, piece in enumerate(got):
+        three = three + piece[:PW].astype(f32) * weights[:, k * NV : (k + 1) * NV]
     three_index = three[:, None, :]
 
-    met = met.astype(f32)
-    vir = jnp.sum(met[:, :VW, :] * jnp.exp2(met[:, VW : VW + 1, :] - SCALE), 0)
     vir = vir.reshape(NO, VW // NO, HALF_V)
     vir = lax.all_to_all(vir, AUX, split_axis=0, concat_axis=0, tiled=True)
     vir = jnp.sum(vir.reshape(Y * XH, C, VW // NO, HALF_V), 0)

time: 131 us -> 119 us (0.908)
  starting transfers between devices: 76.4 us -> 62.7 us
  Pallas kernels: 15.3 us -> 12.1 us
  local copies, waits for them, and re-layouts: 12.4 us -> 15 us
  waiting for transfers between devices: 17.3 us -> 19.2 us
    ppermute x8, starting transfers between devices: 28.1 us -> 9.98 us  [ring(): return lax.ppermute(array, 'z', [(i, (i + by) % Z) for i in range(Z)])]
    all_to_all x1, starting transfers between devices: 8 us -> 14.9 us  [per_device(): local = lax.all_to_all(native, OCC, split_axis=0, concat_axis=0, tiled=True)]
    ppermute x8, waiting for transfers between devices: 2.14 us -> 5.36 us  [ring(): return lax.ppermute(array, 'z', [(i, (i + by) % Z) for i in range(Z)])]
    unnamed x18 -> x24, local copies, waits for them, and re-layouts: 6.82 us -> 9.87 us
    pallas_call x2 -> x3, Pallas kernels: 3.06 us -> 0.03 us  [paced(): pl.pallas_call(kernel, out_shape=jax.ShapeDtypeStruct(array.shape, array....]
    all_to_all x1, waiting for transfers between devices: 2.7 us -> 0.01 us  [per_device(): met = lax.all_to_all(packed, OCC, split_axis=0, concat_axis=0, tiled=True)]
    all_to_all x1, waiting for transfers between devices: 1.19 us -> 3.75 us  [per_device(): lax.all_to_all(jnp.broadcast_to(local, (Y * XH, PW, NV)), CHIPS, split_ax...]
    ppermute x7, starting transfers between devices: 18.8 us -> 16.5 us  [next_chip(): return lax.ppermute(array, CHIPS, pairs)]
  transfers between devices with their start and end apart: 24 -> 24, of which waited for: 8 -> 10; matrix products, arithmetic and copies ran while one was open for 8% -> 12% of each run, Pallas kernels for 8% -> 6%
where the time goes in v4:
time: 119 us; the launch traced here: 116 us
  starting transfers between devices  62.7 us (53%)
  waiting for transfers between devices  19.2 us (16%)
  local copies, waits for them, and re-layouts  15 us (13%)
  Pallas kernels  12.1 us (10%)
  other arithmetic  4.01 us (3%)
  matrix products  2 us (2%)
  between operations  1.36 us (1%)
    ppermute x7, starting transfers between devices, next_chip(): return lax.ppermute(array, CHIPS, pairs)  16.5 us
    all_to_all x1, starting transfers between devices, per_device(): local = lax.all_to_all(native, OCC, split_axis=0, concat_axis=0, tiled=True)  14.9 us
    pallas_call x4, Pallas kernels, call(): pl.pallas_call(kernel, out_shape=[jax.ShapeDtypeStruct(s, t) for s, t in...  12 us
    ppermute x8, starting transfers between devices, ring(): return lax.ppermute(array, 'z', [(i, (i + by) % Z) for i in range(Z)])  9.98 us
    unnamed x24, local copies, waits for them, and re-layouts  9.87 us
    all_to_all x1, starting transfers between devices, per_device(): vir = lax.all_to_all(vir, AUX, split_axis=0, concat_axis=0, tiled=True)  5.74 us
    all_to_all x1, starting transfers between devices, per_device(): lax.all_to_all(jnp.broadcast_to(local, (Y * XH, PW, NV)), CHIPS, split_ax...  5.6 us
    ppermute x8, waiting for transfers between devices, ring(): return lax.ppermute(array, 'z', [(i, (i + by) % Z) for i in range(Z)])  5.36 us
  transfers between devices with their start and end apart: 24, of which 10 were waited for; matrix products, arithmetic and copies ran while one was open for 12% of the time, Pallas kernels for 6%

profile of v4, /device:TPU:32, one launch (start us, length us, event | category | flops | bytes accessed | tf_op | source)
XLA Modules:
  0.0 116.3 jit_solution(3448234915523398034)
XLA Ops:
  0.7 1.6 %copy-done = bf16[16,64,1024]{2,1,0:T(8,128)(2,1)S(1)} copy-done((bf16[16,64,1024]{2,1,0:T(8,128)(2,1)S(1)}, bf16[16,64,1024]{2,1,0:T(8,128)(2,1)}, u32[]{:S(2)}) %copy-start) | copy-done | bytes 2097176
  2.2 2.0 %convolution_convert_fusion = bf16[16,64,48]{1,2,0:T(8,128)(2,1)S(1)} fusion(bf16[16,64,1024]{2,1,0:T(8,128)(2,1)S(1)} %copy-done, bf16[1024,48]{0,1:T(8,128)(2,1)} %param.5), kind=kOutput, calls=%fused_computation.1 | convolution fusion | flops 100712448 | bytes 2293760 | tf_op jit(solution)/shard_map/ipm,ma->ipa/dot_general | solution.py:158
  4.9 4.1 %collective-permute-start = (bf16[64,768]{1,0:T(8,128)(2,1)S(1)}, bf16[64,768]{1,0:T(8,128)(2,1)S(1)}, u32[]{:S(2)}, u32[]{:S(2)}) collective-permute-start(bf16[64,768]{1,0:T(8,128)(2,1)S(1)} %copy.17), channel_id=1, source_target_pairs={{0,0},{1,16},{2,32},{3,48},{4,64},{5,80},{6,96},{7,112},{8,128},{9... | collective-permute-start | bytes 294920 | tf_op jit(solution)/shard_map/ppermute | solution.py:165
  9.8 14.9 %all-to-all-start = ((bf16[16,2,1536]{2,1,0:T(2,128)(2,1)}), bf16[16,2,1536]{2,1,0:T(2,128)(2,1)S(1)}, u32[]{:S(2)}, u32[]{:S(2)}) async-start(bf16[16,2,1536]{2,1,0:T(2,128)(2,1)} %reshape.64), calls=%async_computation | async-start | bytes 196608 | tf_op jit(solution)/shard_map/all_to_all | solution.py:175
  27.7 4.9 %all-to-all-done = bf16[16,2,1536]{2,1,0:T(2,128)(2,1)S(1)} async-done(((bf16[16,2,1536]{2,1,0:T(2,128)(2,1)}), bf16[16,2,1536]{2,1,0:T(2,128)(2,1)S(1)}, u32[]{:S(2)}, u32[]{:S(2)}) %all-to-all-start) | async-done | bytes 98336 | tf_op jit(solution)/shard_map/all_to_all | solution.py:175
  32.7 1.7 %collective-permute-start.5 = (bf16[128,768]{1,0:T(8,128)(2,1)S(1)}, bf16[128,768]{1,0:T(8,128)(2,1)S(1)}, u32[]{:S(2)}, u32[]{:S(2)}) collective-permute-start(bf16[128,768]{1,0:T(8,128)(2,1)S(1)} %pad_maximum_fusion.refs_0_), channel_id=1, source_target_pairs={{0,96},{16,112},{32,0},{48,16},{64,32},{80,48},{96,64},{112,80},{1... | collective-permute-start | bytes 589832 | tf_op jit(solution)/shard_map/ppermute | solution.py:27
  38.8 5.6 %all-to-all-start.1 = ((bf16[8,64,768]{2,1,0:T(8,128)(2,1)}), bf16[8,64,768]{2,1,0:T(8,128)(2,1)S(1)}, u32[]{:S(2)}, u32[]{:S(2)}) async-start(bf16[8,64,768]{2,1,0:T(8,128)(2,1)} %broadcast_in_dim.12), calls=%async_computation.1 | async-start | bytes 1572864 | tf_op jit(solution)/shard_map/all_to_all | solution.py:180
  44.4 2.0 %collective-permute-done.4.refs_3_ = bf16[128,768]{1,0:T(8,128)(2,1)S(1)} collective-permute-done((bf16[128,768]{1,0:T(8,128)(2,1)S(1)}, bf16[128,768]{1,0:T(8,128)(2,1)S(1)}, u32[]{:S(2)}, u32[]{:S(2)}) %collective-permute-start.4) | collective-permute-done | bytes 196640 | tf_op jit(solution)/shard_map/ppermute | solution.py:27
  47.8 2.0 %collective-permute-start.7 = (bf16[128,768]{1,0:T(8,128)(2,1)S(1)}, bf16[128,768]{1,0:T(8,128)(2,1)}, u32[]{:S(2)}, u32[]{:S(2)}) collective-permute-start(bf16[128,768]{1,0:T(8,128)(2,1)S(1)} %collective-permute-done.5.refs_4_), channel_id=1, source_target_pairs={{0,112},{16,0},{32,16},{48,32},{64,48},{80,64},{96,80},{112,96},{1... | collective-permute-start | bytes 589832 | tf_op jit(solution)/shard_map/ppermute | solution.py:27
  49.8 2.0 %collective-permute-start.9 = (bf16[64,768]{1,0:T(8,128)(2,1)}, bf16[64,768]{1,0:T(8,128)(2,1)}, u32[]{:S(2)}, u32[]{:S(2)}) collective-permute-start(bf16[64,768]{1,0:T(8,128)(2,1)} %slice.85), channel_id=1, source_target_pairs={{0,96},{16,112},{32,0},{48,16},{64,32},{80,48},{96,64},{112,80},{1... | collective-permute-start | bytes 294920 | tf_op jit(solution)/shard_map/ppermute | solution.py:27
  52.7 3.8 %all-to-all-done.1 = bf16[8,64,768]{2,1,0:T(8,128)(2,1)S(1)} async-done(((bf16[8,64,768]{2,1,0:T(8,128)(2,1)}), bf16[8,64,768]{2,1,0:T(8,128)(2,1)S(1)}, u32[]{:S(2)}, u32[]{:S(2)}) %all-to-all-start.1) | async-done | bytes 786464 | tf_op jit(solution)/shard_map/all_to_all | solution.py:180
  56.5 3.3 %collective-permute-done.8.refs_7_ = bf16[64,768]{1,0:T(8,128)(2,1)} collective-permute-done((bf16[64,768]{1,0:T(8,128)(2,1)}, bf16[64,768]{1,0:T(8,128)(2,1)}, u32[]{:S(2)}, u32[]{:S(2)}) %collective-permute-start.8) | collective-permute-done | bytes 98336 | tf_op jit(solution)/shard_map/ppermute | solution.py:27
  59.8 5.2 %shard_map.62 = (bf16[1024,768]{1,0:T(8,128)(2,1)S(1)}, bf16[768,768]{1,0:T(8,128)(2,1)S(1)}, f32[768,384]{1,0:T(8,128)S(1)}) custom-call(s32[25]{0:T(128)S(1)} %stack.103.place, bf16[128,768]{1,0:T(8,128)(2,1)S(1)} %pad_maximum_fusion.refs_0_, bf16[128,768]{1,0:T(8,128)(2,1)} %collective-permute-done.2.refs_1_, ...), custom_call_target="tpu_custom_call" | custom-call | flops 1660944384 | bytes 6291456 | tf_op jit(solution)/shard_map/pallas_call | solution.py:143
  65.1 2.7 %shard_map.63 = (f32[512,768]{1,0:T(8,128)}, f32[512,768]{1,0:T(8,128)S(1)}) custom-call(s32[25]{0:T(128)S(1)} %stack.103.place, bf16[1024,768]{1,0:T(8,128)(2,1)S(1)} %get-tuple-element.47.rows, bf16[768,768]{1,0:T(8,128)(2,1)S(1)} %get-tuple-element.45.amp), custom_call_target="tpu_custom_call" | custom-call | flops 1207959552 | bytes 6291456 | tf_op jit(solution)/shard_map/pallas_call | solution.py:143
  68.3 1.6 %shard_map.64 = f32[16,56,384]{2,1,0:T(8,128)S(1)} custom-call(s32[25]{0:T(128)S(1)} %stack.103.place, bf16[768,768]{1,0:T(8,128)(2,1)S(1)} %get-tuple-element.45.amp, f32[768,384]{1,0:T(8,128)S(1)} %collective-permute-done.11.got), custom_call_target="tpu_custom_call" | custom-call | flops 452984832 | bytes 6291456 | tf_op jit(solution)/shard_map/pallas_call | solution.py:143
  70.9 4.9 %all-to-all-start.2 = ((f16[16,56,384]{2,1,0:T(8,128)(2,1)}), f16[16,56,384]{2,1,0:T(8,128)(2,1)S(1)}, u32[]{:S(2)}, u32[]{:S(2)}) async-start(f16[16,56,384]{2,1,0:T(8,128)(2,1)} %convert_element_type.70), calls=%async_computation.2 | async-start | bytes 1376256 | tf_op jit(solution)/shard_map/all_to_all | solution.py:227
  77.2 2.6 %shard_map.65 = (f32[64,768]{1,0:T(8,128)S(1)}, f32[7,72,768]{2,1,0:T(8,128)S(1)}) custom-call(s32[25]{0:T(128)S(1)} %stack.103.place, f32[512,768]{1,0:T(8,128)S(1)} %copy-done.2, f32[512,768]{1,0:T(8,128)} %collective-permute-done.12.got), custom_call_target="tpu_custom_call" | custom-call | bytes 6291456 | tf_op jit(solution)/shard_map/pallas_call | solution.py:143
  80.0 5.6 %collective-permute-start.19 = (f16[72,768]{1,0:T(8,128)(2,1)S(1)}, f16[72,768]{1,0:T(8,128)(2,1)}, u32[]{:S(2)}, u32[]{:S(2)}) collective-permute-start(f16[72,768]{1,0:T(8,128)(2,1)S(1)} %get-tuple-element.85), channel_id=1, source_target_pairs={{0,14},{2,12},{4,2},{6,0},{8,6},{10,4},{12,10},{14,8},{1,15},{3,13... | collective-permute-start | bytes 331784 | tf_op jit(solution)/shard_map/ppermute | solution.py:32
  87.7 2.3 %collective-permute-start.16 = (f16[72,768]{1,0:T(8,128)(2,1)S(1)}, f16[72,768]{1,0:T(8,128)(2,1)}, u32[]{:S(2)}, u32[]{:S(2)}) collective-permute-start(f16[72,768]{1,0:T(8,128)(2,1)S(1)} %get-tuple-element.88), channel_id=1, source_target_pairs={{0,8},{2,10},{4,12},{6,14},{8,0},{10,2},{12,4},{14,6},{1,9},{3,11}... | collective-permute-start | bytes 331784 | tf_op jit(solution)/shard_map/ppermute | solution.py:32
  90.0 3.6 %collective-permute-start.15 = (f16[72,768]{1,0:T(8,128)(2,1)S(1)}, f16[72,768]{1,0:T(8,128)(2,1)}, u32[]{:S(2)}, u32[]{:S(2)}) collective-permute-start(f16[72,768]{1,0:T(8,128)(2,1)S(1)} %get-tuple-element.89), channel_id=1, source_target_pairs={{0,6},{2,4},{4,10},{6,8},{8,14},{10,12},{12,2},{14,0},{1,7},{3,5},... | collective-permute-start | bytes 331784 | tf_op jit(solution)/shard_map/ppermute | solution.py:32
  93.7 2.9 %collective-permute-start.13 = (f16[72,768]{1,0:T(8,128)(2,1)S(1)}, f16[72,768]{1,0:T(8,128)(2,1)}, u32[]{:S(2)}, u32[]{:S(2)}) collective-permute-start(f16[72,768]{1,0:T(8,128)(2,1)S(1)} %get-tuple-element.91), channel_id=1, source_target_pairs={{0,2},{2,0},{4,6},{6,4},{8,10},{10,8},{12,14},{14,12},{1,3},{3,1},... | collective-permute-start | bytes 331784 | tf_op jit(solution)/shard_map/ppermute | solution.py:32
  96.6 1.6 %collective-permute-done.17 = f16[72,768]{1,0:T(8,128)(2,1)} collective-permute-done((f16[72,768]{1,0:T(8,128)(2,1)S(1)}, f16[72,768]{1,0:T(8,128)(2,1)}, u32[]{:S(2)}, u32[]{:S(2)}) %collective-permute-start.17) | collective-permute-done | bytes 110624 | tf_op jit(solution)/shard_map/ppermute | solution.py:32
  98.2 2.8 %collective-permute-done.15 = f16[72,768]{1,0:T(8,128)(2,1)} collective-permute-done((f16[72,768]{1,0:T(8,128)(2,1)S(1)}, f16[72,768]{1,0:T(8,128)(2,1)}, u32[]{:S(2)}, u32[]{:S(2)}) %collective-permute-start.15) | collective-permute-done | bytes 110624 | tf_op jit(solution)/shard_map/ppermute | solution.py:32
  102.0 5.7 %all-to-all-start.3 = ((f32[16,3,384]{2,1,0:T(4,128)}), f32[16,3,384]{2,1,0:T(4,128)S(1)}, u32[]{:S(2)}, u32[]{:S(2)}) async-start(f32[16,3,384]{2,1,0:T(4,128)} %reshape.54), calls=%async_computation.3 | async-start | bytes 196608 | tf_op jit(solution)/shard_map/all_to_all | solution.py:247
  (84 shorter events, 25.6 us)
Async XLA Ops:
  4.4 23.2 %collective-permute-start.1 = (bf16[64,768]{1,0:T(8,128)(2,1)S(1)}, bf16[64,768]{1,0:T(8,128)(2,1)S(1)}, u32[]{:S(2)}, u32[]{:S(2)}) collective-permute-start(bf16[64,768]{1,0:T(8,128)(2,1)S(1)} %copy.17), channel_id=1, source_target_pairs={{0,128},{1,144},{2,160},{3,176},{4,192},{5,208},{6,224},{7,240},{8... | collective-permute-start | bytes 294920 | tf_op jit(solution)/shard_map/ppermute | solution.py:165
  4.9 22.7 %collective-permute-start = (bf16[64,768]{1,0:T(8,128)(2,1)S(1)}, bf16[64,768]{1,0:T(8,128)(2,1)S(1)}, u32[]{:S(2)}, u32[]{:S(2)}) collective-permute-start(bf16[64,768]{1,0:T(8,128)(2,1)S(1)} %copy.17), channel_id=1, source_target_pairs={{0,0},{1,16},{2,32},{3,48},{4,64},{5,80},{6,96},{7,112},{8,128},{9... | collective-permute-start | bytes 294920 | tf_op jit(solution)/shard_map/ppermute | solution.py:165
  9.8 22.7 %all-to-all-start = ((bf16[16,2,1536]{2,1,0:T(2,128)(2,1)}), bf16[16,2,1536]{2,1,0:T(2,128)(2,1)S(1)}, u32[]{:S(2)}, u32[]{:S(2)}) async-start(bf16[16,2,1536]{2,1,0:T(2,128)(2,1)} %reshape.64), calls=%async_computation | async-start | bytes 196608 | tf_op jit(solution)/shard_map/all_to_all | solution.py:175
  32.7 11.7 %collective-permute-start.5 = (bf16[128,768]{1,0:T(8,128)(2,1)S(1)}, bf16[128,768]{1,0:T(8,128)(2,1)S(1)}, u32[]{:S(2)}, u32[]{:S(2)}) collective-permute-start(bf16[128,768]{1,0:T(8,128)(2,1)S(1)} %pad_maximum_fusion.refs_0_), channel_id=1, source_target_pairs={{0,96},{16,112},{32,0},{48,16},{64,32},{80,48},{96,64},{112,80},{1... | collective-permute-start | bytes 589832 | tf_op jit(solution)/shard_map/ppermute | solution.py:27
  34.4 12.1 %collective-permute-start.4 = (bf16[128,768]{1,0:T(8,128)(2,1)S(1)}, bf16[128,768]{1,0:T(8,128)(2,1)S(1)}, u32[]{:S(2)}, u32[]{:S(2)}) collective-permute-start(bf16[128,768]{1,0:T(8,128)(2,1)S(1)} %pad_maximum_fusion.refs_0_), channel_id=1, source_target_pairs={{0,32},{16,48},{32,64},{48,80},{64,96},{80,112},{96,0},{112,16},{1... | collective-permute-start | bytes 589832 | tf_op jit(solution)/shard_map/ppermute | solution.py:27
  35.7 16.1 %collective-permute-start.3 = (bf16[128,768]{1,0:T(8,128)(2,1)S(1)}, bf16[128,768]{1,0:T(8,128)(2,1)}, u32[]{:S(2)}, u32[]{:S(2)}) collective-permute-start(bf16[128,768]{1,0:T(8,128)(2,1)S(1)} %pad_maximum_fusion.refs_0_), channel_id=1, source_target_pairs={{0,112},{16,0},{32,16},{48,32},{64,48},{80,64},{96,80},{112,96},{1... | collective-permute-start | bytes 589832 | tf_op jit(solution)/shard_map/ppermute | solution.py:27
  36.6 16.1 %collective-permute-start.2 = (bf16[128,768]{1,0:T(8,128)(2,1)S(1)}, bf16[128,768]{1,0:T(8,128)(2,1)}, u32[]{:S(2)}, u32[]{:S(2)}) collective-permute-start(bf16[128,768]{1,0:T(8,128)(2,1)S(1)} %pad_maximum_fusion.refs_0_), channel_id=1, source_target_pairs={{0,16},{16,32},{32,48},{48,64},{64,80},{80,96},{96,112},{112,0},{1... | collective-permute-start | bytes 589832 | tf_op jit(solution)/shard_map/ppermute | solution.py:27
  38.8 17.7 %all-to-all-start.1 = ((bf16[8,64,768]{2,1,0:T(8,128)(2,1)}), bf16[8,64,768]{2,1,0:T(8,128)(2,1)S(1)}, u32[]{:S(2)}, u32[]{:S(2)}) async-start(bf16[8,64,768]{2,1,0:T(8,128)(2,1)} %broadcast_in_dim.12), calls=%async_computation.1 | async-start | bytes 1572864 | tf_op jit(solution)/shard_map/all_to_all | solution.py:180
  47.1 12.7 %collective-permute-start.6 = (bf16[128,768]{1,0:T(8,128)(2,1)S(1)}, bf16[128,768]{1,0:T(8,128)(2,1)}, u32[]{:S(2)}, u32[]{:S(2)}) collective-permute-start(bf16[128,768]{1,0:T(8,128)(2,1)S(1)} %collective-permute-done.4.refs_3_), channel_id=1, source_target_pairs={{0,16},{16,32},{32,48},{48,64},{64,80},{80,96},{96,112},{112,0},{1... | collective-permute-start | bytes 589832 | tf_op jit(solution)/shard_map/ppermute | solution.py:27
  47.8 12.1 %collective-permute-start.7 = (bf16[128,768]{1,0:T(8,128)(2,1)S(1)}, bf16[128,768]{1,0:T(8,128)(2,1)}, u32[]{:S(2)}, u32[]{:S(2)}) collective-permute-start(bf16[128,768]{1,0:T(8,128)(2,1)S(1)} %collective-permute-done.5.refs_4_), channel_id=1, source_target_pairs={{0,112},{16,0},{32,16},{48,32},{64,48},{80,64},{96,80},{112,96},{1... | collective-permute-start | bytes 589832 | tf_op jit(solution)/shard_map/ppermute | solution.py:27
  49.8 6.7 %collective-permute-start.9 = (bf16[64,768]{1,0:T(8,128)(2,1)}, bf16[64,768]{1,0:T(8,128)(2,1)}, u32[]{:S(2)}, u32[]{:S(2)}) collective-permute-start(bf16[64,768]{1,0:T(8,128)(2,1)} %slice.85), channel_id=1, source_target_pairs={{0,96},{16,112},{32,0},{48,16},{64,32},{80,48},{96,64},{112,80},{1... | collective-permute-start | bytes 294920 | tf_op jit(solution)/shard_map/ppermute | solution.py:27
  51.8 8.0 %collective-permute-start.8 = (bf16[64,768]{1,0:T(8,128)(2,1)}, bf16[64,768]{1,0:T(8,128)(2,1)}, u32[]{:S(2)}, u32[]{:S(2)}) collective-permute-start(bf16[64,768]{1,0:T(8,128)(2,1)} %slice.84), channel_id=1, source_target_pairs={{0,32},{16,48},{32,64},{48,80},{64,96},{80,112},{96,0},{112,16},{1... | collective-permute-start | bytes 294920 | tf_op jit(solution)/shard_map/ppermute | solution.py:27
  56.5 3.3 %collective-permute-start.10 = (bf16[512,768]{1,0:T(8,128)(2,1)S(1)}, bf16[512,768]{1,0:T(8,128)(2,1)S(1)}, u32[]{:S(2)}, u32[]{:S(2)}) collective-permute-start(bf16[512,768]{1,0:T(8,128)(2,1)S(1)} %bitcast.63), channel_id=1, source_target_pairs={{0,1},{1,0},{2,3},{3,2},{4,5},{5,4},{6,7},{7,6},{8,9},{9,8},{10,11... | collective-permute-start | bytes 2359304 | tf_op jit(solution)/shard_map/ppermute | solution.py:23
  65.0 2.9 %collective-permute-start.11 = (f32[768,384]{1,0:T(8,128)S(1)}, f32[768,384]{1,0:T(8,128)S(1)}, u32[]{:S(2)}, u32[]{:S(2)}) collective-permute-start(f32[768,384]{1,0:T(8,128)S(1)} %get-tuple-element.46), channel_id=1, source_target_pairs={{0,1},{1,0},{2,3},{3,2},{4,5},{5,4},{6,7},{7,6},{8,9},{9,8},{10,11... | collective-permute-start | bytes 3538952 | tf_op jit(solution)/shard_map/ppermute | solution.py:23
  67.9 7.9 %collective-permute-start.12 = (f32[512,768]{1,0:T(8,128)}, f32[512,768]{1,0:T(8,128)}, u32[]{:S(2)}, u32[]{:S(2)}) collective-permute-start(f32[512,768]{1,0:T(8,128)} %get-tuple-element.52), channel_id=1, source_target_pairs={{0,1},{1,0},{2,3},{3,2},{4,5},{5,4},{6,7},{7,6},{8,9},{9,8},{10,11... | collective-permute-start | bytes 4718600 | tf_op jit(solution)/shard_map/ppermute | solution.py:23
  70.9 25.7 %all-to-all-start.2 = ((f16[16,56,384]{2,1,0:T(8,128)(2,1)}), f16[16,56,384]{2,1,0:T(8,128)(2,1)S(1)}, u32[]{:S(2)}, u32[]{:S(2)}) async-start(f16[16,56,384]{2,1,0:T(8,128)(2,1)} %convert_element_type.70), calls=%async_computation.2 | async-start | bytes 1376256 | tf_op jit(solution)/shard_map/all_to_all | solution.py:227
  80.0 13.6 %collective-permute-start.19 = (f16[72,768]{1,0:T(8,128)(2,1)S(1)}, f16[72,768]{1,0:T(8,128)(2,1)}, u32[]{:S(2)}, u32[]{:S(2)}) collective-permute-start(f16[72,768]{1,0:T(8,128)(2,1)S(1)} %get-tuple-element.85), channel_id=1, source_target_pairs={{0,14},{2,12},{4,2},{6,0},{8,6},{10,4},{12,10},{14,8},{1,15},{3,13... | collective-permute-start | bytes 331784 | tf_op jit(solution)/shard_map/ppermute | solution.py:32
  85.7 8.1 %collective-permute-start.18 = (f16[72,768]{1,0:T(8,128)(2,1)S(1)}, f16[72,768]{1,0:T(8,128)(2,1)}, u32[]{:S(2)}, u32[]{:S(2)}) collective-permute-start(f16[72,768]{1,0:T(8,128)(2,1)S(1)} %get-tuple-element.86), channel_id=1, source_target_pairs={{0,12},{2,14},{4,0},{6,2},{8,4},{10,6},{12,8},{14,10},{1,13},{3,15... | collective-permute-start | bytes 331784 | tf_op jit(solution)/shard_map/ppermute | solution.py:32
  86.5 11.7 %collective-permute-start.17 = (f16[72,768]{1,0:T(8,128)(2,1)S(1)}, f16[72,768]{1,0:T(8,128)(2,1)}, u32[]{:S(2)}, u32[]{:S(2)}) collective-permute-start(f16[72,768]{1,0:T(8,128)(2,1)S(1)} %get-tuple-element.87), channel_id=1, source_target_pairs={{0,10},{2,8},{4,14},{6,12},{8,2},{10,0},{12,6},{14,4},{1,11},{3,9}... | collective-permute-start | bytes 331784 | tf_op jit(solution)/shard_map/ppermute | solution.py:32
  87.7 10.5 %collective-permute-start.16 = (f16[72,768]{1,0:T(8,128)(2,1)S(1)}, f16[72,768]{1,0:T(8,128)(2,1)}, u32[]{:S(2)}, u32[]{:S(2)}) collective-permute-start(f16[72,768]{1,0:T(8,128)(2,1)S(1)} %get-tuple-element.88), channel_id=1, source_target_pairs={{0,8},{2,10},{4,12},{6,14},{8,0},{10,2},{12,4},{14,6},{1,9},{3,11}... | collective-permute-start | bytes 331784 | tf_op jit(solution)/shard_map/ppermute | solution.py:32
  90.0 11.0 %collective-permute-start.15 = (f16[72,768]{1,0:T(8,128)(2,1)S(1)}, f16[72,768]{1,0:T(8,128)(2,1)}, u32[]{:S(2)}, u32[]{:S(2)}) collective-permute-start(f16[72,768]{1,0:T(8,128)(2,1)S(1)} %get-tuple-element.89), channel_id=1, source_target_pairs={{0,6},{2,4},{4,10},{6,8},{8,14},{10,12},{12,2},{14,0},{1,7},{3,5},... | collective-permute-start | bytes 331784 | tf_op jit(solution)/shard_map/ppermute | solution.py:32
  93.6 7.5 %collective-permute-start.14 = (f16[72,768]{1,0:T(8,128)(2,1)S(1)}, f16[72,768]{1,0:T(8,128)(2,1)}, u32[]{:S(2)}, u32[]{:S(2)}) collective-permute-start(f16[72,768]{1,0:T(8,128)(2,1)S(1)} %get-tuple-element.90), channel_id=1, source_target_pairs={{0,4},{2,6},{4,8},{6,10},{8,12},{10,14},{12,0},{14,2},{1,5},{3,7},... | collective-permute-start | bytes 331784 | tf_op jit(solution)/shard_map/ppermute | solution.py:32
  93.7 7.4 %collective-permute-start.13 = (f16[72,768]{1,0:T(8,128)(2,1)S(1)}, f16[72,768]{1,0:T(8,128)(2,1)}, u32[]{:S(2)}, u32[]{:S(2)}) collective-permute-start(f16[72,768]{1,0:T(8,128)(2,1)S(1)} %get-tuple-element.91), channel_id=1, source_target_pairs={{0,2},{2,0},{4,6},{6,4},{8,10},{10,8},{12,14},{14,12},{1,3},{3,1},... | collective-permute-start | bytes 331784 | tf_op jit(solution)/shard_map/ppermute | solution.py:32
  102.0 13.6 %all-to-all-start.3 = ((f32[16,3,384]{2,1,0:T(4,128)}), f32[16,3,384]{2,1,0:T(4,128)S(1)}, u32[]{:S(2)}, u32[]{:S(2)}) async-start(f32[16,3,384]{2,1,0:T(4,128)} %reshape.54), calls=%async_computation.3 | async-start | bytes 196608 | tf_op jit(solution)/shard_map/all_to_all | solution.py:247
  (7 other events, 57.0 us)

commit v5 on v4

--- a/solution.py
+++ b/solution.py
@@ -118,6 +118,14 @@
     for hop in range(1, Y * XH):
         out[hop - 1, :PW, :] = kept[pl.ds(pl.multiple_of(place[16 + hop], PW), PW), :] * scale
         out[hop - 1, PW:, :] = jnp.broadcast_to(power, (8, NV))
+
+
+def sum_three(own, *refs):
+    *got, out = refs
+    total = own[...]
+    for ref in got:
+        total += ref[:PW, :] * jnp.exp2(ref[PW : PW + 1, :] - SCALE)
+    out[...] = total
 
 
 def scale_of(total):
@@ -234,13 +242,11 @@
         n_sems=2,
     )
     got = [next_chip(piece.astype(jnp.float16), hop) for hop, piece in enumerate(pieces, 1)]
-    met, *got = lax.optimization_barrier((met, *got))
+    met, *got[3:] = lax.optimization_barrier((met, *got[3:]))
     vir = jnp.sum(met[:, :VW].astype(f32) * weight_of(met, VW), 0)
-    vir, *got = lax.optimization_barrier((vir, *got))
-    weights = weight_of(jnp.concatenate([piece[PW:] for piece in got], 1), 0)
-    three = own_piece
-    for k, piece in enumerate(got):
-        three = three + piece[:PW].astype(f32) * weights[:, k * NV : (k + 1) * NV]
+    vir, *got[3:] = lax.optimization_barrier((vir, *got[3:]))
+    got = [piece.astype(f32) for piece in got]
+    (three,) = call(sum_three, [((PW, NV), f32)], [own_piece, *got])
     three_index = three[:, None, :]
 
     vir = vir.reshape(NO, VW // NO, HALF_V)

time: 119 us -> 117 us (0.983)
  local copies, waits for them, and re-layouts: 15 us -> 10.8 us
  other arithmetic: 4.01 us -> 8.12 us
  waiting for transfers between devices: 19.2 us -> 16.7 us
    convert_element_type x0 -> x7, other arithmetic: none -> 5.5 us  [per_device(): got = [piece.astype(f32) for piece in got]]
    unnamed x24 -> x22, local copies, waits for them, and re-layouts: 9.87 us -> 5.92 us
    ppermute x7, waiting for transfers between devices: 4.6 us -> 1.38 us  [next_chip(): return lax.ppermute(array, CHIPS, pairs)]
    broadcast_in_dim x1 -> x0, other arithmetic: 1.33 us -> none  [per_device(): three_index = three[:, None, :]]
    pallas_call x4 -> x5, Pallas kernels: 12 us -> 12.1 us  [call(): pl.pallas_call(kernel, out_shape=[jax.ShapeDtypeStruct(s, t) for s, t in...]
  transfers between devices with their start and end apart: 24 -> 24, of which waited for: 10 -> 8; matrix products, arithmetic and copies ran while one was open for 12% -> 12% of each run, Pallas kernels for 6% -> 6%
where the time goes in v5:
time: 117 us; the launch traced here: 115 us
  starting transfers between devices  63.5 us (54%)
  waiting for transfers between devices  16.7 us (14%)
  Pallas kernels  12.2 us (10%)
  local copies, waits for them, and re-layouts  10.8 us (9%)
  other arithmetic  8.12 us (7%)
  matrix products  2 us (2%)
  between operations  1.38 us (1%)
    ppermute x7, starting transfers between devices, next_chip(): return lax.ppermute(array, CHIPS, pairs)  16.2 us
    all_to_all x1, starting transfers between devices, per_device(): local = lax.all_to_all(native, OCC, split_axis=0, concat_axis=0, tiled=True)  14.9 us
    pallas_call x5, Pallas kernels, call(): pl.pallas_call(kernel, out_shape=[jax.ShapeDtypeStruct(s, t) for s, t in...  12.1 us
    ppermute x8, starting transfers between devices, ring(): return lax.ppermute(array, 'z', [(i, (i + by) % Z) for i in range(Z)])  9.98 us
    all_to_all x1, starting transfers between devices, per_device(): vir = lax.all_to_all(vir, AUX, split_axis=0, concat_axis=0, tiled=True)  6.82 us
    unnamed x22, local copies, waits for them, and re-layouts  5.92 us
    all_to_all x1, starting transfers between devices, per_device(): lax.all_to_all(jnp.broadcast_to(local, (Y * XH, PW, NV)), CHIPS, split_ax...  5.6 us
    convert_element_type x7, other arithmetic, per_device(): got = [piece.astype(f32) for piece in got]  5.5 us
  transfers between devices with their start and end apart: 24, of which 8 were waited for; matrix products, arithmetic and copies ran while one was open for 12% of the time, Pallas kernels for 6%

profile of v5, /device:TPU:32, one launch (start us, length us, event | category | flops | bytes accessed | tf_op | source)
XLA Modules:
  0.0 114.7 jit_solution(18105432841335840498)
XLA Ops:
  0.7 1.6 %copy-done = bf16[16,64,1024]{2,1,0:T(8,128)(2,1)S(1)} copy-done((bf16[16,64,1024]{2,1,0:T(8,128)(2,1)S(1)}, bf16[16,64,1024]{2,1,0:T(8,128)(2,1)}, u32[]{:S(2)}) %copy-start) | copy-done | bytes 2097176
  2.2 2.0 %convolution_convert_fusion = bf16[16,64,48]{1,2,0:T(8,128)(2,1)S(1)} fusion(bf16[16,64,1024]{2,1,0:T(8,128)(2,1)S(1)} %copy-done, bf16[1024,48]{0,1:T(8,128)(2,1)} %param.5), kind=kOutput, calls=%fused_computation.1 | convolution fusion | flops 100712448 | bytes 2293760 | tf_op jit(solution)/shard_map/ipm,ma->ipa/dot_general | solution.py:166
  4.9 4.1 %collective-permute-start = (bf16[64,768]{1,0:T(8,128)(2,1)S(1)}, bf16[64,768]{1,0:T(8,128)(2,1)S(1)}, u32[]{:S(2)}, u32[]{:S(2)}) collective-permute-start(bf16[64,768]{1,0:T(8,128)(2,1)S(1)} %copy.17), channel_id=1, source_target_pairs={{0,0},{1,16},{2,32},{3,48},{4,64},{5,80},{6,96},{7,112},{8,128},{9... | collective-permute-start | bytes 294920 | tf_op jit(solution)/shard_map/ppermute | solution.py:173
  9.8 14.9 %all-to-all-start = ((bf16[16,2,1536]{2,1,0:T(2,128)(2,1)}), bf16[16,2,1536]{2,1,0:T(2,128)(2,1)S(1)}, u32[]{:S(2)}, u32[]{:S(2)}) async-start(bf16[16,2,1536]{2,1,0:T(2,128)(2,1)} %reshape.57), calls=%async_computation | async-start | bytes 196608 | tf_op jit(solution)/shard_map/all_to_all | solution.py:183
  27.7 4.9 %all-to-all-done = bf16[16,2,1536]{2,1,0:T(2,128)(2,1)S(1)} async-done(((bf16[16,2,1536]{2,1,0:T(2,128)(2,1)}), bf16[16,2,1536]{2,1,0:T(2,128)(2,1)S(1)}, u32[]{:S(2)}, u32[]{:S(2)}) %all-to-all-start) | async-done | bytes 98336 | tf_op jit(solution)/shard_map/all_to_all | solution.py:183
  32.7 1.7 %collective-permute-start.5 = (bf16[128,768]{1,0:T(8,128)(2,1)S(1)}, bf16[128,768]{1,0:T(8,128)(2,1)S(1)}, u32[]{:S(2)}, u32[]{:S(2)}) collective-permute-start(bf16[128,768]{1,0:T(8,128)(2,1)S(1)} %pad_maximum_fusion.refs_0_), channel_id=1, source_target_pairs={{0,96},{16,112},{32,0},{48,16},{64,32},{80,48},{96,64},{112,80},{1... | collective-permute-start | bytes 589832 | tf_op jit(solution)/shard_map/ppermute | solution.py:27
  34.4 1.3 %collective-permute-start.4 = (bf16[128,768]{1,0:T(8,128)(2,1)S(1)}, bf16[128,768]{1,0:T(8,128)(2,1)S(1)}, u32[]{:S(2)}, u32[]{:S(2)}) collective-permute-start(bf16[128,768]{1,0:T(8,128)(2,1)S(1)} %pad_maximum_fusion.refs_0_), channel_id=1, source_target_pairs={{0,32},{16,48},{32,64},{48,80},{64,96},{80,112},{96,0},{112,16},{1... | collective-permute-start | bytes 589832 | tf_op jit(solution)/shard_map/ppermute | solution.py:27
  38.8 5.6 %all-to-all-start.1 = ((bf16[8,64,768]{2,1,0:T(8,128)(2,1)}), bf16[8,64,768]{2,1,0:T(8,128)(2,1)S(1)}, u32[]{:S(2)}, u32[]{:S(2)}) async-start(bf16[8,64,768]{2,1,0:T(8,128)(2,1)} %broadcast_in_dim.12), calls=%async_computation.1 | async-start | bytes 1572864 | tf_op jit(solution)/shard_map/all_to_all | solution.py:188
  44.4 2.1 %collective-permute-done.4.refs_3_ = bf16[128,768]{1,0:T(8,128)(2,1)S(1)} collective-permute-done((bf16[128,768]{1,0:T(8,128)(2,1)S(1)}, bf16[128,768]{1,0:T(8,128)(2,1)S(1)}, u32[]{:S(2)}, u32[]{:S(2)}) %collective-permute-start.4) | collective-permute-done | bytes 196640 | tf_op jit(solution)/shard_map/ppermute | solution.py:27
  47.8 2.0 %collective-permute-start.7 = (bf16[128,768]{1,0:T(8,128)(2,1)S(1)}, bf16[128,768]{1,0:T(8,128)(2,1)}, u32[]{:S(2)}, u32[]{:S(2)}) collective-permute-start(bf16[128,768]{1,0:T(8,128)(2,1)S(1)} %collective-permute-done.5.refs_4_), channel_id=1, source_target_pairs={{0,112},{16,0},{32,16},{48,32},{64,48},{80,64},{96,80},{112,96},{1... | collective-permute-start | bytes 589832 | tf_op jit(solution)/shard_map/ppermute | solution.py:27
  49.8 2.0 %collective-permute-start.9 = (bf16[64,768]{1,0:T(8,128)(2,1)}, bf16[64,768]{1,0:T(8,128)(2,1)}, u32[]{:S(2)}, u32[]{:S(2)}) collective-permute-start(bf16[64,768]{1,0:T(8,128)(2,1)} %slice.19), channel_id=1, source_target_pairs={{0,96},{16,112},{32,0},{48,16},{64,32},{80,48},{96,64},{112,80},{1... | collective-permute-start | bytes 294920 | tf_op jit(solution)/shard_map/ppermute | solution.py:27
  52.7 3.7 %all-to-all-done.1 = bf16[8,64,768]{2,1,0:T(8,128)(2,1)S(1)} async-done(((bf16[8,64,768]{2,1,0:T(8,128)(2,1)}), bf16[8,64,768]{2,1,0:T(8,128)(2,1)S(1)}, u32[]{:S(2)}, u32[]{:S(2)}) %all-to-all-start.1) | async-done | bytes 786464 | tf_op jit(solution)/shard_map/all_to_all | solution.py:188
  56.5 3.3 %collective-permute-done.8.refs_7_ = bf16[64,768]{1,0:T(8,128)(2,1)} collective-permute-done((bf16[64,768]{1,0:T(8,128)(2,1)}, bf16[64,768]{1,0:T(8,128)(2,1)}, u32[]{:S(2)}, u32[]{:S(2)}) %collective-permute-start.8) | collective-permute-done | bytes 98336 | tf_op jit(solution)/shard_map/ppermute | solution.py:27
  59.8 5.1 %shard_map.62 = (bf16[1024,768]{1,0:T(8,128)(2,1)S(1)}, bf16[768,768]{1,0:T(8,128)(2,1)S(1)}, f32[768,384]{1,0:T(8,128)S(1)}) custom-call(s32[25]{0:T(128)S(1)} %stack.103.place, bf16[128,768]{1,0:T(8,128)(2,1)S(1)} %pad_maximum_fusion.refs_0_, bf16[128,768]{1,0:T(8,128)(2,1)} %collective-permute-done.2.refs_1_, ...), custom_call_target="tpu_custom_call" | custom-call | flops 1660944384 | bytes 6291456 | tf_op jit(solution)/shard_map/pallas_call | solution.py:151
  65.1 2.7 %shard_map.63 = (f32[512,768]{1,0:T(8,128)}, f32[512,768]{1,0:T(8,128)S(1)}) custom-call(s32[25]{0:T(128)S(1)} %stack.103.place, bf16[1024,768]{1,0:T(8,128)(2,1)S(1)} %get-tuple-element.41.rows, bf16[768,768]{1,0:T(8,128)(2,1)S(1)} %get-tuple-element.39.amp), custom_call_target="tpu_custom_call" | custom-call | flops 1207959552 | bytes 6291456 | tf_op jit(solution)/shard_map/pallas_call | solution.py:151
  68.3 1.6 %shard_map.64 = f32[16,56,384]{2,1,0:T(8,128)S(1)} custom-call(s32[25]{0:T(128)S(1)} %stack.103.place, bf16[768,768]{1,0:T(8,128)(2,1)S(1)} %get-tuple-element.39.amp, f32[768,384]{1,0:T(8,128)S(1)} %collective-permute-done.11.got), custom_call_target="tpu_custom_call" | custom-call | flops 452984832 | bytes 6291456 | tf_op jit(solution)/shard_map/pallas_call | solution.py:151
  70.9 4.9 %all-to-all-start.2 = ((f16[16,56,384]{2,1,0:T(8,128)(2,1)}), f16[16,56,384]{2,1,0:T(8,128)(2,1)S(1)}, u32[]{:S(2)}, u32[]{:S(2)}) async-start(f16[16,56,384]{2,1,0:T(8,128)(2,1)} %convert_element_type.67), calls=%async_computation.2 | async-start | bytes 1376256 | tf_op jit(solution)/shard_map/all_to_all | solution.py:235
  75.8 1.4 %copy-done.2 = f32[512,768]{1,0:T(8,128)S(1)} copy-done((f32[512,768]{1,0:T(8,128)S(1)}, f32[512,768]{1,0:T(8,128)}, u32[]{:S(2)}) %copy-start.2) | copy-done | bytes 1572888
  77.2 2.6 %shard_map.65 = (f32[64,768]{1,0:T(8,128)S(1)}, f32[7,72,768]{2,1,0:T(8,128)S(1)}) custom-call(s32[25]{0:T(128)S(1)} %stack.103.place, f32[512,768]{1,0:T(8,128)S(1)} %copy-done.2, f32[512,768]{1,0:T(8,128)} %collective-permute-done.12.got), custom_call_target="tpu_custom_call" | custom-call | bytes 6291456 | tf_op jit(solution)/shard_map/pallas_call | solution.py:151
  80.6 5.5 %collective-permute-start.19 = (f16[72,768]{1,0:T(8,128)(2,1)S(1)}, f16[72,768]{1,0:T(8,128)(2,1)S(1)}, u32[]{:S(2)}, u32[]{:S(2)}) collective-permute-start(f16[72,768]{1,0:T(8,128)(2,1)S(1)} %get-tuple-element.66), channel_id=1, source_target_pairs={{0,14},{2,12},{4,2},{6,0},{8,6},{10,4},{12,10},{14,8},{1,15},{3,13... | collective-permute-start | bytes 331784 | tf_op jit(solution)/shard_map/ppermute | solution.py:32
  88.2 2.3 %collective-permute-start.16 = (f16[72,768]{1,0:T(8,128)(2,1)S(1)}, f16[72,768]{1,0:T(8,128)(2,1)}, u32[]{:S(2)}, u32[]{:S(2)}) collective-permute-start(f16[72,768]{1,0:T(8,128)(2,1)S(1)} %get-tuple-element.69), channel_id=1, source_target_pairs={{0,8},{2,10},{4,12},{6,14},{8,0},{10,2},{12,4},{14,6},{1,9},{3,11}... | collective-permute-start | bytes 331784 | tf_op jit(solution)/shard_map/ppermute | solution.py:32
  90.5 3.6 %collective-permute-start.15 = (f16[72,768]{1,0:T(8,128)(2,1)S(1)}, f16[72,768]{1,0:T(8,128)(2,1)}, u32[]{:S(2)}, u32[]{:S(2)}) collective-permute-start(f16[72,768]{1,0:T(8,128)(2,1)S(1)} %get-tuple-element.70), channel_id=1, source_target_pairs={{0,6},{2,4},{4,10},{6,8},{8,14},{10,12},{12,2},{14,0},{1,7},{3,5},... | collective-permute-start | bytes 331784 | tf_op jit(solution)/shard_map/ppermute | solution.py:32
  94.8 2.8 %collective-permute-start.13 = (f16[72,768]{1,0:T(8,128)(2,1)S(1)}, f16[72,768]{1,0:T(8,128)(2,1)}, u32[]{:S(2)}, u32[]{:S(2)}) collective-permute-start(f16[72,768]{1,0:T(8,128)(2,1)S(1)} %get-tuple-element.72), channel_id=1, source_target_pairs={{0,2},{2,0},{4,6},{6,4},{8,10},{10,8},{12,14},{14,12},{1,3},{3,1},... | collective-permute-start | bytes 331784 | tf_op jit(solution)/shard_map/ppermute | solution.py:32
  99.5 6.8 %all-to-all-start.3 = ((f32[16,3,384]{2,1,0:T(4,128)}), f32[16,3,384]{2,1,0:T(4,128)S(1)}, u32[]{:S(2)}, u32[]{:S(2)}) async-start(f32[16,3,384]{2,1,0:T(4,128)} %reshape.54), calls=%async_computation.3 | async-start | bytes 196608 | tf_op jit(solution)/shard_map/all_to_all | solution.py:253
  (85 shorter events, 24.9 us)
Async XLA Ops:
  4.4 23.2 %collective-permute-start.1 = (bf16[64,768]{1,0:T(8,128)(2,1)S(1)}, bf16[64,768]{1,0:T(8,128)(2,1)S(1)}, u32[]{:S(2)}, u32[]{:S(2)}) collective-permute-start(bf16[64,768]{1,0:T(8,128)(2,1)S(1)} %copy.17), channel_id=1, source_target_pairs={{0,128},{1,144},{2,160},{3,176},{4,192},{5,208},{6,224},{7,240},{8... | collective-permute-start | bytes 294920 | tf_op jit(solution)/shard_map/ppermute | solution.py:173
  4.9 22.7 %collective-permute-start = (bf16[64,768]{1,0:T(8,128)(2,1)S(1)}, bf16[64,768]{1,0:T(8,128)(2,1)S(1)}, u32[]{:S(2)}, u32[]{:S(2)}) collective-permute-start(bf16[64,768]{1,0:T(8,128)(2,1)S(1)} %copy.17), channel_id=1, source_target_pairs={{0,0},{1,16},{2,32},{3,48},{4,64},{5,80},{6,96},{7,112},{8,128},{9... | collective-permute-start | bytes 294920 | tf_op jit(solution)/shard_map/ppermute | solution.py:173
  9.8 22.7 %all-to-all-start = ((bf16[16,2,1536]{2,1,0:T(2,128)(2,1)}), bf16[16,2,1536]{2,1,0:T(2,128)(2,1)S(1)}, u32[]{:S(2)}, u32[]{:S(2)}) async-start(bf16[16,2,1536]{2,1,0:T(2,128)(2,1)} %reshape.57), calls=%async_computation | async-start | bytes 196608 | tf_op jit(solution)/shard_map/all_to_all | solution.py:183
  32.7 11.7 %collective-permute-start.5 = (bf16[128,768]{1,0:T(8,128)(2,1)S(1)}, bf16[128,768]{1,0:T(8,128)(2,1)S(1)}, u32[]{:S(2)}, u32[]{:S(2)}) collective-permute-start(bf16[128,768]{1,0:T(8,128)(2,1)S(1)} %pad_maximum_fusion.refs_0_), channel_id=1, source_target_pairs={{0,96},{16,112},{32,0},{48,16},{64,32},{80,48},{96,64},{112,80},{1... | collective-permute-start | bytes 589832 | tf_op jit(solution)/shard_map/ppermute | solution.py:27
  34.4 12.1 %collective-permute-start.4 = (bf16[128,768]{1,0:T(8,128)(2,1)S(1)}, bf16[128,768]{1,0:T(8,128)(2,1)S(1)}, u32[]{:S(2)}, u32[]{:S(2)}) collective-permute-start(bf16[128,768]{1,0:T(8,128)(2,1)S(1)} %pad_maximum_fusion.refs_0_), channel_id=1, source_target_pairs={{0,32},{16,48},{32,64},{48,80},{64,96},{80,112},{96,0},{112,16},{1... | collective-permute-start | bytes 589832 | tf_op jit(solution)/shard_map/ppermute | solution.py:27
  35.7 16.1 %collective-permute-start.3 = (bf16[128,768]{1,0:T(8,128)(2,1)S(1)}, bf16[128,768]{1,0:T(8,128)(2,1)}, u32[]{:S(2)}, u32[]{:S(2)}) collective-permute-start(bf16[128,768]{1,0:T(8,128)(2,1)S(1)} %pad_maximum_fusion.refs_0_), channel_id=1, source_target_pairs={{0,112},{16,0},{32,16},{48,32},{64,48},{80,64},{96,80},{112,96},{1... | collective-permute-start | bytes 589832 | tf_op jit(solution)/shard_map/ppermute | solution.py:27
  36.6 16.1 %collective-permute-start.2 = (bf16[128,768]{1,0:T(8,128)(2,1)S(1)}, bf16[128,768]{1,0:T(8,128)(2,1)}, u32[]{:S(2)}, u32[]{:S(2)}) collective-permute-start(bf16[128,768]{1,0:T(8,128)(2,1)S(1)} %pad_maximum_fusion.refs_0_), channel_id=1, source_target_pairs={{0,16},{16,32},{32,48},{48,64},{64,80},{80,96},{96,112},{112,0},{1... | collective-permute-start | bytes 589832 | tf_op jit(solution)/shard_map/ppermute | solution.py:27
  38.8 17.7 %all-to-all-start.1 = ((bf16[8,64,768]{2,1,0:T(8,128)(2,1)}), bf16[8,64,768]{2,1,0:T(8,128)(2,1)S(1)}, u32[]{:S(2)}, u32[]{:S(2)}) async-start(bf16[8,64,768]{2,1,0:T(8,128)(2,1)} %broadcast_in_dim.12), calls=%async_computation.1 | async-start | bytes 1572864 | tf_op jit(solution)/shard_map/all_to_all | solution.py:188
  47.1 12.7 %collective-permute-start.6 = (bf16[128,768]{1,0:T(8,128)(2,1)S(1)}, bf16[128,768]{1,0:T(8,128)(2,1)}, u32[]{:S(2)}, u32[]{:S(2)}) collective-permute-start(bf16[128,768]{1,0:T(8,128)(2,1)S(1)} %collective-permute-done.4.refs_3_), channel_id=1, source_target_pairs={{0,16},{16,32},{32,48},{48,64},{64,80},{80,96},{96,112},{112,0},{1... | collective-permute-start | bytes 589832 | tf_op jit(solution)/shard_map/ppermute | solution.py:27
  47.8 12.1 %collective-permute-start.7 = (bf16[128,768]{1,0:T(8,128)(2,1)S(1)}, bf16[128,768]{1,0:T(8,128)(2,1)}, u32[]{:S(2)}, u32[]{:S(2)}) collective-permute-start(bf16[128,768]{1,0:T(8,128)(2,1)S(1)} %collective-permute-done.5.refs_4_), channel_id=1, source_target_pairs={{0,112},{16,0},{32,16},{48,32},{64,48},{80,64},{96,80},{112,96},{1... | collective-permute-start | bytes 589832 | tf_op jit(solution)/shard_map/ppermute | solution.py:27
  49.8 6.7 %collective-permute-start.9 = (bf16[64,768]{1,0:T(8,128)(2,1)}, bf16[64,768]{1,0:T(8,128)(2,1)}, u32[]{:S(2)}, u32[]{:S(2)}) collective-permute-start(bf16[64,768]{1,0:T(8,128)(2,1)} %slice.19), channel_id=1, source_target_pairs={{0,96},{16,112},{32,0},{48,16},{64,32},{80,48},{96,64},{112,80},{1... | collective-permute-start | bytes 294920 | tf_op jit(solution)/shard_map/ppermute | solution.py:27
  51.8 8.0 %collective-permute-start.8 = (bf16[64,768]{1,0:T(8,128)(2,1)}, bf16[64,768]{1,0:T(8,128)(2,1)}, u32[]{:S(2)}, u32[]{:S(2)}) collective-permute-start(bf16[64,768]{1,0:T(8,128)(2,1)} %slice.18), channel_id=1, source_target_pairs={{0,32},{16,48},{32,64},{48,80},{64,96},{80,112},{96,0},{112,16},{1... | collective-permute-start | bytes 294920 | tf_op jit(solution)/shard_map/ppermute | solution.py:27
  56.5 3.4 %collective-permute-start.10 = (bf16[512,768]{1,0:T(8,128)(2,1)S(1)}, bf16[512,768]{1,0:T(8,128)(2,1)S(1)}, u32[]{:S(2)}, u32[]{:S(2)}) collective-permute-start(bf16[512,768]{1,0:T(8,128)(2,1)S(1)} %bitcast.63), channel_id=1, source_target_pairs={{0,1},{1,0},{2,3},{3,2},{4,5},{5,4},{6,7},{7,6},{8,9},{9,8},{10,11... | collective-permute-start | bytes 2359304 | tf_op jit(solution)/shard_map/ppermute | solution.py:23
  65.0 2.9 %collective-permute-start.11 = (f32[768,384]{1,0:T(8,128)S(1)}, f32[768,384]{1,0:T(8,128)S(1)}, u32[]{:S(2)}, u32[]{:S(2)}) collective-permute-start(f32[768,384]{1,0:T(8,128)S(1)} %get-tuple-element.40), channel_id=1, source_target_pairs={{0,1},{1,0},{2,3},{3,2},{4,5},{5,4},{6,7},{7,6},{8,9},{9,8},{10,11... | collective-permute-start | bytes 3538952 | tf_op jit(solution)/shard_map/ppermute | solution.py:23
  67.9 7.9 %collective-permute-start.12 = (f32[512,768]{1,0:T(8,128)}, f32[512,768]{1,0:T(8,128)}, u32[]{:S(2)}, u32[]{:S(2)}) collective-permute-start(f32[512,768]{1,0:T(8,128)} %get-tuple-element.46), channel_id=1, source_target_pairs={{0,1},{1,0},{2,3},{3,2},{4,5},{5,4},{6,7},{7,6},{8,9},{9,8},{10,11... | collective-permute-start | bytes 4718600 | tf_op jit(solution)/shard_map/ppermute | solution.py:23
  70.9 26.6 %all-to-all-start.2 = ((f16[16,56,384]{2,1,0:T(8,128)(2,1)}), f16[16,56,384]{2,1,0:T(8,128)(2,1)S(1)}, u32[]{:S(2)}, u32[]{:S(2)}) async-start(f16[16,56,384]{2,1,0:T(8,128)(2,1)} %convert_element_type.67), calls=%async_computation.2 | async-start | bytes 1376256 | tf_op jit(solution)/shard_map/all_to_all | solution.py:235
  80.6 13.5 %collective-permute-start.19 = (f16[72,768]{1,0:T(8,128)(2,1)S(1)}, f16[72,768]{1,0:T(8,128)(2,1)S(1)}, u32[]{:S(2)}, u32[]{:S(2)}) collective-permute-start(f16[72,768]{1,0:T(8,128)(2,1)S(1)} %get-tuple-element.66), channel_id=1, source_target_pairs={{0,14},{2,12},{4,2},{6,0},{8,6},{10,4},{12,10},{14,8},{1,15},{3,13... | collective-permute-start | bytes 331784 | tf_op jit(solution)/shard_map/ppermute | solution.py:32
  86.2 8.3 %collective-permute-start.18 = (f16[72,768]{1,0:T(8,128)(2,1)S(1)}, f16[72,768]{1,0:T(8,128)(2,1)}, u32[]{:S(2)}, u32[]{:S(2)}) collective-permute-start(f16[72,768]{1,0:T(8,128)(2,1)S(1)} %get-tuple-element.67), channel_id=1, source_target_pairs={{0,12},{2,14},{4,0},{6,2},{8,4},{10,6},{12,8},{14,10},{1,13},{3,15... | collective-permute-start | bytes 331784 | tf_op jit(solution)/shard_map/ppermute | solution.py:32
  87.0 11.6 %collective-permute-start.17 = (f16[72,768]{1,0:T(8,128)(2,1)}, f16[72,768]{1,0:T(8,128)(2,1)}, u32[]{:S(2)}, u32[]{:S(2)}) collective-permute-start(f16[72,768]{1,0:T(8,128)(2,1)} %get-tuple-element.68), channel_id=1, source_target_pairs={{0,10},{2,8},{4,14},{6,12},{8,2},{10,0},{12,6},{14,4},{1,11},{3,9}... | collective-permute-start | bytes 331784 | tf_op jit(solution)/shard_map/ppermute | solution.py:32
  88.2 10.4 %collective-permute-start.16 = (f16[72,768]{1,0:T(8,128)(2,1)S(1)}, f16[72,768]{1,0:T(8,128)(2,1)}, u32[]{:S(2)}, u32[]{:S(2)}) collective-permute-start(f16[72,768]{1,0:T(8,128)(2,1)S(1)} %get-tuple-element.69), channel_id=1, source_target_pairs={{0,8},{2,10},{4,12},{6,14},{8,0},{10,2},{12,4},{14,6},{1,9},{3,11}... | collective-permute-start | bytes 331784 | tf_op jit(solution)/shard_map/ppermute | solution.py:32
  90.5 18.6 %collective-permute-start.15 = (f16[72,768]{1,0:T(8,128)(2,1)S(1)}, f16[72,768]{1,0:T(8,128)(2,1)}, u32[]{:S(2)}, u32[]{:S(2)}) collective-permute-start(f16[72,768]{1,0:T(8,128)(2,1)S(1)} %get-tuple-element.70), channel_id=1, source_target_pairs={{0,6},{2,4},{4,10},{6,8},{8,14},{10,12},{12,2},{14,0},{1,7},{3,5},... | collective-permute-start | bytes 331784 | tf_op jit(solution)/shard_map/ppermute | solution.py:32
  94.1 15.9 %collective-permute-start.14 = (f16[72,768]{1,0:T(8,128)(2,1)S(1)}, f16[72,768]{1,0:T(8,128)(2,1)}, u32[]{:S(2)}, u32[]{:S(2)}) collective-permute-start(f16[72,768]{1,0:T(8,128)(2,1)S(1)} %get-tuple-element.71), channel_id=1, source_target_pairs={{0,4},{2,6},{4,8},{6,10},{8,12},{10,14},{12,0},{14,2},{1,5},{3,7},... | collective-permute-start | bytes 331784 | tf_op jit(solution)/shard_map/ppermute | solution.py:32
  94.8 16.2 %collective-permute-start.13 = (f16[72,768]{1,0:T(8,128)(2,1)S(1)}, f16[72,768]{1,0:T(8,128)(2,1)}, u32[]{:S(2)}, u32[]{:S(2)}) collective-permute-start(f16[72,768]{1,0:T(8,128)(2,1)S(1)} %get-tuple-element.72), channel_id=1, source_target_pairs={{0,2},{2,0},{4,6},{6,4},{8,10},{10,8},{12,14},{14,12},{1,3},{3,1},... | collective-permute-start | bytes 331784 | tf_op jit(solution)/shard_map/ppermute | solution.py:32
  99.5 14.6 %all-to-all-start.3 = ((f32[16,3,384]{2,1,0:T(4,128)}), f32[16,3,384]{2,1,0:T(4,128)S(1)}, u32[]{:S(2)}, u32[]{:S(2)}) async-start(f32[16,3,384]{2,1,0:T(4,128)} %reshape.54), calls=%async_computation.3 | async-start | bytes 196608 | tf_op jit(solution)/shard_map/all_to_all | solution.py:253
  (9 other events, 68.1 us)

commit v6 on v5

--- a/solution.py
+++ b/solution.py
@@ -24,7 +24,10 @@
 
 
 def ring(array, by):
-    return lax.ppermute(array, "z", [(i, (i + by) % Z) for i in range(Z)])
+    pairs = [
+        (z * C + c, (z + (1 - 2 * c) * by) % Z * C + c) for z in range(Z) for c in range(C)
+    ]
+    return lax.ppermute(array, ("z", "c"), pairs)
 
 
 def next_chip(array, hop):
@@ -71,8 +74,8 @@
         copy.start()
     for copy in copies:
         copy.wait()
-    for k in range(NV // 256):
-        here = slice(k * 256, (k + 1) * 256)
+    for k in range(NV // 384):
+        here = slice(k * 384, (k + 1) * 384)
         coulomb = lax.dot_general(
             rows[:, here], cols[...], TRANSPOSED, preferred_element_type=jnp.float32
         )
@@ -82,8 +85,8 @@
 
 def virtual_block(amp, half, vir):
     side = amp[:, pl.ds(pl.multiple_of(half * HALF_V, HALF_V), HALF_V)]
-    for k in range(NV // 256):
-        here = slice(k * 256, (k + 1) * 256)
+    for k in range(NV // 384):
+        here = slice(k * 384, (k + 1) * 384)
         vir[here, :] = lax.dot_general(
             amp[:, here], side, TRANSPOSED, preferred_element_type=jnp.float32
         )
@@ -192,13 +195,13 @@
     col_energy = paced(col_energy, PACE)
     up2, down2, col_energy = lax.optimization_barrier((up2, down2, col_energy))
     col_energy = paced(col_energy, PACE)
-    up3, down3 = ring(up2, 1), ring(down2, -1)
-    up4, down4 = ring(up2[:PW], 2), ring(down2[PW:], -2)
+    up3, down3, far = ring(up2, 1), ring(down2, -1), ring(up2, 2)
     other_cols = swap(own_cols, "c")
-    row_arrays = [pair, up1, down1, up2, down2, up3, down3, up4, down4]
+    row_arrays = [pair, up1, down1, up2, down2, up3, down3, far]
     owners = []
     for step in (0, -1, 1, -2, 2, -3, 3, Z // 2):
-        owners += [(xl * Z + (z + step) % Z), ((1 - xl) * Z + (z + step) % Z)]
+        at = (z + (1 - 2 * c) * step) % Z
+        owners += [xl * Z + at, (1 - xl) * Z + at]
     places = [o % C * HALF_P + o // C * PW for o in owners]
     places += [hop_from(chip, hop) * PW for hop in range(Y * XH)] + [c]
     place = jnp.stack(places).astype(jnp.int32)

time: 117 us -> 115 us (0.983)
  starting transfers between devices: 63.5 us -> 60.3 us
  waiting for transfers between devices: 16.7 us -> 19.9 us
    ppermute x8 -> x7, waiting for transfers between devices: 5.42 us -> 0.66 us  [ring(): return lax.ppermute(array, ('z', 'c'), pairs)]
    all_to_all x1, waiting for transfers between devices: 3.72 us -> 7.85 us  [per_device(): lax.all_to_all(jnp.broadcast_to(local, (Y * XH, PW, NV)), CHIPS, split_ax...]
    ppermute x7, starting transfers between devices: 16.2 us -> 12.6 us  [next_chip(): return lax.ppermute(array, CHIPS, pairs)]
    ppermute x3, waiting for transfers between devices: 0.1 us -> 2.24 us  [swap(): return lax.ppermute(array, axis, [(0, 1), (1, 0)])]
    slice x2 -> x0, local copies, waits for them, and re-layouts: 1.3 us -> none  [per_device(): up4, down4 = (ring(up2[:PW], 2), ring(down2[PW:], -2))]
    ppermute x8 -> x7, starting transfers between devices: 9.98 us -> 9.54 us  [ring(): return lax.ppermute(array, ('z', 'c'), pairs)]
  transfers between devices with their start and end apart: 24 -> 23, of which waited for: 8 -> 8; matrix products, arithmetic and copies ran while one was open for 12% -> 11% of each run, Pallas kernels for 6% -> 6%
where the time goes in v6:
time: 115 us; the launch traced here: 114 us
  starting transfers between devices  60.3 us (52%)
  waiting for transfers between devices  19.9 us (17%)
  Pallas kernels  11.9 us (10%)
  local copies, waits for them, and re-layouts  9.87 us (9%)
  other arithmetic  8.12 us (7%)
  matrix products  2 us (2%)
  between operations  1.42 us (1%)
    all_to_all x1, starting transfers between devices, per_device(): local = lax.all_to_all(native, OCC, split_axis=0, concat_axis=0, tiled=True)  14.9 us
    ppermute x7, starting transfers between devices, next_chip(): return lax.ppermute(array, CHIPS, pairs)  12.6 us
    pallas_call x5, Pallas kernels, call(): pl.pallas_call(kernel, out_shape=[jax.ShapeDtypeStruct(s, t) for s, t in...  11.9 us
    ppermute x7, starting transfers between devices, ring(): return lax.ppermute(array, ('z', 'c'), pairs)  9.54 us
    all_to_all x1, waiting for transfers between devices, per_device(): lax.all_to_all(jnp.broadcast_to(local, (Y * XH, PW, NV)), CHIPS, split_ax...  7.85 us
    unnamed x22, local copies, waits for them, and re-layouts  6.24 us
    all_to_all x1, starting transfers between devices, per_device(): vir = lax.all_to_all(vir, AUX, split_axis=0, concat_axis=0, tiled=True)  6.24 us
    all_to_all x1, starting transfers between devices, per_device(): met = lax.all_to_all(packed, OCC, split_axis=0, concat_axis=0, tiled=True)  6.03 us
  transfers between devices with their start and end apart: 23, of which 8 were waited for; matrix products, arithmetic and copies ran while one was open for 11% of the time, Pallas kernels for 6%

profile of v6, /device:TPU:32, one launch (start us, length us, event | category | flops | bytes accessed | tf_op | source)
XLA Modules:
  0.0 113.5 jit_solution(5872370645065091925)
XLA Ops:
  0.7 1.6 %copy-done = bf16[16,64,1024]{2,1,0:T(8,128)(2,1)S(1)} copy-done((bf16[16,64,1024]{2,1,0:T(8,128)(2,1)S(1)}, bf16[16,64,1024]{2,1,0:T(8,128)(2,1)}, u32[]{:S(2)}) %copy-start) | copy-done | bytes 2097176
  2.2 2.0 %convolution_convert_fusion = bf16[16,64,48]{1,2,0:T(8,128)(2,1)S(1)} fusion(bf16[16,64,1024]{2,1,0:T(8,128)(2,1)S(1)} %copy-done, bf16[1024,48]{0,1:T(8,128)(2,1)} %param.5), kind=kOutput, calls=%fused_computation.1 | convolution fusion | flops 100712448 | bytes 2293760 | tf_op jit(solution)/shard_map/ipm,ma->ipa/dot_general | solution.py:169
  4.9 4.1 %collective-permute-start = (bf16[64,768]{1,0:T(8,128)(2,1)S(1)}, bf16[64,768]{1,0:T(8,128)(2,1)S(1)}, u32[]{:S(2)}, u32[]{:S(2)}) collective-permute-start(bf16[64,768]{1,0:T(8,128)(2,1)S(1)} %copy.17), channel_id=1, source_target_pairs={{0,0},{1,16},{2,32},{3,48},{4,64},{5,80},{6,96},{7,112},{8,128},{9... | collective-permute-start | bytes 294920 | tf_op jit(solution)/shard_map/ppermute | solution.py:176
  9.8 14.9 %all-to-all-start = ((bf16[16,2,1536]{2,1,0:T(2,128)(2,1)}), bf16[16,2,1536]{2,1,0:T(2,128)(2,1)S(1)}, u32[]{:S(2)}, u32[]{:S(2)}) async-start(bf16[16,2,1536]{2,1,0:T(2,128)(2,1)} %reshape.57), calls=%async_computation | async-start | bytes 196608 | tf_op jit(solution)/shard_map/all_to_all | solution.py:186
  27.7 4.8 %all-to-all-done = bf16[16,2,1536]{2,1,0:T(2,128)(2,1)S(1)} async-done(((bf16[16,2,1536]{2,1,0:T(2,128)(2,1)}), bf16[16,2,1536]{2,1,0:T(2,128)(2,1)S(1)}, u32[]{:S(2)}, u32[]{:S(2)}) %all-to-all-start) | async-done | bytes 98336 | tf_op jit(solution)/shard_map/all_to_all | solution.py:186
  32.7 1.7 %collective-permute-start.5 = (bf16[128,768]{1,0:T(8,128)(2,1)S(1)}, bf16[128,768]{1,0:T(8,128)(2,1)S(1)}, u32[]{:S(2)}, u32[]{:S(2)}) collective-permute-start(bf16[128,768]{1,0:T(8,128)(2,1)S(1)} %pad_maximum_fusion.refs_0_), channel_id=1, source_target_pairs={{0,96},{1,33},{16,112},{17,49},{32,0},{33,65},{48,16},{49,81},{64,... | collective-permute-start | bytes 589832 | tf_op jit(solution)/shard_map/ppermute | solution.py:30
  34.4 1.3 %collective-permute-start.4 = (bf16[128,768]{1,0:T(8,128)(2,1)S(1)}, bf16[128,768]{1,0:T(8,128)(2,1)S(1)}, u32[]{:S(2)}, u32[]{:S(2)}) collective-permute-start(bf16[128,768]{1,0:T(8,128)(2,1)S(1)} %pad_maximum_fusion.refs_0_), channel_id=1, source_target_pairs={{0,32},{1,97},{16,48},{17,113},{32,64},{33,1},{48,80},{49,17},{64,... | collective-permute-start | bytes 589832 | tf_op jit(solution)/shard_map/ppermute | solution.py:30
  38.8 5.6 %all-to-all-start.1 = ((bf16[8,64,768]{2,1,0:T(8,128)(2,1)}), bf16[8,64,768]{2,1,0:T(8,128)(2,1)S(1)}, u32[]{:S(2)}, u32[]{:S(2)}) async-start(bf16[8,64,768]{2,1,0:T(8,128)(2,1)} %broadcast_in_dim.12), calls=%async_computation.1 | async-start | bytes 1572864 | tf_op jit(solution)/shard_map/all_to_all | solution.py:191
  45.1 2.5 %collective-permute-start.8 = (bf16[128,768]{1,0:T(8,128)(2,1)S(1)}, bf16[128,768]{1,0:T(8,128)(2,1)}, u32[]{:S(2)}, u32[]{:S(2)}) collective-permute-start(bf16[128,768]{1,0:T(8,128)(2,1)S(1)} %collective-permute-done.4.refs_3_), channel_id=1, source_target_pairs={{0,32},{1,97},{16,48},{17,113},{32,64},{33,1},{48,80},{49,17},{64,... | collective-permute-start | bytes 589832 | tf_op jit(solution)/shard_map/ppermute | solution.py:30
  47.6 2.0 %collective-permute-start.7 = (bf16[128,768]{1,0:T(8,128)(2,1)S(1)}, bf16[128,768]{1,0:T(8,128)(2,1)}, u32[]{:S(2)}, u32[]{:S(2)}) collective-permute-start(bf16[128,768]{1,0:T(8,128)(2,1)S(1)} %collective-permute-done.5.refs_4_), channel_id=1, source_target_pairs={{0,112},{1,17},{16,0},{17,33},{32,16},{33,49},{48,32},{49,65},{64,... | collective-permute-start | bytes 589832 | tf_op jit(solution)/shard_map/ppermute | solution.py:30
  49.6 7.9 %all-to-all-done.1 = bf16[8,64,768]{2,1,0:T(8,128)(2,1)S(1)} async-done(((bf16[8,64,768]{2,1,0:T(8,128)(2,1)}), bf16[8,64,768]{2,1,0:T(8,128)(2,1)S(1)}, u32[]{:S(2)}, u32[]{:S(2)}) %all-to-all-start.1) | async-done | bytes 786464 | tf_op jit(solution)/shard_map/all_to_all | solution.py:191
  57.5 2.2 %collective-permute-done.9.refs_9_ = bf16[512,768]{1,0:T(8,128)(2,1)S(1)} collective-permute-done((bf16[512,768]{1,0:T(8,128)(2,1)S(1)}, bf16[512,768]{1,0:T(8,128)(2,1)S(1)}, u32[]{:S(2)}, u32[]{:S(2)}) %collective-permute-start.9) | collective-permute-done | bytes 786464 | tf_op jit(solution)/shard_map/ppermute | solution.py:23
  59.7 4.9 %shard_map.62 = (bf16[1024,768]{1,0:T(8,128)(2,1)S(1)}, bf16[768,768]{1,0:T(8,128)(2,1)S(1)}, f32[768,384]{1,0:T(8,128)S(1)}) custom-call(s32[25]{0:T(128)S(1)} %stack.103.place, bf16[128,768]{1,0:T(8,128)(2,1)S(1)} %pad_maximum_fusion.refs_0_, bf16[128,768]{1,0:T(8,128)(2,1)} %collective-permute-done.2.refs_1_, ...), custom_call_target="tpu_custom_call" | custom-call | flops 1660944384 | bytes 6291456 | tf_op jit(solution)/shard_map/pallas_call | solution.py:154
  65.0 2.7 %shard_map.63 = (f32[512,768]{1,0:T(8,128)}, f32[512,768]{1,0:T(8,128)S(1)}) custom-call(s32[25]{0:T(128)S(1)} %stack.103.place, bf16[1024,768]{1,0:T(8,128)(2,1)S(1)} %get-tuple-element.41.rows, bf16[768,768]{1,0:T(8,128)(2,1)S(1)} %get-tuple-element.39.amp), custom_call_target="tpu_custom_call" | custom-call | flops 1207959552 | bytes 6291456 | tf_op jit(solution)/shard_map/pallas_call | solution.py:154
  68.2 1.6 %shard_map.64 = f32[16,56,384]{2,1,0:T(8,128)S(1)} custom-call(s32[25]{0:T(128)S(1)} %stack.103.place, bf16[768,768]{1,0:T(8,128)(2,1)S(1)} %get-tuple-element.39.amp, f32[768,384]{1,0:T(8,128)S(1)} %collective-permute-done.10.got), custom_call_target="tpu_custom_call" | custom-call | flops 452984832 | bytes 6291456 | tf_op jit(solution)/shard_map/pallas_call | solution.py:154
  70.7 6.0 %all-to-all-start.2 = ((f16[16,56,384]{2,1,0:T(8,128)(2,1)}), f16[16,56,384]{2,1,0:T(8,128)(2,1)S(1)}, u32[]{:S(2)}, u32[]{:S(2)}) async-start(f16[16,56,384]{2,1,0:T(8,128)(2,1)} %convert_element_type.67), calls=%async_computation.2 | async-start | bytes 1376256 | tf_op jit(solution)/shard_map/all_to_all | solution.py:238
  76.8 1.4 %copy-done.2 = f32[512,768]{1,0:T(8,128)S(1)} copy-done((f32[512,768]{1,0:T(8,128)S(1)}, f32[512,768]{1,0:T(8,128)}, u32[]{:S(2)}) %copy-start.2) | copy-done | bytes 1572888
  78.2 2.6 %shard_map.65 = (f32[64,768]{1,0:T(8,128)S(1)}, f32[7,72,768]{2,1,0:T(8,128)S(1)}) custom-call(s32[25]{0:T(128)S(1)} %stack.103.place, f32[512,768]{1,0:T(8,128)S(1)} %copy-done.2, f32[512,768]{1,0:T(8,128)} %collective-permute-done.11.got), custom_call_target="tpu_custom_call" | custom-call | bytes 6291456 | tf_op jit(solution)/shard_map/pallas_call | solution.py:154
  81.6 2.9 %collective-permute-start.18 = (f16[72,768]{1,0:T(8,128)(2,1)S(1)}, f16[72,768]{1,0:T(8,128)(2,1)S(1)}, u32[]{:S(2)}, u32[]{:S(2)}) collective-permute-start(f16[72,768]{1,0:T(8,128)(2,1)S(1)} %get-tuple-element.66), channel_id=1, source_target_pairs={{0,14},{2,12},{4,2},{6,0},{8,6},{10,4},{12,10},{14,8},{1,15},{3,13... | collective-permute-start | bytes 331784 | tf_op jit(solution)/shard_map/ppermute | solution.py:35
  85.3 2.8 %collective-permute-start.16 = (f16[72,768]{1,0:T(8,128)(2,1)}, f16[72,768]{1,0:T(8,128)(2,1)}, u32[]{:S(2)}, u32[]{:S(2)}) collective-permute-start(f16[72,768]{1,0:T(8,128)(2,1)} %get-tuple-element.68), channel_id=1, source_target_pairs={{0,10},{2,8},{4,14},{6,12},{8,2},{10,0},{12,6},{14,4},{1,11},{3,9}... | collective-permute-start | bytes 331784 | tf_op jit(solution)/shard_map/ppermute | solution.py:35
  89.2 3.2 %collective-permute-start.14 = (f16[72,768]{1,0:T(8,128)(2,1)S(1)}, f16[72,768]{1,0:T(8,128)(2,1)}, u32[]{:S(2)}, u32[]{:S(2)}) collective-permute-start(f16[72,768]{1,0:T(8,128)(2,1)S(1)} %get-tuple-element.70), channel_id=1, source_target_pairs={{0,6},{2,4},{4,10},{6,8},{8,14},{10,12},{12,2},{14,0},{1,7},{3,5},... | collective-permute-start | bytes 331784 | tf_op jit(solution)/shard_map/ppermute | solution.py:35
  93.0 1.8 %collective-permute-start.12 = (f16[72,768]{1,0:T(8,128)(2,1)S(1)}, f16[72,768]{1,0:T(8,128)(2,1)}, u32[]{:S(2)}, u32[]{:S(2)}) collective-permute-start(f16[72,768]{1,0:T(8,128)(2,1)S(1)} %get-tuple-element.72), channel_id=1, source_target_pairs={{0,2},{2,0},{4,6},{6,4},{8,10},{10,8},{12,14},{14,12},{1,3},{3,1},... | collective-permute-start | bytes 331784 | tf_op jit(solution)/shard_map/ppermute | solution.py:35
  98.8 6.2 %all-to-all-start.3 = ((f32[16,3,384]{2,1,0:T(4,128)}), f32[16,3,384]{2,1,0:T(4,128)S(1)}, u32[]{:S(2)}, u32[]{:S(2)}) async-start(f32[16,3,384]{2,1,0:T(4,128)} %reshape.54), calls=%async_computation.3 | async-start | bytes 196608 | tf_op jit(solution)/shard_map/all_to_all | solution.py:256
  111.7 1.2 %all-to-all-done.3 = f32[16,3,384]{2,1,0:T(4,128)S(1)} async-done(((f32[16,3,384]{2,1,0:T(4,128)}), f32[16,3,384]{2,1,0:T(4,128)S(1)}, u32[]{:S(2)}, u32[]{:S(2)}) %all-to-all-start.3) | async-done | bytes 73760 | tf_op jit(solution)/shard_map/all_to_all | solution.py:256
  (81 shorter events, 24.3 us)
Async XLA Ops:
  0.6 24.1 %copy-start.8 = (f32[16]{0:T(128)S(1)}, f32[16]{0:T(128)}, u32[]{:S(2)}) copy-start(f32[16]{0:T(128)} %param.6) | copy-start | bytes 196
  4.4 23.3 %collective-permute-start.1 = (bf16[64,768]{1,0:T(8,128)(2,1)S(1)}, bf16[64,768]{1,0:T(8,128)(2,1)S(1)}, u32[]{:S(2)}, u32[]{:S(2)}) collective-permute-start(bf16[64,768]{1,0:T(8,128)(2,1)S(1)} %copy.17), channel_id=1, source_target_pairs={{0,128},{1,144},{2,160},{3,176},{4,192},{5,208},{6,224},{7,240},{8... | collective-permute-start | bytes 294920 | tf_op jit(solution)/shard_map/ppermute | solution.py:176
  4.9 22.7 %collective-permute-start = (bf16[64,768]{1,0:T(8,128)(2,1)S(1)}, bf16[64,768]{1,0:T(8,128)(2,1)S(1)}, u32[]{:S(2)}, u32[]{:S(2)}) collective-permute-start(bf16[64,768]{1,0:T(8,128)(2,1)S(1)} %copy.17), channel_id=1, source_target_pairs={{0,0},{1,16},{2,32},{3,48},{4,64},{5,80},{6,96},{7,112},{8,128},{9... | collective-permute-start | bytes 294920 | tf_op jit(solution)/shard_map/ppermute | solution.py:176
  9.8 22.7 %all-to-all-start = ((bf16[16,2,1536]{2,1,0:T(2,128)(2,1)}), bf16[16,2,1536]{2,1,0:T(2,128)(2,1)S(1)}, u32[]{:S(2)}, u32[]{:S(2)}) async-start(bf16[16,2,1536]{2,1,0:T(2,128)(2,1)} %reshape.57), calls=%async_computation | async-start | bytes 196608 | tf_op jit(solution)/shard_map/all_to_all | solution.py:186
  32.7 11.7 %collective-permute-start.5 = (bf16[128,768]{1,0:T(8,128)(2,1)S(1)}, bf16[128,768]{1,0:T(8,128)(2,1)S(1)}, u32[]{:S(2)}, u32[]{:S(2)}) collective-permute-start(bf16[128,768]{1,0:T(8,128)(2,1)S(1)} %pad_maximum_fusion.refs_0_), channel_id=1, source_target_pairs={{0,96},{1,33},{16,112},{17,49},{32,0},{33,65},{48,16},{49,81},{64,... | collective-permute-start | bytes 589832 | tf_op jit(solution)/shard_map/ppermute | solution.py:30
  34.4 10.6 %collective-permute-start.4 = (bf16[128,768]{1,0:T(8,128)(2,1)S(1)}, bf16[128,768]{1,0:T(8,128)(2,1)S(1)}, u32[]{:S(2)}, u32[]{:S(2)}) collective-permute-start(bf16[128,768]{1,0:T(8,128)(2,1)S(1)} %pad_maximum_fusion.refs_0_), channel_id=1, source_target_pairs={{0,32},{1,97},{16,48},{17,113},{32,64},{33,1},{48,80},{49,17},{64,... | collective-permute-start | bytes 589832 | tf_op jit(solution)/shard_map/ppermute | solution.py:30
  35.7 13.9 %collective-permute-start.3 = (bf16[128,768]{1,0:T(8,128)(2,1)S(1)}, bf16[128,768]{1,0:T(8,128)(2,1)}, u32[]{:S(2)}, u32[]{:S(2)}) collective-permute-start(bf16[128,768]{1,0:T(8,128)(2,1)S(1)} %pad_maximum_fusion.refs_0_), channel_id=1, source_target_pairs={{0,112},{1,17},{16,0},{17,33},{32,16},{33,49},{48,32},{49,65},{64,... | collective-permute-start | bytes 589832 | tf_op jit(solution)/shard_map/ppermute | solution.py:30
  36.6 20.8 %collective-permute-start.2 = (bf16[128,768]{1,0:T(8,128)(2,1)S(1)}, bf16[128,768]{1,0:T(8,128)(2,1)}, u32[]{:S(2)}, u32[]{:S(2)}) collective-permute-start(bf16[128,768]{1,0:T(8,128)(2,1)S(1)} %pad_maximum_fusion.refs_0_), channel_id=1, source_target_pairs={{0,16},{1,113},{16,32},{17,1},{32,48},{33,17},{48,64},{49,33},{64,... | collective-permute-start | bytes 589832 | tf_op jit(solution)/shard_map/ppermute | solution.py:30
  38.8 18.6 %all-to-all-start.1 = ((bf16[8,64,768]{2,1,0:T(8,128)(2,1)}), bf16[8,64,768]{2,1,0:T(8,128)(2,1)S(1)}, u32[]{:S(2)}, u32[]{:S(2)}) async-start(bf16[8,64,768]{2,1,0:T(8,128)(2,1)} %broadcast_in_dim.12), calls=%async_computation.1 | async-start | bytes 1572864 | tf_op jit(solution)/shard_map/all_to_all | solution.py:191
  45.1 12.4 %collective-permute-start.8 = (bf16[128,768]{1,0:T(8,128)(2,1)S(1)}, bf16[128,768]{1,0:T(8,128)(2,1)}, u32[]{:S(2)}, u32[]{:S(2)}) collective-permute-start(bf16[128,768]{1,0:T(8,128)(2,1)S(1)} %collective-permute-done.4.refs_3_), channel_id=1, source_target_pairs={{0,32},{1,97},{16,48},{17,113},{32,64},{33,1},{48,80},{49,17},{64,... | collective-permute-start | bytes 589832 | tf_op jit(solution)/shard_map/ppermute | solution.py:30
  47.5 9.9 %collective-permute-start.6 = (bf16[128,768]{1,0:T(8,128)(2,1)S(1)}, bf16[128,768]{1,0:T(8,128)(2,1)}, u32[]{:S(2)}, u32[]{:S(2)}) collective-permute-start(bf16[128,768]{1,0:T(8,128)(2,1)S(1)} %collective-permute-done.4.refs_3_), channel_id=1, source_target_pairs={{0,16},{1,113},{16,32},{17,1},{32,48},{33,17},{48,64},{49,33},{64,... | collective-permute-start | bytes 589832 | tf_op jit(solution)/shard_map/ppermute | solution.py:30
  47.6 9.9 %collective-permute-start.7 = (bf16[128,768]{1,0:T(8,128)(2,1)S(1)}, bf16[128,768]{1,0:T(8,128)(2,1)}, u32[]{:S(2)}, u32[]{:S(2)}) collective-permute-start(bf16[128,768]{1,0:T(8,128)(2,1)S(1)} %collective-permute-done.5.refs_4_), channel_id=1, source_target_pairs={{0,112},{1,17},{16,0},{17,33},{32,16},{33,49},{48,32},{49,65},{64,... | collective-permute-start | bytes 589832 | tf_op jit(solution)/shard_map/ppermute | solution.py:30
  57.4 2.3 %collective-permute-start.9 = (bf16[512,768]{1,0:T(8,128)(2,1)S(1)}, bf16[512,768]{1,0:T(8,128)(2,1)S(1)}, u32[]{:S(2)}, u32[]{:S(2)}) collective-permute-start(bf16[512,768]{1,0:T(8,128)(2,1)S(1)} %bitcast.63), channel_id=1, source_target_pairs={{0,1},{1,0},{2,3},{3,2},{4,5},{5,4},{6,7},{7,6},{8,9},{9,8},{10,11... | collective-permute-start | bytes 2359304 | tf_op jit(solution)/shard_map/ppermute | solution.py:23
  64.6 3.1 %collective-permute-start.10 = (f32[768,384]{1,0:T(8,128)S(1)}, f32[768,384]{1,0:T(8,128)S(1)}, u32[]{:S(2)}, u32[]{:S(2)}) collective-permute-start(f32[768,384]{1,0:T(8,128)S(1)} %get-tuple-element.40), channel_id=1, source_target_pairs={{0,1},{1,0},{2,3},{3,2},{4,5},{5,4},{6,7},{7,6},{8,9},{9,8},{10,11... | collective-permute-start | bytes 3538952 | tf_op jit(solution)/shard_map/ppermute | solution.py:23
  67.8 9.0 %collective-permute-start.11 = (f32[512,768]{1,0:T(8,128)}, f32[512,768]{1,0:T(8,128)}, u32[]{:S(2)}, u32[]{:S(2)}) collective-permute-start(f32[512,768]{1,0:T(8,128)} %get-tuple-element.46), channel_id=1, source_target_pairs={{0,1},{1,0},{2,3},{3,2},{4,5},{5,4},{6,7},{7,6},{8,9},{9,8},{10,11... | collective-permute-start | bytes 4718600 | tf_op jit(solution)/shard_map/ppermute | solution.py:23
  70.7 25.0 %all-to-all-start.2 = ((f16[16,56,384]{2,1,0:T(8,128)(2,1)}), f16[16,56,384]{2,1,0:T(8,128)(2,1)S(1)}, u32[]{:S(2)}, u32[]{:S(2)}) async-start(f16[16,56,384]{2,1,0:T(8,128)(2,1)} %convert_element_type.67), calls=%async_computation.2 | async-start | bytes 1376256 | tf_op jit(solution)/shard_map/all_to_all | solution.py:238
  81.6 10.8 %collective-permute-start.18 = (f16[72,768]{1,0:T(8,128)(2,1)S(1)}, f16[72,768]{1,0:T(8,128)(2,1)S(1)}, u32[]{:S(2)}, u32[]{:S(2)}) collective-permute-start(f16[72,768]{1,0:T(8,128)(2,1)S(1)} %get-tuple-element.66), channel_id=1, source_target_pairs={{0,14},{2,12},{4,2},{6,0},{8,6},{10,4},{12,10},{14,8},{1,15},{3,13... | collective-permute-start | bytes 331784 | tf_op jit(solution)/shard_map/ppermute | solution.py:35
  84.4 8.0 %collective-permute-start.17 = (f16[72,768]{1,0:T(8,128)(2,1)S(1)}, f16[72,768]{1,0:T(8,128)(2,1)}, u32[]{:S(2)}, u32[]{:S(2)}) collective-permute-start(f16[72,768]{1,0:T(8,128)(2,1)S(1)} %get-tuple-element.67), channel_id=1, source_target_pairs={{0,12},{2,14},{4,0},{6,2},{8,4},{10,6},{12,8},{14,10},{1,13},{3,15... | collective-permute-start | bytes 331784 | tf_op jit(solution)/shard_map/ppermute | solution.py:35
  85.3 11.6 %collective-permute-start.16 = (f16[72,768]{1,0:T(8,128)(2,1)}, f16[72,768]{1,0:T(8,128)(2,1)}, u32[]{:S(2)}, u32[]{:S(2)}) collective-permute-start(f16[72,768]{1,0:T(8,128)(2,1)} %get-tuple-element.68), channel_id=1, source_target_pairs={{0,10},{2,8},{4,14},{6,12},{8,2},{10,0},{12,6},{14,4},{1,11},{3,9}... | collective-permute-start | bytes 331784 | tf_op jit(solution)/shard_map/ppermute | solution.py:35
  88.1 9.8 %collective-permute-start.15 = (f16[72,768]{1,0:T(8,128)(2,1)S(1)}, f16[72,768]{1,0:T(8,128)(2,1)}, u32[]{:S(2)}, u32[]{:S(2)}) collective-permute-start(f16[72,768]{1,0:T(8,128)(2,1)S(1)} %get-tuple-element.69), channel_id=1, source_target_pairs={{0,8},{2,10},{4,12},{6,14},{8,0},{10,2},{12,4},{14,6},{1,9},{3,11}... | collective-permute-start | bytes 331784 | tf_op jit(solution)/shard_map/ppermute | solution.py:35
  89.2 18.6 %collective-permute-start.14 = (f16[72,768]{1,0:T(8,128)(2,1)S(1)}, f16[72,768]{1,0:T(8,128)(2,1)}, u32[]{:S(2)}, u32[]{:S(2)}) collective-permute-start(f16[72,768]{1,0:T(8,128)(2,1)S(1)} %get-tuple-element.70), channel_id=1, source_target_pairs={{0,6},{2,4},{4,10},{6,8},{8,14},{10,12},{12,2},{14,0},{1,7},{3,5},... | collective-permute-start | bytes 331784 | tf_op jit(solution)/shard_map/ppermute | solution.py:35
  92.4 16.4 %collective-permute-start.13 = (f16[72,768]{1,0:T(8,128)(2,1)S(1)}, f16[72,768]{1,0:T(8,128)(2,1)}, u32[]{:S(2)}, u32[]{:S(2)}) collective-permute-start(f16[72,768]{1,0:T(8,128)(2,1)S(1)} %get-tuple-element.71), channel_id=1, source_target_pairs={{0,4},{2,6},{4,8},{6,10},{8,12},{10,14},{12,0},{14,2},{1,5},{3,7},... | collective-permute-start | bytes 331784 | tf_op jit(solution)/shard_map/ppermute | solution.py:35
  93.0 16.7 %collective-permute-start.12 = (f16[72,768]{1,0:T(8,128)(2,1)S(1)}, f16[72,768]{1,0:T(8,128)(2,1)}, u32[]{:S(2)}, u32[]{:S(2)}) collective-permute-start(f16[72,768]{1,0:T(8,128)(2,1)S(1)} %get-tuple-element.72), channel_id=1, source_target_pairs={{0,2},{2,0},{4,6},{6,4},{8,10},{10,8},{12,14},{14,12},{1,3},{3,1},... | collective-permute-start | bytes 331784 | tf_op jit(solution)/shard_map/ppermute | solution.py:35
  98.8 14.1 %all-to-all-start.3 = ((f32[16,3,384]{2,1,0:T(4,128)}), f32[16,3,384]{2,1,0:T(4,128)S(1)}, u32[]{:S(2)}, u32[]{:S(2)}) async-start(f32[16,3,384]{2,1,0:T(4,128)} %reshape.54), calls=%async_computation.3 | async-start | bytes 196608 | tf_op jit(solution)/shard_map/all_to_all | solution.py:256
  (8 other events, 42.3 us)

commit v7 on v6

--- a/solution.py
+++ b/solution.py
@@ -31,12 +31,12 @@
 
 
 def next_chip(array, hop):
-    pairs = [(q, hop_from(q, hop)) for q in range(Y * XH)]
-    return lax.ppermute(array, CHIPS, pairs)
-
-
-def hop_from(q, hop):
-    return (q // XH + hop // XH) % Y * XH + (q + hop) % XH
+    pairs = [(q * C + c, hop_from(q, hop, c) * C + c) for q in range(Y * XH) for c in range(C)]
+    return lax.ppermute(array, AUX, pairs)
+
+
+def hop_from(q, hop, c):
+    return (q // XH + (1 - 2 * c) * (hop // XH)) % Y * XH + (q + hop) % XH
 
 
 def paced(array, us):
@@ -203,7 +203,7 @@
         at = (z + (1 - 2 * c) * step) % Z
         owners += [xl * Z + at, (1 - xl) * Z + at]
     places = [o % C * HALF_P + o // C * PW for o in owners]
-    places += [hop_from(chip, hop) * PW for hop in range(Y * XH)] + [c]
+    places += [hop_from(chip, hop, c) * PW for hop in range(Y * XH)] + [c]
     place = jnp.stack(places).astype(jnp.int32)
 
     bf16, f32 = jnp.bfloat16, jnp.float32

time: 115 us -> 114 us (level)
  transfers between devices with their start and end apart: 23 -> 23, of which waited for: 8 -> 7; matrix products, arithmetic and copies ran while one was open for 11% -> 11% of each run, Pallas kernels for 6% -> 6%
where the time goes in v7:
time: 114 us; the launch traced here: 112 us
  starting transfers between devices  59.9 us (53%)
  waiting for transfers between devices  18.8 us (16%)
  Pallas kernels  11.9 us (10%)
  local copies, waits for them, and re-layouts  9.87 us (9%)
  other arithmetic  8.12 us (7%)
  matrix products  2 us (2%)
  between operations  1.43 us (1%)
    all_to_all x1, starting transfers between devices, per_device(): local = lax.all_to_all(native, OCC, split_axis=0, concat_axis=0, tiled=True)  14.9 us
    ppermute x7, starting transfers between devices, next_chip(): return lax.ppermute(array, AUX, pairs)  12.7 us
    pallas_call x5, Pallas kernels, call(): pl.pallas_call(kernel, out_shape=[jax.ShapeDtypeStruct(s, t) for s, t in...  11.9 us
    ppermute x7, starting transfers between devices, ring(): return lax.ppermute(array, ('z', 'c'), pairs)  9.54 us
    all_to_all x1, waiting for transfers between devices, per_device(): lax.all_to_all(jnp.broadcast_to(local, (Y * XH, PW, NV)), CHIPS, split_ax...  7.85 us
    unnamed x22, local copies, waits for them, and re-layouts  6.24 us
    all_to_all x1, starting transfers between devices, per_device(): met = lax.all_to_all(packed, OCC, split_axis=0, concat_axis=0, tiled=True)  6.03 us
    all_to_all x1, starting transfers between devices, per_device(): vir = lax.all_to_all(vir, AUX, split_axis=0, concat_axis=0, tiled=True)  5.76 us
  transfers between devices with their start and end apart: 23, of which 7 were waited for; matrix products, arithmetic and copies ran while one was open for 11% of the time, Pallas kernels for 6%

profile of v7, /device:TPU:32, one launch (start us, length us, event | category | flops | bytes accessed | tf_op | source)
XLA Modules:
  0.0 112.0 jit_solution(14420889415995959953)
XLA Ops:
  0.7 1.6 %copy-done = bf16[16,64,1024]{2,1,0:T(8,128)(2,1)S(1)} copy-done((bf16[16,64,1024]{2,1,0:T(8,128)(2,1)S(1)}, bf16[16,64,1024]{2,1,0:T(8,128)(2,1)}, u32[]{:S(2)}) %copy-start) | copy-done | bytes 2097176
  2.2 2.0 %convolution_convert_fusion = bf16[16,64,48]{1,2,0:T(8,128)(2,1)S(1)} fusion(bf16[16,64,1024]{2,1,0:T(8,128)(2,1)S(1)} %copy-done, bf16[1024,48]{0,1:T(8,128)(2,1)} %param.5), kind=kOutput, calls=%fused_computation.1 | convolution fusion | flops 100712448 | bytes 2293760 | tf_op jit(solution)/shard_map/ipm,ma->ipa/dot_general | solution.py:169
  4.9 4.1 %collective-permute-start = (bf16[64,768]{1,0:T(8,128)(2,1)S(1)}, bf16[64,768]{1,0:T(8,128)(2,1)S(1)}, u32[]{:S(2)}, u32[]{:S(2)}) collective-permute-start(bf16[64,768]{1,0:T(8,128)(2,1)S(1)} %copy.17), channel_id=1, source_target_pairs={{0,0},{1,16},{2,32},{3,48},{4,64},{5,80},{6,96},{7,112},{8,128},{9... | collective-permute-start | bytes 294920 | tf_op jit(solution)/shard_map/ppermute | solution.py:176
  9.8 14.9 %all-to-all-start = ((bf16[16,2,1536]{2,1,0:T(2,128)(2,1)}), bf16[16,2,1536]{2,1,0:T(2,128)(2,1)S(1)}, u32[]{:S(2)}, u32[]{:S(2)}) async-start(bf16[16,2,1536]{2,1,0:T(2,128)(2,1)} %reshape.57), calls=%async_computation | async-start | bytes 196608 | tf_op jit(solution)/shard_map/all_to_all | solution.py:186
  27.7 4.8 %all-to-all-done = bf16[16,2,1536]{2,1,0:T(2,128)(2,1)S(1)} async-done(((bf16[16,2,1536]{2,1,0:T(2,128)(2,1)}), bf16[16,2,1536]{2,1,0:T(2,128)(2,1)S(1)}, u32[]{:S(2)}, u32[]{:S(2)}) %all-to-all-start) | async-done | bytes 98336 | tf_op jit(solution)/shard_map/all_to_all | solution.py:186
  32.7 1.7 %collective-permute-start.5 = (bf16[128,768]{1,0:T(8,128)(2,1)S(1)}, bf16[128,768]{1,0:T(8,128)(2,1)S(1)}, u32[]{:S(2)}, u32[]{:S(2)}) collective-permute-start(bf16[128,768]{1,0:T(8,128)(2,1)S(1)} %pad_maximum_fusion.refs_0_), channel_id=1, source_target_pairs={{0,96},{1,33},{16,112},{17,49},{32,0},{33,65},{48,16},{49,81},{64,... | collective-permute-start | bytes 589832 | tf_op jit(solution)/shard_map/ppermute | solution.py:30
  34.4 1.3 %collective-permute-start.4 = (bf16[128,768]{1,0:T(8,128)(2,1)S(1)}, bf16[128,768]{1,0:T(8,128)(2,1)S(1)}, u32[]{:S(2)}, u32[]{:S(2)}) collective-permute-start(bf16[128,768]{1,0:T(8,128)(2,1)S(1)} %pad_maximum_fusion.refs_0_), channel_id=1, source_target_pairs={{0,32},{1,97},{16,48},{17,113},{32,64},{33,1},{48,80},{49,17},{64,... | collective-permute-start | bytes 589832 | tf_op jit(solution)/shard_map/ppermute | solution.py:30
  38.8 5.6 %all-to-all-start.1 = ((bf16[8,64,768]{2,1,0:T(8,128)(2,1)}), bf16[8,64,768]{2,1,0:T(8,128)(2,1)S(1)}, u32[]{:S(2)}, u32[]{:S(2)}) async-start(bf16[8,64,768]{2,1,0:T(8,128)(2,1)} %broadcast_in_dim.12), calls=%async_computation.1 | async-start | bytes 1572864 | tf_op jit(solution)/shard_map/all_to_all | solution.py:191
  45.1 2.5 %collective-permute-start.8 = (bf16[128,768]{1,0:T(8,128)(2,1)S(1)}, bf16[128,768]{1,0:T(8,128)(2,1)}, u32[]{:S(2)}, u32[]{:S(2)}) collective-permute-start(bf16[128,768]{1,0:T(8,128)(2,1)S(1)} %collective-permute-done.4.refs_3_), channel_id=1, source_target_pairs={{0,32},{1,97},{16,48},{17,113},{32,64},{33,1},{48,80},{49,17},{64,... | collective-permute-start | bytes 589832 | tf_op jit(solution)/shard_map/ppermute | solution.py:30
  47.6 2.0 %collective-permute-start.7 = (bf16[128,768]{1,0:T(8,128)(2,1)S(1)}, bf16[128,768]{1,0:T(8,128)(2,1)}, u32[]{:S(2)}, u32[]{:S(2)}) collective-permute-start(bf16[128,768]{1,0:T(8,128)(2,1)S(1)} %collective-permute-done.5.refs_4_), channel_id=1, source_target_pairs={{0,112},{1,17},{16,0},{17,33},{32,16},{33,49},{48,32},{49,65},{64,... | collective-permute-start | bytes 589832 | tf_op jit(solution)/shard_map/ppermute | solution.py:30
  49.6 7.9 %all-to-all-done.1 = bf16[8,64,768]{2,1,0:T(8,128)(2,1)S(1)} async-done(((bf16[8,64,768]{2,1,0:T(8,128)(2,1)}), bf16[8,64,768]{2,1,0:T(8,128)(2,1)S(1)}, u32[]{:S(2)}, u32[]{:S(2)}) %all-to-all-start.1) | async-done | bytes 786464 | tf_op jit(solution)/shard_map/all_to_all | solution.py:191
  57.5 2.2 %collective-permute-done.9.refs_9_ = bf16[512,768]{1,0:T(8,128)(2,1)S(1)} collective-permute-done((bf16[512,768]{1,0:T(8,128)(2,1)S(1)}, bf16[512,768]{1,0:T(8,128)(2,1)S(1)}, u32[]{:S(2)}, u32[]{:S(2)}) %collective-permute-start.9) | collective-permute-done | bytes 786464 | tf_op jit(solution)/shard_map/ppermute | solution.py:23
  59.7 4.9 %shard_map.62 = (bf16[1024,768]{1,0:T(8,128)(2,1)S(1)}, bf16[768,768]{1,0:T(8,128)(2,1)S(1)}, f32[768,384]{1,0:T(8,128)S(1)}) custom-call(s32[25]{0:T(128)S(1)} %stack.103.place, bf16[128,768]{1,0:T(8,128)(2,1)S(1)} %pad_maximum_fusion.refs_0_, bf16[128,768]{1,0:T(8,128)(2,1)} %collective-permute-done.2.refs_1_, ...), custom_call_target="tpu_custom_call" | custom-call | flops 1660944384 | bytes 6291456 | tf_op jit(solution)/shard_map/pallas_call | solution.py:154
  65.0 2.7 %shard_map.63 = (f32[512,768]{1,0:T(8,128)}, f32[512,768]{1,0:T(8,128)S(1)}) custom-call(s32[25]{0:T(128)S(1)} %stack.103.place, bf16[1024,768]{1,0:T(8,128)(2,1)S(1)} %get-tuple-element.41.rows, bf16[768,768]{1,0:T(8,128)(2,1)S(1)} %get-tuple-element.39.amp), custom_call_target="tpu_custom_call" | custom-call | flops 1207959552 | bytes 6291456 | tf_op jit(solution)/shard_map/pallas_call | solution.py:154
  68.2 1.6 %shard_map.64 = f32[16,56,384]{2,1,0:T(8,128)S(1)} custom-call(s32[25]{0:T(128)S(1)} %stack.103.place, bf16[768,768]{1,0:T(8,128)(2,1)S(1)} %get-tuple-element.39.amp, f32[768,384]{1,0:T(8,128)S(1)} %collective-permute-done.10.got), custom_call_target="tpu_custom_call" | custom-call | flops 452984832 | bytes 6291456 | tf_op jit(solution)/shard_map/pallas_call | solution.py:154
  70.7 6.0 %all-to-all-start.2 = ((f16[16,56,384]{2,1,0:T(8,128)(2,1)}), f16[16,56,384]{2,1,0:T(8,128)(2,1)S(1)}, u32[]{:S(2)}, u32[]{:S(2)}) async-start(f16[16,56,384]{2,1,0:T(8,128)(2,1)} %convert_element_type.67), calls=%async_computation.2 | async-start | bytes 1376256 | tf_op jit(solution)/shard_map/all_to_all | solution.py:238
  76.8 1.4 %copy-done.2 = f32[512,768]{1,0:T(8,128)S(1)} copy-done((f32[512,768]{1,0:T(8,128)S(1)}, f32[512,768]{1,0:T(8,128)}, u32[]{:S(2)}) %copy-start.2) | copy-done | bytes 1572888
  78.2 2.6 %shard_map.65 = (f32[64,768]{1,0:T(8,128)S(1)}, f32[7,72,768]{2,1,0:T(8,128)S(1)}) custom-call(s32[25]{0:T(128)S(1)} %stack.103.place, f32[512,768]{1,0:T(8,128)S(1)} %copy-done.2, f32[512,768]{1,0:T(8,128)} %collective-permute-done.11.got), custom_call_target="tpu_custom_call" | custom-call | bytes 6291456 | tf_op jit(solution)/shard_map/pallas_call | solution.py:154
  81.6 2.9 %collective-permute-start.18 = (f16[72,768]{1,0:T(8,128)(2,1)S(1)}, f16[72,768]{1,0:T(8,128)(2,1)S(1)}, u32[]{:S(2)}, u32[]{:S(2)}) collective-permute-start(f16[72,768]{1,0:T(8,128)(2,1)S(1)} %get-tuple-element.66), channel_id=1, source_target_pairs={{0,14},{1,7},{2,12},{3,5},{4,2},{5,11},{6,0},{7,9},{8,6},{9,15},{1... | collective-permute-start | bytes 331784 | tf_op jit(solution)/shard_map/ppermute | solution.py:35
  85.3 2.8 %collective-permute-start.16 = (f16[72,768]{1,0:T(8,128)(2,1)}, f16[72,768]{1,0:T(8,128)(2,1)}, u32[]{:S(2)}, u32[]{:S(2)}) collective-permute-start(f16[72,768]{1,0:T(8,128)(2,1)} %get-tuple-element.68), channel_id=1, source_target_pairs={{0,10},{1,11},{2,8},{3,9},{4,14},{5,15},{6,12},{7,13},{8,2},{9,3},... | collective-permute-start | bytes 331784 | tf_op jit(solution)/shard_map/ppermute | solution.py:35
  89.2 3.2 %collective-permute-start.14 = (f16[72,768]{1,0:T(8,128)(2,1)S(1)}, f16[72,768]{1,0:T(8,128)(2,1)}, u32[]{:S(2)}, u32[]{:S(2)}) collective-permute-start(f16[72,768]{1,0:T(8,128)(2,1)S(1)} %get-tuple-element.70), channel_id=1, source_target_pairs={{0,6},{1,15},{2,4},{3,13},{4,10},{5,3},{6,8},{7,1},{8,14},{9,7},{1... | collective-permute-start | bytes 331784 | tf_op jit(solution)/shard_map/ppermute | solution.py:35
  93.0 1.9 %collective-permute-start.12 = (f16[72,768]{1,0:T(8,128)(2,1)S(1)}, f16[72,768]{1,0:T(8,128)(2,1)}, u32[]{:S(2)}, u32[]{:S(2)}) collective-permute-start(f16[72,768]{1,0:T(8,128)(2,1)S(1)} %get-tuple-element.72), channel_id=1, source_target_pairs={{0,2},{1,3},{2,0},{3,1},{4,6},{5,7},{6,4},{7,5},{8,10},{9,11},{10,... | collective-permute-start | bytes 331784 | tf_op jit(solution)/shard_map/ppermute | solution.py:35
  97.8 5.8 %all-to-all-start.3 = ((f32[16,3,384]{2,1,0:T(4,128)}), f32[16,3,384]{2,1,0:T(4,128)S(1)}, u32[]{:S(2)}, u32[]{:S(2)}) async-start(f32[16,3,384]{2,1,0:T(4,128)} %reshape.54), calls=%async_computation.3 | async-start | bytes 196608 | tf_op jit(solution)/shard_map/all_to_all | solution.py:256
  110.1 1.2 %all-to-all-done.3 = f32[16,3,384]{2,1,0:T(4,128)S(1)} async-done(((f32[16,3,384]{2,1,0:T(4,128)}), f32[16,3,384]{2,1,0:T(4,128)S(1)}, u32[]{:S(2)}, u32[]{:S(2)}) %all-to-all-start.3) | async-done | bytes 73760 | tf_op jit(solution)/shard_map/all_to_all | solution.py:256
  (81 shorter events, 23.2 us)
Async XLA Ops:
  0.6 24.1 %copy-start.8 = (f32[16]{0:T(128)S(1)}, f32[16]{0:T(128)}, u32[]{:S(2)}) copy-start(f32[16]{0:T(128)} %param.6) | copy-start | bytes 196
  4.4 23.3 %collective-permute-start.1 = (bf16[64,768]{1,0:T(8,128)(2,1)S(1)}, bf16[64,768]{1,0:T(8,128)(2,1)S(1)}, u32[]{:S(2)}, u32[]{:S(2)}) collective-permute-start(bf16[64,768]{1,0:T(8,128)(2,1)S(1)} %copy.17), channel_id=1, source_target_pairs={{0,128},{1,144},{2,160},{3,176},{4,192},{5,208},{6,224},{7,240},{8... | collective-permute-start | bytes 294920 | tf_op jit(solution)/shard_map/ppermute | solution.py:176
  4.9 22.7 %collective-permute-start = (bf16[64,768]{1,0:T(8,128)(2,1)S(1)}, bf16[64,768]{1,0:T(8,128)(2,1)S(1)}, u32[]{:S(2)}, u32[]{:S(2)}) collective-permute-start(bf16[64,768]{1,0:T(8,128)(2,1)S(1)} %copy.17), channel_id=1, source_target_pairs={{0,0},{1,16},{2,32},{3,48},{4,64},{5,80},{6,96},{7,112},{8,128},{9... | collective-permute-start | bytes 294920 | tf_op jit(solution)/shard_map/ppermute | solution.py:176
  9.8 22.7 %all-to-all-start = ((bf16[16,2,1536]{2,1,0:T(2,128)(2,1)}), bf16[16,2,1536]{2,1,0:T(2,128)(2,1)S(1)}, u32[]{:S(2)}, u32[]{:S(2)}) async-start(bf16[16,2,1536]{2,1,0:T(2,128)(2,1)} %reshape.57), calls=%async_computation | async-start | bytes 196608 | tf_op jit(solution)/shard_map/all_to_all | solution.py:186
  32.7 11.7 %collective-permute-start.5 = (bf16[128,768]{1,0:T(8,128)(2,1)S(1)}, bf16[128,768]{1,0:T(8,128)(2,1)S(1)}, u32[]{:S(2)}, u32[]{:S(2)}) collective-permute-start(bf16[128,768]{1,0:T(8,128)(2,1)S(1)} %pad_maximum_fusion.refs_0_), channel_id=1, source_target_pairs={{0,96},{1,33},{16,112},{17,49},{32,0},{33,65},{48,16},{49,81},{64,... | collective-permute-start | bytes 589832 | tf_op jit(solution)/shard_map/ppermute | solution.py:30
  34.4 10.6 %collective-permute-start.4 = (bf16[128,768]{1,0:T(8,128)(2,1)S(1)}, bf16[128,768]{1,0:T(8,128)(2,1)S(1)}, u32[]{:S(2)}, u32[]{:S(2)}) collective-permute-start(bf16[128,768]{1,0:T(8,128)(2,1)S(1)} %pad_maximum_fusion.refs_0_), channel_id=1, source_target_pairs={{0,32},{1,97},{16,48},{17,113},{32,64},{33,1},{48,80},{49,17},{64,... | collective-permute-start | bytes 589832 | tf_op jit(solution)/shard_map/ppermute | solution.py:30
  35.7 13.9 %collective-permute-start.3 = (bf16[128,768]{1,0:T(8,128)(2,1)S(1)}, bf16[128,768]{1,0:T(8,128)(2,1)}, u32[]{:S(2)}, u32[]{:S(2)}) collective-permute-start(bf16[128,768]{1,0:T(8,128)(2,1)S(1)} %pad_maximum_fusion.refs_0_), channel_id=1, source_target_pairs={{0,112},{1,17},{16,0},{17,33},{32,16},{33,49},{48,32},{49,65},{64,... | collective-permute-start | bytes 589832 | tf_op jit(solution)/shard_map/ppermute | solution.py:30
  36.6 20.8 %collective-permute-start.2 = (bf16[128,768]{1,0:T(8,128)(2,1)S(1)}, bf16[128,768]{1,0:T(8,128)(2,1)}, u32[]{:S(2)}, u32[]{:S(2)}) collective-permute-start(bf16[128,768]{1,0:T(8,128)(2,1)S(1)} %pad_maximum_fusion.refs_0_), channel_id=1, source_target_pairs={{0,16},{1,113},{16,32},{17,1},{32,48},{33,17},{48,64},{49,33},{64,... | collective-permute-start | bytes 589832 | tf_op jit(solution)/shard_map/ppermute | solution.py:30
  38.8 18.6 %all-to-all-start.1 = ((bf16[8,64,768]{2,1,0:T(8,128)(2,1)}), bf16[8,64,768]{2,1,0:T(8,128)(2,1)S(1)}, u32[]{:S(2)}, u32[]{:S(2)}) async-start(bf16[8,64,768]{2,1,0:T(8,128)(2,1)} %broadcast_in_dim.12), calls=%async_computation.1 | async-start | bytes 1572864 | tf_op jit(solution)/shard_map/all_to_all | solution.py:191
  45.1 12.4 %collective-permute-start.8 = (bf16[128,768]{1,0:T(8,128)(2,1)S(1)}, bf16[128,768]{1,0:T(8,128)(2,1)}, u32[]{:S(2)}, u32[]{:S(2)}) collective-permute-start(bf16[128,768]{1,0:T(8,128)(2,1)S(1)} %collective-permute-done.4.refs_3_), channel_id=1, source_target_pairs={{0,32},{1,97},{16,48},{17,113},{32,64},{33,1},{48,80},{49,17},{64,... | collective-permute-start | bytes 589832 | tf_op jit(solution)/shard_map/ppermute | solution.py:30
  47.5 9.9 %collective-permute-start.6 = (bf16[128,768]{1,0:T(8,128)(2,1)S(1)}, bf16[128,768]{1,0:T(8,128)(2,1)}, u32[]{:S(2)}, u32[]{:S(2)}) collective-permute-start(bf16[128,768]{1,0:T(8,128)(2,1)S(1)} %collective-permute-done.4.refs_3_), channel_id=1, source_target_pairs={{0,16},{1,113},{16,32},{17,1},{32,48},{33,17},{48,64},{49,33},{64,... | collective-permute-start | bytes 589832 | tf_op jit(solution)/shard_map/ppermute | solution.py:30
  47.6 9.9 %collective-permute-start.7 = (bf16[128,768]{1,0:T(8,128)(2,1)S(1)}, bf16[128,768]{1,0:T(8,128)(2,1)}, u32[]{:S(2)}, u32[]{:S(2)}) collective-permute-start(bf16[128,768]{1,0:T(8,128)(2,1)S(1)} %collective-permute-done.5.refs_4_), channel_id=1, source_target_pairs={{0,112},{1,17},{16,0},{17,33},{32,16},{33,49},{48,32},{49,65},{64,... | collective-permute-start | bytes 589832 | tf_op jit(solution)/shard_map/ppermute | solution.py:30
  57.4 2.3 %collective-permute-start.9 = (bf16[512,768]{1,0:T(8,128)(2,1)S(1)}, bf16[512,768]{1,0:T(8,128)(2,1)S(1)}, u32[]{:S(2)}, u32[]{:S(2)}) collective-permute-start(bf16[512,768]{1,0:T(8,128)(2,1)S(1)} %bitcast.63), channel_id=1, source_target_pairs={{0,1},{1,0},{2,3},{3,2},{4,5},{5,4},{6,7},{7,6},{8,9},{9,8},{10,11... | collective-permute-start | bytes 2359304 | tf_op jit(solution)/shard_map/ppermute | solution.py:23
  64.6 3.1 %collective-permute-start.10 = (f32[768,384]{1,0:T(8,128)S(1)}, f32[768,384]{1,0:T(8,128)S(1)}, u32[]{:S(2)}, u32[]{:S(2)}) collective-permute-start(f32[768,384]{1,0:T(8,128)S(1)} %get-tuple-element.40), channel_id=1, source_target_pairs={{0,1},{1,0},{2,3},{3,2},{4,5},{5,4},{6,7},{7,6},{8,9},{9,8},{10,11... | collective-permute-start | bytes 3538952 | tf_op jit(solution)/shard_map/ppermute | solution.py:23
  67.8 9.0 %collective-permute-start.11 = (f32[512,768]{1,0:T(8,128)}, f32[512,768]{1,0:T(8,128)}, u32[]{:S(2)}, u32[]{:S(2)}) collective-permute-start(f32[512,768]{1,0:T(8,128)} %get-tuple-element.46), channel_id=1, source_target_pairs={{0,1},{1,0},{2,3},{3,2},{4,5},{5,4},{6,7},{7,6},{8,9},{9,8},{10,11... | collective-permute-start | bytes 4718600 | tf_op jit(solution)/shard_map/ppermute | solution.py:23
  70.7 25.0 %all-to-all-start.2 = ((f16[16,56,384]{2,1,0:T(8,128)(2,1)}), f16[16,56,384]{2,1,0:T(8,128)(2,1)S(1)}, u32[]{:S(2)}, u32[]{:S(2)}) async-start(f16[16,56,384]{2,1,0:T(8,128)(2,1)} %convert_element_type.67), calls=%async_computation.2 | async-start | bytes 1376256 | tf_op jit(solution)/shard_map/all_to_all | solution.py:238
  81.6 10.8 %collective-permute-start.18 = (f16[72,768]{1,0:T(8,128)(2,1)S(1)}, f16[72,768]{1,0:T(8,128)(2,1)S(1)}, u32[]{:S(2)}, u32[]{:S(2)}) collective-permute-start(f16[72,768]{1,0:T(8,128)(2,1)S(1)} %get-tuple-element.66), channel_id=1, source_target_pairs={{0,14},{1,7},{2,12},{3,5},{4,2},{5,11},{6,0},{7,9},{8,6},{9,15},{1... | collective-permute-start | bytes 331784 | tf_op jit(solution)/shard_map/ppermute | solution.py:35
  84.4 8.0 %collective-permute-start.17 = (f16[72,768]{1,0:T(8,128)(2,1)S(1)}, f16[72,768]{1,0:T(8,128)(2,1)}, u32[]{:S(2)}, u32[]{:S(2)}) collective-permute-start(f16[72,768]{1,0:T(8,128)(2,1)S(1)} %get-tuple-element.67), channel_id=1, source_target_pairs={{0,12},{1,5},{2,14},{3,7},{4,0},{5,9},{6,2},{7,11},{8,4},{9,13},{1... | collective-permute-start | bytes 331784 | tf_op jit(solution)/shard_map/ppermute | solution.py:35
  85.3 11.6 %collective-permute-start.16 = (f16[72,768]{1,0:T(8,128)(2,1)}, f16[72,768]{1,0:T(8,128)(2,1)}, u32[]{:S(2)}, u32[]{:S(2)}) collective-permute-start(f16[72,768]{1,0:T(8,128)(2,1)} %get-tuple-element.68), channel_id=1, source_target_pairs={{0,10},{1,11},{2,8},{3,9},{4,14},{5,15},{6,12},{7,13},{8,2},{9,3},... | collective-permute-start | bytes 331784 | tf_op jit(solution)/shard_map/ppermute | solution.py:35
  88.1 8.8 %collective-permute-start.15 = (f16[72,768]{1,0:T(8,128)(2,1)S(1)}, f16[72,768]{1,0:T(8,128)(2,1)}, u32[]{:S(2)}, u32[]{:S(2)}) collective-permute-start(f16[72,768]{1,0:T(8,128)(2,1)S(1)} %get-tuple-element.69), channel_id=1, source_target_pairs={{0,8},{1,9},{2,10},{3,11},{4,12},{5,13},{6,14},{7,15},{8,0},{9,1},... | collective-permute-start | bytes 331784 | tf_op jit(solution)/shard_map/ppermute | solution.py:35
  89.2 17.1 %collective-permute-start.14 = (f16[72,768]{1,0:T(8,128)(2,1)S(1)}, f16[72,768]{1,0:T(8,128)(2,1)}, u32[]{:S(2)}, u32[]{:S(2)}) collective-permute-start(f16[72,768]{1,0:T(8,128)(2,1)S(1)} %get-tuple-element.70), channel_id=1, source_target_pairs={{0,6},{1,15},{2,4},{3,13},{4,10},{5,3},{6,8},{7,1},{8,14},{9,7},{1... | collective-permute-start | bytes 331784 | tf_op jit(solution)/shard_map/ppermute | solution.py:35
  92.4 14.9 %collective-permute-start.13 = (f16[72,768]{1,0:T(8,128)(2,1)S(1)}, f16[72,768]{1,0:T(8,128)(2,1)}, u32[]{:S(2)}, u32[]{:S(2)}) collective-permute-start(f16[72,768]{1,0:T(8,128)(2,1)S(1)} %get-tuple-element.71), channel_id=1, source_target_pairs={{0,4},{1,13},{2,6},{3,15},{4,8},{5,1},{6,10},{7,3},{8,12},{9,5},{1... | collective-permute-start | bytes 331784 | tf_op jit(solution)/shard_map/ppermute | solution.py:35
  93.0 15.2 %collective-permute-start.12 = (f16[72,768]{1,0:T(8,128)(2,1)S(1)}, f16[72,768]{1,0:T(8,128)(2,1)}, u32[]{:S(2)}, u32[]{:S(2)}) collective-permute-start(f16[72,768]{1,0:T(8,128)(2,1)S(1)} %get-tuple-element.72), channel_id=1, source_target_pairs={{0,2},{1,3},{2,0},{3,1},{4,6},{5,7},{6,4},{7,5},{8,10},{9,11},{10,... | collective-permute-start | bytes 331784 | tf_op jit(solution)/shard_map/ppermute | solution.py:35
  97.8 13.6 %all-to-all-start.3 = ((f32[16,3,384]{2,1,0:T(4,128)}), f32[16,3,384]{2,1,0:T(4,128)S(1)}, u32[]{:S(2)}, u32[]{:S(2)}) async-start(f32[16,3,384]{2,1,0:T(4,128)} %reshape.54), calls=%async_computation.3 | async-start | bytes 196608 | tf_op jit(solution)/shard_map/all_to_all | solution.py:256
  (8 other events, 41.8 us)

commit v8 on v7

--- a/solution.py
+++ b/solution.py
@@ -245,9 +245,9 @@
         n_sems=2,
     )
     got = [next_chip(piece.astype(jnp.float16), hop) for hop, piece in enumerate(pieces, 1)]
-    met, *got[3:] = lax.optimization_barrier((met, *got[3:]))
+    met, *got[4:] = lax.optimization_barrier((met, *got[4:]))
     vir = jnp.sum(met[:, :VW].astype(f32) * weight_of(met, VW), 0)
-    vir, *got[3:] = lax.optimization_barrier((vir, *got[3:]))
+    vir, *got[4:] = lax.optimization_barrier((vir, *got[4:]))
     got = [piece.astype(f32) for piece in got]
     (three,) = call(sum_three, [((PW, NV), f32)], [own_piece, *got])
     three_index = three[:, None, :]

time: 114 us -> 113 us (level)
    all_to_all x1, starting transfers between devices: 5.76 us -> 4.58 us  [per_device(): vir = lax.all_to_all(vir, AUX, split_axis=0, concat_axis=0, tiled=True)]
    unnamed x22 -> x18, local copies, waits for them, and re-layouts: 6.24 us -> 5.61 us
  transfers between devices with their start and end apart: 23 -> 23, of which waited for: 7 -> 7; matrix products, arithmetic and copies ran while one was open for 11% -> 12% of each run, Pallas kernels for 6% -> 6%
where the time goes in v8:
time: 113 us; the launch traced here: 111 us
  starting transfers between devices  59.5 us (53%)
  waiting for transfers between devices  17.8 us (16%)
  Pallas kernels  11.9 us (11%)
  local copies, waits for them, and re-layouts  9.26 us (8%)
  other arithmetic  9.01 us (8%)
  matrix products  2 us (2%)
  between operations  1.41 us (1%)
    all_to_all x1, starting transfers between devices, per_device(): local = lax.all_to_all(native, OCC, split_axis=0, concat_axis=0, tiled=True)  14.9 us
    ppermute x7, starting transfers between devices, next_chip(): return lax.ppermute(array, AUX, pairs)  13.4 us
    pallas_call x5, Pallas kernels, call(): pl.pallas_call(kernel, out_shape=[jax.ShapeDtypeStruct(s, t) for s, t in...  11.9 us
    ppermute x7, starting transfers between devices, ring(): return lax.ppermute(array, ('z', 'c'), pairs)  9.56 us
    all_to_all x1, waiting for transfers between devices, per_device(): lax.all_to_all(jnp.broadcast_to(local, (Y * XH, PW, NV)), CHIPS, split_ax...  7.85 us
    convert_element_type x7, other arithmetic, per_device(): got = [piece.astype(f32) for piece in got]  6.4 us
    all_to_all x1, starting transfers between devices, per_device(): met = lax.all_to_all(packed, OCC, split_axis=0, concat_axis=0, tiled=True)  6.02 us
    unnamed x18, local copies, waits for them, and re-layouts  5.61 us
  transfers between devices with their start and end apart: 23, of which 7 were waited for; matrix products, arithmetic and copies ran while one was open for 12% of the time, Pallas kernels for 6%

profile of v8, /device:TPU:32, one launch (start us, length us, event | category | flops | bytes accessed | tf_op | source)
XLA Modules:
  0.0 110.8 jit_solution(5282339575259894702)
XLA Ops:
  0.7 1.6 %copy-done = bf16[16,64,1024]{2,1,0:T(8,128)(2,1)S(1)} copy-done((bf16[16,64,1024]{2,1,0:T(8,128)(2,1)S(1)}, bf16[16,64,1024]{2,1,0:T(8,128)(2,1)}, u32[]{:S(2)}) %copy-start) | copy-done | bytes 2097176
  2.2 2.0 %convolution_convert_fusion = bf16[16,64,48]{1,2,0:T(8,128)(2,1)S(1)} fusion(bf16[16,64,1024]{2,1,0:T(8,128)(2,1)S(1)} %copy-done, bf16[1024,48]{0,1:T(8,128)(2,1)} %param.5), kind=kOutput, calls=%fused_computation.1 | convolution fusion | flops 100712448 | bytes 2293760 | tf_op jit(solution)/shard_map/ipm,ma->ipa/dot_general | solution.py:169
  4.9 4.1 %collective-permute-start = (bf16[64,768]{1,0:T(8,128)(2,1)S(1)}, bf16[64,768]{1,0:T(8,128)(2,1)S(1)}, u32[]{:S(2)}, u32[]{:S(2)}) collective-permute-start(bf16[64,768]{1,0:T(8,128)(2,1)S(1)} %copy.17), channel_id=1, source_target_pairs={{0,0},{1,16},{2,32},{3,48},{4,64},{5,80},{6,96},{7,112},{8,128},{9... | collective-permute-start | bytes 294920 | tf_op jit(solution)/shard_map/ppermute | solution.py:176
  9.8 14.9 %all-to-all-start = ((bf16[16,2,1536]{2,1,0:T(2,128)(2,1)}), bf16[16,2,1536]{2,1,0:T(2,128)(2,1)S(1)}, u32[]{:S(2)}, u32[]{:S(2)}) async-start(bf16[16,2,1536]{2,1,0:T(2,128)(2,1)} %reshape.57), calls=%async_computation | async-start | bytes 196608 | tf_op jit(solution)/shard_map/all_to_all | solution.py:186
  27.7 4.8 %all-to-all-done = bf16[16,2,1536]{2,1,0:T(2,128)(2,1)S(1)} async-done(((bf16[16,2,1536]{2,1,0:T(2,128)(2,1)}), bf16[16,2,1536]{2,1,0:T(2,128)(2,1)S(1)}, u32[]{:S(2)}, u32[]{:S(2)}) %all-to-all-start) | async-done | bytes 98336 | tf_op jit(solution)/shard_map/all_to_all | solution.py:186
  32.7 1.7 %collective-permute-start.5 = (bf16[128,768]{1,0:T(8,128)(2,1)S(1)}, bf16[128,768]{1,0:T(8,128)(2,1)S(1)}, u32[]{:S(2)}, u32[]{:S(2)}) collective-permute-start(bf16[128,768]{1,0:T(8,128)(2,1)S(1)} %pad_maximum_fusion.refs_0_), channel_id=1, source_target_pairs={{0,96},{1,33},{16,112},{17,49},{32,0},{33,65},{48,16},{49,81},{64,... | collective-permute-start | bytes 589832 | tf_op jit(solution)/shard_map/ppermute | solution.py:30
  34.4 1.3 %collective-permute-start.4 = (bf16[128,768]{1,0:T(8,128)(2,1)S(1)}, bf16[128,768]{1,0:T(8,128)(2,1)S(1)}, u32[]{:S(2)}, u32[]{:S(2)}) collective-permute-start(bf16[128,768]{1,0:T(8,128)(2,1)S(1)} %pad_maximum_fusion.refs_0_), channel_id=1, source_target_pairs={{0,32},{1,97},{16,48},{17,113},{32,64},{33,1},{48,80},{49,17},{64,... | collective-permute-start | bytes 589832 | tf_op jit(solution)/shard_map/ppermute | solution.py:30
  38.8 5.6 %all-to-all-start.1 = ((bf16[8,64,768]{2,1,0:T(8,128)(2,1)}), bf16[8,64,768]{2,1,0:T(8,128)(2,1)S(1)}, u32[]{:S(2)}, u32[]{:S(2)}) async-start(bf16[8,64,768]{2,1,0:T(8,128)(2,1)} %broadcast_in_dim.12), calls=%async_computation.1 | async-start | bytes 1572864 | tf_op jit(solution)/shard_map/all_to_all | solution.py:191
  45.1 2.5 %collective-permute-start.8 = (bf16[128,768]{1,0:T(8,128)(2,1)S(1)}, bf16[128,768]{1,0:T(8,128)(2,1)}, u32[]{:S(2)}, u32[]{:S(2)}) collective-permute-start(bf16[128,768]{1,0:T(8,128)(2,1)S(1)} %collective-permute-done.4.refs_3_), channel_id=1, source_target_pairs={{0,32},{1,97},{16,48},{17,113},{32,64},{33,1},{48,80},{49,17},{64,... | collective-permute-start | bytes 589832 | tf_op jit(solution)/shard_map/ppermute | solution.py:30
  47.6 2.0 %collective-permute-start.7 = (bf16[128,768]{1,0:T(8,128)(2,1)S(1)}, bf16[128,768]{1,0:T(8,128)(2,1)}, u32[]{:S(2)}, u32[]{:S(2)}) collective-permute-start(bf16[128,768]{1,0:T(8,128)(2,1)S(1)} %collective-permute-done.5.refs_4_), channel_id=1, source_target_pairs={{0,112},{1,17},{16,0},{17,33},{32,16},{33,49},{48,32},{49,65},{64,... | collective-permute-start | bytes 589832 | tf_op jit(solution)/shard_map/ppermute | solution.py:30
  49.6 7.9 %all-to-all-done.1 = bf16[8,64,768]{2,1,0:T(8,128)(2,1)S(1)} async-done(((bf16[8,64,768]{2,1,0:T(8,128)(2,1)}), bf16[8,64,768]{2,1,0:T(8,128)(2,1)S(1)}, u32[]{:S(2)}, u32[]{:S(2)}) %all-to-all-start.1) | async-done | bytes 786464 | tf_op jit(solution)/shard_map/all_to_all | solution.py:191
  57.5 2.2 %collective-permute-done.9.refs_9_ = bf16[512,768]{1,0:T(8,128)(2,1)S(1)} collective-permute-done((bf16[512,768]{1,0:T(8,128)(2,1)S(1)}, bf16[512,768]{1,0:T(8,128)(2,1)S(1)}, u32[]{:S(2)}, u32[]{:S(2)}) %collective-permute-start.9) | collective-permute-done | bytes 786464 | tf_op jit(solution)/shard_map/ppermute | solution.py:23
  59.7 4.9 %shard_map.62 = (bf16[1024,768]{1,0:T(8,128)(2,1)S(1)}, bf16[768,768]{1,0:T(8,128)(2,1)S(1)}, f32[768,384]{1,0:T(8,128)S(1)}) custom-call(s32[25]{0:T(128)S(1)} %stack.103.place, bf16[128,768]{1,0:T(8,128)(2,1)S(1)} %pad_maximum_fusion.refs_0_, bf16[128,768]{1,0:T(8,128)(2,1)} %collective-permute-done.2.refs_1_, ...), custom_call_target="tpu_custom_call" | custom-call | flops 1660944384 | bytes 6291456 | tf_op jit(solution)/shard_map/pallas_call | solution.py:154
  65.0 2.7 %shard_map.63 = (f32[512,768]{1,0:T(8,128)}, f32[512,768]{1,0:T(8,128)S(1)}) custom-call(s32[25]{0:T(128)S(1)} %stack.103.place, bf16[1024,768]{1,0:T(8,128)(2,1)S(1)} %get-tuple-element.39.rows, bf16[768,768]{1,0:T(8,128)(2,1)S(1)} %get-tuple-element.37.amp), custom_call_target="tpu_custom_call" | custom-call | flops 1207959552 | bytes 6291456 | tf_op jit(solution)/shard_map/pallas_call | solution.py:154
  68.2 1.6 %shard_map.64 = f32[16,56,384]{2,1,0:T(8,128)S(1)} custom-call(s32[25]{0:T(128)S(1)} %stack.103.place, bf16[768,768]{1,0:T(8,128)(2,1)S(1)} %get-tuple-element.37.amp, f32[768,384]{1,0:T(8,128)S(1)} %collective-permute-done.10.got), custom_call_target="tpu_custom_call" | custom-call | flops 452984832 | bytes 6291456 | tf_op jit(solution)/shard_map/pallas_call | solution.py:154
  70.7 6.0 %all-to-all-start.2 = ((f16[16,56,384]{2,1,0:T(8,128)(2,1)}), f16[16,56,384]{2,1,0:T(8,128)(2,1)S(1)}, u32[]{:S(2)}, u32[]{:S(2)}) async-start(f16[16,56,384]{2,1,0:T(8,128)(2,1)} %convert_element_type.67), calls=%async_computation.2 | async-start | bytes 1376256 | tf_op jit(solution)/shard_map/all_to_all | solution.py:238
  76.8 1.4 %copy-done.2 = f32[512,768]{1,0:T(8,128)S(1)} copy-done((f32[512,768]{1,0:T(8,128)S(1)}, f32[512,768]{1,0:T(8,128)}, u32[]{:S(2)}) %copy-start.2) | copy-done | bytes 1572888
  78.2 2.6 %shard_map.65 = (f32[64,768]{1,0:T(8,128)S(1)}, f32[7,72,768]{2,1,0:T(8,128)S(1)}) custom-call(s32[25]{0:T(128)S(1)} %stack.103.place, f32[512,768]{1,0:T(8,128)S(1)} %copy-done.2, f32[512,768]{1,0:T(8,128)} %collective-permute-done.11.got), custom_call_target="tpu_custom_call" | custom-call | bytes 6291456 | tf_op jit(solution)/shard_map/pallas_call | solution.py:154
  81.6 2.9 %collective-permute-start.18 = (f16[72,768]{1,0:T(8,128)(2,1)S(1)}, f16[72,768]{1,0:T(8,128)(2,1)}, u32[]{:S(2)}, u32[]{:S(2)}) collective-permute-start(f16[72,768]{1,0:T(8,128)(2,1)S(1)} %get-tuple-element.62), channel_id=1, source_target_pairs={{0,14},{1,7},{2,12},{3,5},{4,2},{5,11},{6,0},{7,9},{8,6},{9,15},{1... | collective-permute-start | bytes 331784 | tf_op jit(solution)/shard_map/ppermute | solution.py:35
  85.3 2.8 %collective-permute-start.16 = (f16[72,768]{1,0:T(8,128)(2,1)}, f16[72,768]{1,0:T(8,128)(2,1)}, u32[]{:S(2)}, u32[]{:S(2)}) collective-permute-start(f16[72,768]{1,0:T(8,128)(2,1)} %get-tuple-element.64), channel_id=1, source_target_pairs={{0,10},{1,11},{2,8},{3,9},{4,14},{5,15},{6,12},{7,13},{8,2},{9,3},... | collective-permute-start | bytes 331784 | tf_op jit(solution)/shard_map/ppermute | solution.py:35
  89.2 3.2 %collective-permute-start.14 = (f16[72,768]{1,0:T(8,128)(2,1)S(1)}, f16[72,768]{1,0:T(8,128)(2,1)}, u32[]{:S(2)}, u32[]{:S(2)}) collective-permute-start(f16[72,768]{1,0:T(8,128)(2,1)S(1)} %get-tuple-element.66), channel_id=1, source_target_pairs={{0,6},{1,15},{2,4},{3,13},{4,10},{5,3},{6,8},{7,1},{8,14},{9,7},{1... | collective-permute-start | bytes 331784 | tf_op jit(solution)/shard_map/ppermute | solution.py:35
  92.4 2.6 %collective-permute-start.12 = (f16[72,768]{1,0:T(8,128)(2,1)S(1)}, f16[72,768]{1,0:T(8,128)(2,1)}, u32[]{:S(2)}, u32[]{:S(2)}) collective-permute-start(f16[72,768]{1,0:T(8,128)(2,1)S(1)} %get-tuple-element.68), channel_id=1, source_target_pairs={{0,2},{1,3},{2,0},{3,1},{4,6},{5,7},{6,4},{7,5},{8,10},{9,11},{10,... | collective-permute-start | bytes 331784 | tf_op jit(solution)/shard_map/ppermute | solution.py:35
  95.7 1.2 %collective-permute-done.16 = f16[72,768]{1,0:T(8,128)(2,1)} collective-permute-done((f16[72,768]{1,0:T(8,128)(2,1)}, f16[72,768]{1,0:T(8,128)(2,1)}, u32[]{:S(2)}, u32[]{:S(2)}) %collective-permute-start.16) | collective-permute-done | bytes 110624 | tf_op jit(solution)/shard_map/ppermute | solution.py:35
  97.8 4.6 %all-to-all-start.3 = ((f32[16,3,384]{2,1,0:T(4,128)}), f32[16,3,384]{2,1,0:T(4,128)S(1)}, u32[]{:S(2)}, u32[]{:S(2)}) async-start(f32[16,3,384]{2,1,0:T(4,128)} %reshape.54), calls=%async_computation.3 | async-start | bytes 196608 | tf_op jit(solution)/shard_map/all_to_all | solution.py:256
  (77 shorter events, 22.5 us)
Async XLA Ops:
  0.6 24.1 %copy-start.6 = (f32[16]{0:T(128)S(1)}, f32[16]{0:T(128)}, u32[]{:S(2)}) copy-start(f32[16]{0:T(128)} %param.6) | copy-start | bytes 196
  4.4 23.3 %collective-permute-start.1 = (bf16[64,768]{1,0:T(8,128)(2,1)S(1)}, bf16[64,768]{1,0:T(8,128)(2,1)S(1)}, u32[]{:S(2)}, u32[]{:S(2)}) collective-permute-start(bf16[64,768]{1,0:T(8,128)(2,1)S(1)} %copy.17), channel_id=1, source_target_pairs={{0,128},{1,144},{2,160},{3,176},{4,192},{5,208},{6,224},{7,240},{8... | collective-permute-start | bytes 294920 | tf_op jit(solution)/shard_map/ppermute | solution.py:176
  4.9 22.7 %collective-permute-start = (bf16[64,768]{1,0:T(8,128)(2,1)S(1)}, bf16[64,768]{1,0:T(8,128)(2,1)S(1)}, u32[]{:S(2)}, u32[]{:S(2)}) collective-permute-start(bf16[64,768]{1,0:T(8,128)(2,1)S(1)} %copy.17), channel_id=1, source_target_pairs={{0,0},{1,16},{2,32},{3,48},{4,64},{5,80},{6,96},{7,112},{8,128},{9... | collective-permute-start | bytes 294920 | tf_op jit(solution)/shard_map/ppermute | solution.py:176
  9.8 22.7 %all-to-all-start = ((bf16[16,2,1536]{2,1,0:T(2,128)(2,1)}), bf16[16,2,1536]{2,1,0:T(2,128)(2,1)S(1)}, u32[]{:S(2)}, u32[]{:S(2)}) async-start(bf16[16,2,1536]{2,1,0:T(2,128)(2,1)} %reshape.57), calls=%async_computation | async-start | bytes 196608 | tf_op jit(solution)/shard_map/all_to_all | solution.py:186
  32.7 11.7 %collective-permute-start.5 = (bf16[128,768]{1,0:T(8,128)(2,1)S(1)}, bf16[128,768]{1,0:T(8,128)(2,1)S(1)}, u32[]{:S(2)}, u32[]{:S(2)}) collective-permute-start(bf16[128,768]{1,0:T(8,128)(2,1)S(1)} %pad_maximum_fusion.refs_0_), channel_id=1, source_target_pairs={{0,96},{1,33},{16,112},{17,49},{32,0},{33,65},{48,16},{49,81},{64,... | collective-permute-start | bytes 589832 | tf_op jit(solution)/shard_map/ppermute | solution.py:30
  34.4 10.6 %collective-permute-start.4 = (bf16[128,768]{1,0:T(8,128)(2,1)S(1)}, bf16[128,768]{1,0:T(8,128)(2,1)S(1)}, u32[]{:S(2)}, u32[]{:S(2)}) collective-permute-start(bf16[128,768]{1,0:T(8,128)(2,1)S(1)} %pad_maximum_fusion.refs_0_), channel_id=1, source_target_pairs={{0,32},{1,97},{16,48},{17,113},{32,64},{33,1},{48,80},{49,17},{64,... | collective-permute-start | bytes 589832 | tf_op jit(solution)/shard_map/ppermute | solution.py:30
  35.7 13.9 %collective-permute-start.3 = (bf16[128,768]{1,0:T(8,128)(2,1)S(1)}, bf16[128,768]{1,0:T(8,128)(2,1)}, u32[]{:S(2)}, u32[]{:S(2)}) collective-permute-start(bf16[128,768]{1,0:T(8,128)(2,1)S(1)} %pad_maximum_fusion.refs_0_), channel_id=1, source_target_pairs={{0,112},{1,17},{16,0},{17,33},{32,16},{33,49},{48,32},{49,65},{64,... | collective-permute-start | bytes 589832 | tf_op jit(solution)/shard_map/ppermute | solution.py:30
  36.6 20.8 %collective-permute-start.2 = (bf16[128,768]{1,0:T(8,128)(2,1)S(1)}, bf16[128,768]{1,0:T(8,128)(2,1)}, u32[]{:S(2)}, u32[]{:S(2)}) collective-permute-start(bf16[128,768]{1,0:T(8,128)(2,1)S(1)} %pad_maximum_fusion.refs_0_), channel_id=1, source_target_pairs={{0,16},{1,113},{16,32},{17,1},{32,48},{33,17},{48,64},{49,33},{64,... | collective-permute-start | bytes 589832 | tf_op jit(solution)/shard_map/ppermute | solution.py:30
  38.8 18.6 %all-to-all-start.1 = ((bf16[8,64,768]{2,1,0:T(8,128)(2,1)}), bf16[8,64,768]{2,1,0:T(8,128)(2,1)S(1)}, u32[]{:S(2)}, u32[]{:S(2)}) async-start(bf16[8,64,768]{2,1,0:T(8,128)(2,1)} %broadcast_in_dim.12), calls=%async_computation.1 | async-start | bytes 1572864 | tf_op jit(solution)/shard_map/all_to_all | solution.py:191
  45.1 12.4 %collective-permute-start.8 = (bf16[128,768]{1,0:T(8,128)(2,1)S(1)}, bf16[128,768]{1,0:T(8,128)(2,1)}, u32[]{:S(2)}, u32[]{:S(2)}) collective-permute-start(bf16[128,768]{1,0:T(8,128)(2,1)S(1)} %collective-permute-done.4.refs_3_), channel_id=1, source_target_pairs={{0,32},{1,97},{16,48},{17,113},{32,64},{33,1},{48,80},{49,17},{64,... | collective-permute-start | bytes 589832 | tf_op jit(solution)/shard_map/ppermute | solution.py:30
  47.6 9.9 %collective-permute-start.6 = (bf16[128,768]{1,0:T(8,128)(2,1)S(1)}, bf16[128,768]{1,0:T(8,128)(2,1)}, u32[]{:S(2)}, u32[]{:S(2)}) collective-permute-start(bf16[128,768]{1,0:T(8,128)(2,1)S(1)} %collective-permute-done.4.refs_3_), channel_id=1, source_target_pairs={{0,16},{1,113},{16,32},{17,1},{32,48},{33,17},{48,64},{49,33},{64,... | collective-permute-start | bytes 589832 | tf_op jit(solution)/shard_map/ppermute | solution.py:30
  47.6 9.9 %collective-permute-start.7 = (bf16[128,768]{1,0:T(8,128)(2,1)S(1)}, bf16[128,768]{1,0:T(8,128)(2,1)}, u32[]{:S(2)}, u32[]{:S(2)}) collective-permute-start(bf16[128,768]{1,0:T(8,128)(2,1)S(1)} %collective-permute-done.5.refs_4_), channel_id=1, source_target_pairs={{0,112},{1,17},{16,0},{17,33},{32,16},{33,49},{48,32},{49,65},{64,... | collective-permute-start | bytes 589832 | tf_op jit(solution)/shard_map/ppermute | solution.py:30
  57.4 2.3 %collective-permute-start.9 = (bf16[512,768]{1,0:T(8,128)(2,1)S(1)}, bf16[512,768]{1,0:T(8,128)(2,1)S(1)}, u32[]{:S(2)}, u32[]{:S(2)}) collective-permute-start(bf16[512,768]{1,0:T(8,128)(2,1)S(1)} %bitcast.63), channel_id=1, source_target_pairs={{0,1},{1,0},{2,3},{3,2},{4,5},{5,4},{6,7},{7,6},{8,9},{9,8},{10,11... | collective-permute-start | bytes 2359304 | tf_op jit(solution)/shard_map/ppermute | solution.py:23
  64.6 3.1 %collective-permute-start.10 = (f32[768,384]{1,0:T(8,128)S(1)}, f32[768,384]{1,0:T(8,128)S(1)}, u32[]{:S(2)}, u32[]{:S(2)}) collective-permute-start(f32[768,384]{1,0:T(8,128)S(1)} %get-tuple-element.38), channel_id=1, source_target_pairs={{0,1},{1,0},{2,3},{3,2},{4,5},{5,4},{6,7},{7,6},{8,9},{9,8},{10,11... | collective-permute-start | bytes 3538952 | tf_op jit(solution)/shard_map/ppermute | solution.py:23
  67.8 9.0 %collective-permute-start.11 = (f32[512,768]{1,0:T(8,128)}, f32[512,768]{1,0:T(8,128)}, u32[]{:S(2)}, u32[]{:S(2)}) collective-permute-start(f32[512,768]{1,0:T(8,128)} %get-tuple-element.44), channel_id=1, source_target_pairs={{0,1},{1,0},{2,3},{3,2},{4,5},{5,4},{6,7},{7,6},{8,9},{9,8},{10,11... | collective-permute-start | bytes 4718600 | tf_op jit(solution)/shard_map/ppermute | solution.py:23
  70.7 25.0 %all-to-all-start.2 = ((f16[16,56,384]{2,1,0:T(8,128)(2,1)}), f16[16,56,384]{2,1,0:T(8,128)(2,1)S(1)}, u32[]{:S(2)}, u32[]{:S(2)}) async-start(f16[16,56,384]{2,1,0:T(8,128)(2,1)} %convert_element_type.67), calls=%async_computation.2 | async-start | bytes 1376256 | tf_op jit(solution)/shard_map/all_to_all | solution.py:238
  81.6 10.8 %collective-permute-start.18 = (f16[72,768]{1,0:T(8,128)(2,1)S(1)}, f16[72,768]{1,0:T(8,128)(2,1)}, u32[]{:S(2)}, u32[]{:S(2)}) collective-permute-start(f16[72,768]{1,0:T(8,128)(2,1)S(1)} %get-tuple-element.62), channel_id=1, source_target_pairs={{0,14},{1,7},{2,12},{3,5},{4,2},{5,11},{6,0},{7,9},{8,6},{9,15},{1... | collective-permute-start | bytes 331784 | tf_op jit(solution)/shard_map/ppermute | solution.py:35
  84.4 8.0 %collective-permute-start.17 = (f16[72,768]{1,0:T(8,128)(2,1)S(1)}, f16[72,768]{1,0:T(8,128)(2,1)}, u32[]{:S(2)}, u32[]{:S(2)}) collective-permute-start(f16[72,768]{1,0:T(8,128)(2,1)S(1)} %get-tuple-element.63), channel_id=1, source_target_pairs={{0,12},{1,5},{2,14},{3,7},{4,0},{5,9},{6,2},{7,11},{8,4},{9,13},{1... | collective-permute-start | bytes 331784 | tf_op jit(solution)/shard_map/ppermute | solution.py:35
  85.3 11.6 %collective-permute-start.16 = (f16[72,768]{1,0:T(8,128)(2,1)}, f16[72,768]{1,0:T(8,128)(2,1)}, u32[]{:S(2)}, u32[]{:S(2)}) collective-permute-start(f16[72,768]{1,0:T(8,128)(2,1)} %get-tuple-element.64), channel_id=1, source_target_pairs={{0,10},{1,11},{2,8},{3,9},{4,14},{5,15},{6,12},{7,13},{8,2},{9,3},... | collective-permute-start | bytes 331784 | tf_op jit(solution)/shard_map/ppermute | solution.py:35
  88.1 17.1 %collective-permute-start.15 = (f16[72,768]{1,0:T(8,128)(2,1)S(1)}, f16[72,768]{1,0:T(8,128)(2,1)}, u32[]{:S(2)}, u32[]{:S(2)}) collective-permute-start(f16[72,768]{1,0:T(8,128)(2,1)S(1)} %get-tuple-element.65), channel_id=1, source_target_pairs={{0,8},{1,9},{2,10},{3,11},{4,12},{5,13},{6,14},{7,15},{8,0},{9,1},... | collective-permute-start | bytes 331784 | tf_op jit(solution)/shard_map/ppermute | solution.py:35
  89.2 16.9 %collective-permute-start.14 = (f16[72,768]{1,0:T(8,128)(2,1)S(1)}, f16[72,768]{1,0:T(8,128)(2,1)}, u32[]{:S(2)}, u32[]{:S(2)}) collective-permute-start(f16[72,768]{1,0:T(8,128)(2,1)S(1)} %get-tuple-element.66), channel_id=1, source_target_pairs={{0,6},{1,15},{2,4},{3,13},{4,10},{5,3},{6,8},{7,1},{8,14},{9,7},{1... | collective-permute-start | bytes 331784 | tf_op jit(solution)/shard_map/ppermute | solution.py:35
  92.4 14.6 %collective-permute-start.13 = (f16[72,768]{1,0:T(8,128)(2,1)S(1)}, f16[72,768]{1,0:T(8,128)(2,1)}, u32[]{:S(2)}, u32[]{:S(2)}) collective-permute-start(f16[72,768]{1,0:T(8,128)(2,1)S(1)} %get-tuple-element.67), channel_id=1, source_target_pairs={{0,4},{1,13},{2,6},{3,15},{4,8},{5,1},{6,10},{7,3},{8,12},{9,5},{1... | collective-permute-start | bytes 331784 | tf_op jit(solution)/shard_map/ppermute | solution.py:35
  92.4 15.5 %collective-permute-start.12 = (f16[72,768]{1,0:T(8,128)(2,1)S(1)}, f16[72,768]{1,0:T(8,128)(2,1)}, u32[]{:S(2)}, u32[]{:S(2)}) collective-permute-start(f16[72,768]{1,0:T(8,128)(2,1)S(1)} %get-tuple-element.68), channel_id=1, source_target_pairs={{0,2},{1,3},{2,0},{3,1},{4,6},{5,7},{6,4},{7,5},{8,10},{9,11},{10,... | collective-permute-start | bytes 331784 | tf_op jit(solution)/shard_map/ppermute | solution.py:35
  97.8 12.4 %all-to-all-start.3 = ((f32[16,3,384]{2,1,0:T(4,128)}), f32[16,3,384]{2,1,0:T(4,128)S(1)}, u32[]{:S(2)}, u32[]{:S(2)}) async-start(f32[16,3,384]{2,1,0:T(4,128)} %reshape.54), calls=%async_computation.3 | async-start | bytes 196608 | tf_op jit(solution)/shard_map/all_to_all | solution.py:256
  (6 other events, 31.7 us)
